TPU v7x, 32 devices: a whole 2x2x4 slice. The times are simulated.
32 devices in a mesh: heads: 4 (over y, x), tok: 8 (over z, core).
Axes of the slice: x: 2, y: 2, z: 4, core: 2. Of those that a mesh axis runs over, the one named last changes fastest.
Arguments:
- queries: bfloat16 [8, 8, 8, 1024], P('tok', None, None, 'heads'), may hold values from -12 to 12
- key_rows: bfloat16 [8, 8, 8, 1024], P('tok', None, None, 'heads'), may hold values from -6 to 6
- value_rows: bfloat16 [8, 8, 8, 1024], P('tok', None, None, 'heads'), may hold values from -6 to 6
- residual: bfloat16 [8, 8, 8, 1024], P('heads', 'tok'), may hold values from -3 to 3
- w_out: bfloat16 [1024, 1024], P('heads'), may hold values from -0.375 to 0.375
- w_neck: bfloat16 [1024, 256], replicated, may hold values from -0.1875 to 0.1875
- w_first: bfloat16 [3, 3, 3, 256, 256], replicated, may hold values from -0.109375 to 0.109375
- w_second: bfloat16 [3, 3, 3, 256, 256], replicated, may hold values from -0.109375 to 0.109375
- w_class: bfloat16 [256], replicated, may hold values from -0.5 to 0.5
- labels: int32 [8, 8, 8], P('heads', None, 'tok'), may hold values from 0 to 1, as said below
Outputs:
- encoded: bfloat16 [8, 8, 8, 1024], P('heads', 'tok')
- dice_loss: float32 [], replicated
- grad_encoded: bfloat16 [8, 8, 8, 1024], P('heads', 'tok')
Inputs may be any that keep to these rules, and one draw needn't show every extreme that they name: `labels`: 1 marks a fault cell.
All inputs are finite; a program needn't handle non-finite values.
Results may differ from a plain program's by a relative error of at most 0.025.
Values may be sent and summed in bfloat16 or wider, within the bound.
No kernel may reach another device: no remote copies, remote signals or barrier semaphores. Data moves between devices by JAX's collectives and lax.ppermute only.
A program may use at most 128 MiB of HBM per device.

v0:
```python
import jax
import jax.numpy as jnp
from jax import lax
from jax.sharding import PartitionSpec as P

HD = 64


OFFSETS = [
    (along_c, along_t, along_x)
    for along_c in range(3)
    for along_t in range(3)
    for along_x in range(3)
]
LOSS_SCALE = 64.0
NEG_LARGE = -1e30


def padded_2(value, sides, width):
    for axis, dim in sides:
        size, length = (lax.axis_size(axis), value.shape[dim])
        up = [(i, (i + 1) % size) for i in range(size - 1)]
        down = [(j, i) for i, j in up]
        last = lax.slice_in_dim(value, length - width, length, axis=dim)
        first = lax.slice_in_dim(value, 0, width, axis=dim)
        before = lax.ppermute(last, axis, up)
        after = lax.ppermute(first, axis, down)
        value = jnp.concatenate([before, value, after], axis=dim)
    return value


def silu_slope(volume):
    sigma = jax.nn.sigmoid(volume)
    return sigma * (1.0 + volume * (1.0 - sigma))


def with_rims(volume):
    padded = padded_2(volume, (("heads", 0), ("tok", 2)), 1)
    return jnp.pad(padded, ((0, 0), (1, 1), (0, 0), (0, 0)))


def conv_apply(volume, weights, flipped):
    extent = volume.shape[:3]
    padded = with_rims(volume)
    pieces = []
    for along_c, along_t, along_x in OFFSETS:
        if flipped:
            anchor = (2 - along_c, 2 - along_t, 2 - along_x)
        else:
            anchor = (along_c, along_t, along_x)
        pieces.append(
            padded[
                anchor[0] : anchor[0] + extent[0],
                anchor[1] : anchor[1] + extent[1],
                anchor[2] : anchor[2] + extent[2],
            ]
        )
    stacked = jnp.stack(pieces, axis=3)
    columns = stacked.reshape(extent[0] * extent[1] * extent[2], 27, volume.shape[3])
    kernel = weights.reshape(27, weights.shape[3], weights.shape[4])
    if flipped:
        contraction = (((1, 2), (0, 2)), ((), ()))
    else:
        contraction = (((1, 2), (0, 1)), ((), ()))
    return lax.dot_general(columns, kernel, contraction, preferred_element_type=jnp.float32)


def online_step(carried, query_block, key_block, value_block, scale):
    row_peak, totals, weighted_sum = carried
    scores = (
        jnp.einsum("qhd,khd->qhk", query_block, key_block, preferred_element_type=jnp.float32)
        * scale
    )
    new_peak = jnp.maximum(row_peak, jnp.max(scores, axis=-1))
    factor = jnp.exp(row_peak - new_peak)
    raw_weights = jnp.exp(scores - new_peak[:, :, None])
    totals = totals * factor + jnp.sum(raw_weights, axis=-1)
    weighted_sum = weighted_sum * factor[:, :, None] + jnp.einsum(
        "qhk,khd->qhd",
        raw_weights.astype(jnp.bfloat16),
        value_block,
        preferred_element_type=jnp.float32,
    )
    return (new_peak, totals, weighted_sum)


def on_device(
    queries, key_rows, value_rows, residual, w_out, w_neck, w_first, w_second, w_class, labels
):
    width_here = queries.shape[-1]
    heads_here = width_here // HD
    scale = HD ** (-0.5)
    local_queries = queries.reshape(-1, heads_here, HD)
    query_total = local_queries.shape[0]
    start_state = (
        jnp.full((query_total, heads_here), NEG_LARGE, jnp.float32),
        jnp.zeros((query_total, heads_here), jnp.float32),
        jnp.zeros((query_total, heads_here, HD), jnp.float32),
    )

    def fold_keys(carried, key_piece):
        key_flat = key_piece[0].reshape(-1, heads_here, HD)
        value_flat = key_piece[1].reshape(-1, heads_here, HD)
        key_total = key_flat.shape[0]
        if key_total > 512 and key_total % 512 == 0:
            key_blocks = key_flat.reshape(key_total // 512, 512, heads_here, HD)
            value_blocks = value_flat.reshape(key_total // 512, 512, heads_here, HD)

            def scan_step(inner, paired):
                return (online_step(inner, local_queries, paired[0], paired[1], scale), None)

            return lax.scan(scan_step, carried, (key_blocks, value_blocks))[0]
        return online_step(carried, local_queries, key_flat, value_flat, scale)

    row_peak, totals, weighted_sum = fold_keys(
        start_state,
        (
            lax.all_gather(key_rows, "tok", axis=0, tiled=True),
            lax.all_gather(value_rows, "tok", axis=0, tiled=True),
        ),
    )
    attended = (weighted_sum / totals[:, :, None]).astype(jnp.bfloat16)
    attended_grid = attended.reshape(queries.shape)
    owned = lax.all_to_all(attended_grid, "heads", split_axis=1, concat_axis=3, tiled=True)
    attention_out = jnp.einsum(
        "tzxe,ed->ztxd",
        owned,
        lax.all_gather(w_out, "heads", axis=0, tiled=True),
        preferred_element_type=jnp.float32,
    )
    encoded = (residual.astype(jnp.float32) + attention_out).astype(jnp.bfloat16)
    tiled = lax.all_to_all(encoded, "tok", split_axis=2, concat_axis=1, tiled=True)
    neck_feats = jnp.einsum(
        "ztxd,dc->ztxc", tiled, w_neck, preferred_element_type=jnp.float32
    ).astype(jnp.bfloat16)
    extent = neck_feats.shape[:3]
    channels = w_neck.shape[1]
    cell_count = extent[0] * extent[1] * extent[2]
    hidden_one = conv_apply(neck_feats, w_first, False)
    active_one = jax.nn.silu(hidden_one).astype(jnp.bfloat16)
    hidden_two = conv_apply(active_one.reshape(extent + (channels,)), w_second, False)
    active_two = jax.nn.silu(hidden_two).astype(jnp.bfloat16)
    logits = jnp.dot(active_two, w_class, preferred_element_type=jnp.float32)
    probability = jax.nn.sigmoid(logits)
    fault_mask = labels.reshape(cell_count).astype(jnp.float32)
    intersection, total_prob, total_fault = lax.psum(
        (jnp.sum(probability * fault_mask), jnp.sum(probability), jnp.sum(fault_mask)),
        ("heads", "tok"),
    )
    dice_denominator = total_prob + total_fault
    dice_loss = 1.0 - 2.0 * intersection / dice_denominator
    cells_all = float(cell_count * lax.axis_size("heads") * lax.axis_size("tok"))
    grad_logits = (
        LOSS_SCALE
        * cells_all
        * -2.0
        * (fault_mask * dice_denominator - intersection)
        / (dice_denominator * dice_denominator)
        * probability
        * (1.0 - probability)
    )
    grad_hidden_two = (
        grad_logits[:, None] * w_class.astype(jnp.float32)[None, :] * silu_slope(hidden_two)
    ).astype(jnp.bfloat16)
    grad_active_one = conv_apply(grad_hidden_two.reshape(extent + (channels,)), w_second, True)
    grad_hidden_one = (grad_active_one * silu_slope(hidden_one)).astype(jnp.bfloat16)
    grad_neck = (
        conv_apply(grad_hidden_one.reshape(extent + (channels,)), w_first, True)
        .astype(jnp.bfloat16)
        .reshape(extent + (channels,))
    )
    grad_tiles = jnp.einsum(
        "ztxc,dc->ztxd", grad_neck, w_neck, preferred_element_type=jnp.float32
    ).astype(jnp.bfloat16)
    grad_encoded = lax.all_to_all(grad_tiles, "tok", split_axis=1, concat_axis=2, tiled=True)
    return (encoded, dice_loss, grad_encoded)


def solution(mesh):
    placed = (
        P("tok", None, None, "heads"),
        P("tok", None, None, "heads"),
        P("tok", None, None, "heads"),
        P("heads", "tok", None, None),
        P("heads", None),
        P(),
        P(),
        P(),
        P(),
        P("heads", None, "tok"),
    )
    return jax.shard_map(
        on_device,
        mesh=mesh,
        in_specs=placed,
        out_specs=(P("heads", "tok", None, None), P(), P("heads", "tok", None, None)),
        check_vma=False,
    )
```

profile of v0, /device:TPU:0, one launch (start us, length us, event | category | flops | bytes accessed | tf_op | source)
XLA Modules:
  0.0 240.1 jit_solution(574017638586258291)
XLA Ops:
  7.9 17.3 %all_gather.9 = bf16[8,8,8,256]{3,2,1,0:T(8,128)(2,1)} all-gather(bf16[1,8,8,256]{3,2,1,0:T(8,128)(2,1)} %param.11), channel_id=1, replica_groups=mesh['heads'=4,'tok'=8] {'tok'}, dimensions={0}, use_global_device_ids=true | all-gather | bytes 294912 | tf_op jit(solution)/shard_map/all_gather | solution.py:118
  25.2 2.1 reshape.308
  27.3 1.5 reshape.309
  28.8 15.5 %all_gather.10 = bf16[8,8,8,256]{3,2,1,0:T(8,128)(2,1)} all-gather(bf16[1,8,8,256]{3,2,1,0:T(8,128)(2,1)} %param.12), channel_id=1, replica_groups=mesh['heads'=4,'tok'=8] {'tok'}, dimensions={0}, use_global_device_ids=true | all-gather | bytes 294912 | tf_op jit(solution)/shard_map/all_gather | solution.py:119
  44.3 2.0 reshape.310
  46.3 1.5 fusion.62
  48.0 1.3 fusion.5
  50.0 1.6 reshape.311
  51.6 8.5 %all_to_all.36 = bf16[1,8,8,256]{3,2,0,1:T(8,128)(2,1)S(1)} all-to-all(bf16[1,8,8,256]{3,2,0,1:T(8,128)(2,1)} %bitcast.575), channel_id=1, replica_groups=mesh['heads'=4,'tok'=8] {'heads'}, dimensions={1} | all-to-all | bytes 65536 | tf_op jit(solution)/shard_map/all_to_all | solution.py:124
  60.7 2.0 fusion.12
  62.8 10.2 %all_to_all.37 = bf16[2,1,8,1024]{3,0,1,2:T(2,128)(2,1)S(1)} all-to-all(bf16[2,1,8,1024]{3,0,1,2:T(2,128)(2,1)S(1)} %copy.62), channel_id=1, replica_groups=mesh['heads'=4,'tok'=8] {'tok'}, dimensions={2} | all-to-all | bytes 65536 | tf_op jit(solution)/shard_map/all_to_all | solution.py:132
  75.5 4.5 %collective-permute-start = (bf16[1,8,1,256]{3,1,0,2:T(8,128)(2,1)S(1)}, bf16[1,8,1,256]{3,1,0,2:T(8,128)(2,1)S(1)}, u32[]{:S(2)}, u32[]{:S(2)}) collective-permute-start(bf16[1,8,1,256]{3,1,0,2:T(8,128)(2,1)S(1)} %get-tuple-element.24), channel_id=1, source_target_pairs={{0,8},{8,16},{16,24},{1,9},{9,17},{17,25},{2,10},{10,18},{18,26},{... | collective-permute-start | bytes 12296 | tf_op jit(solution)/shard_map/ppermute | solution.py:26
  84.0 2.7 %collective-permute-done.3 = bf16[4,8,1,256]{3,1,0,2:T(8,128)(2,1)S(1)} collective-permute-done((bf16[4,8,1,256]{3,1,0,2:T(8,128)(2,1)S(1)}, bf16[4,8,1,256]{3,1,0,2:T(8,128)(2,1)S(1)}, u32[]{:S(2)}, u32[]{:S(2)}) %collective-permute-start.3) | collective-permute-done | bytes 16416 | tf_op jit(solution)/shard_map/ppermute | solution.py:27
  88.2 4.2 %collective-permute-start.4 = (bf16[1,8,1,256]{3,1,2,0:T(8,128)(2,1)S(1)}, bf16[1,8,1,256]{3,1,2,0:T(8,128)(2,1)S(1)}, u32[]{:S(2)}, u32[]{:S(2)}) collective-permute-start(bf16[1,8,1,256]{3,1,2,0:T(8,128)(2,1)S(1)} %get-tuple-element.22), channel_id=1, source_target_pairs={{0,8},{8,16},{16,24},{1,9},{9,17},{17,25},{2,10},{10,18},{18,26},{... | collective-permute-start | bytes 12296 | tf_op jit(solution)/shard_map/ppermute | solution.py:26
  93.7 4.6 %collective-permute-done.5 = bf16[1,8,1,256]{3,1,2,0:T(8,128)(2,1)S(1)} collective-permute-done((bf16[1,8,1,256]{3,1,2,0:T(8,128)(2,1)S(1)}, bf16[1,8,1,256]{3,1,2,0:T(8,128)(2,1)S(1)}, u32[]{:S(2)}, u32[]{:S(2)}) %collective-permute-start.5) | collective-permute-done | bytes 4128 | tf_op jit(solution)/shard_map/ppermute | solution.py:27
  98.9 3.8 %collective-permute-start.6 = (bf16[4,8,1,256]{3,1,0,2:T(8,128)(2,1)}, bf16[4,8,1,256]{3,1,0,2:T(8,128)(2,1)}, u32[]{:S(2)}, u32[]{:S(2)}) collective-permute-start(bf16[4,8,1,256]{3,1,0,2:T(8,128)(2,1)} %pad_maximum_fusion.1), channel_id=1, source_target_pairs={{0,1},{1,2},{2,3},{3,4},{4,5},{5,6},{6,7},{8,9},{9,10},{10,11},{11... | collective-permute-start | bytes 49160 | tf_op jit(solution)/shard_map/ppermute | solution.py:26
  112.3 2.5 %convolution_bitcast_fusion.3 = f32[16,256]{1,0:T(8,128)S(1)} fusion(bf16[16,27,256]{2,0,1:T(8,128)(2,1)S(1)} %constant_dynamic-update-slice_fusion.27, bf16[27,256,256]{2,1,0:T(8,128)(2,1)} %bitcast.559), kind=kOutput, calls=%fused_computation.16 | convolution fusion | flops 56623104 | bytes 3776512 | tf_op jit(solution)/shard_map/dot_general | solution.py:65
  117.5 41.7 %all-reduce.4 = (f32[]{:T(128)}, f32[]{:T(128)}) all-reduce(f32[]{:T(128)} %get-tuple-element.15, f32[]{:T(128)S(6)} %add.54), channel_id=1, replica_groups=mesh['heads'=4,'tok'=8] {'heads','tok'}, use_global_device_ids=true, to_apply=%region_3.4 | all-reduce | flops 2 | bytes 16 | tf_op jit(solution)/shard_map/psum | solution.py:146
  160.4 1.9 fusion.58
  163.1 4.2 %collective-permute-start.8 = (bf16[1,8,1,256]{3,1,2,0:T(8,128)(2,1)S(1)}, bf16[1,8,1,256]{3,1,2,0:T(8,128)(2,1)S(1)}, u32[]{:S(2)}, u32[]{:S(2)}) collective-permute-start(bf16[1,8,1,256]{3,1,2,0:T(8,128)(2,1)S(1)} %get-tuple-element.20), channel_id=1, source_target_pairs={{0,8},{8,16},{16,24},{1,9},{9,17},{17,25},{2,10},{10,18},{18,26},{... | collective-permute-start | bytes 12296 | tf_op jit(solution)/shard_map/ppermute | solution.py:26
  169.3 3.5 %collective-permute-done.9 = bf16[1,8,1,256]{3,1,2,0:T(8,128)(2,1)S(1)} collective-permute-done((bf16[1,8,1,256]{3,1,2,0:T(8,128)(2,1)S(1)}, bf16[1,8,1,256]{3,1,2,0:T(8,128)(2,1)S(1)}, u32[]{:S(2)}, u32[]{:S(2)}) %collective-permute-start.9) | collective-permute-done | bytes 4128 | tf_op jit(solution)/shard_map/ppermute | solution.py:27
  175.4 2.7 %collective-permute-done.11 = bf16[4,8,1,256]{3,1,0,2:T(8,128)(2,1)S(1)} collective-permute-done((bf16[4,8,1,256]{3,1,0,2:T(8,128)(2,1)S(1)}, bf16[4,8,1,256]{3,1,0,2:T(8,128)(2,1)S(1)}, u32[]{:S(2)}, u32[]{:S(2)}) %collective-permute-start.11) | collective-permute-done | bytes 16416 | tf_op jit(solution)/shard_map/ppermute | solution.py:27
  179.2 3.0 %fusion.17 = bf16[16,256]{1,0:T(8,128)(2,1)S(1)} fusion(bf16[16,27,256]{2,0,1:T(8,128)(2,1)S(1)} %constant_dynamic-update-slice_fusion.54, bf16[27,256,256]{2,1,0:T(8,128)(2,1)} %bitcast.560, f32[16,256]{1,0:T(8,128)} %get-tuple-element.31), kind=kOutput, calls=%fused_computation.18 | convolution fusion | flops 56659968 | bytes 3784704 | tf_op jit(solution)/shard_map/dot_general | solution.py:65
  182.2 4.5 %collective-permute-start.12 = (bf16[1,8,1,256]{3,1,2,0:T(8,128)(2,1)S(1)}, bf16[1,8,1,256]{3,1,2,0:T(8,128)(2,1)S(1)}, u32[]{:S(2)}, u32[]{:S(2)}) collective-permute-start(bf16[1,8,1,256]{3,1,2,0:T(8,128)(2,1)S(1)} %get-tuple-element.18), channel_id=1, source_target_pairs={{0,8},{8,16},{16,24},{1,9},{9,17},{17,25},{2,10},{10,18},{18,26},{... | collective-permute-start | bytes 12296 | tf_op jit(solution)/shard_map/ppermute | solution.py:26
  188.0 4.2 %collective-permute-done.13 = bf16[1,8,1,256]{3,1,2,0:T(8,128)(2,1)S(1)} collective-permute-done((bf16[1,8,1,256]{3,1,2,0:T(8,128)(2,1)S(1)}, bf16[1,8,1,256]{3,1,2,0:T(8,128)(2,1)S(1)}, u32[]{:S(2)}, u32[]{:S(2)}) %collective-permute-start.13) | collective-permute-done | bytes 4128 | tf_op jit(solution)/shard_map/ppermute | solution.py:27
  192.2 2.9 %collective-permute-start.14 = (bf16[4,8,1,256]{3,1,0,2:T(8,128)(2,1)S(1)}, bf16[4,8,1,256]{3,1,0,2:T(8,128)(2,1)S(1)}, u32[]{:S(2)}, u32[]{:S(2)}) collective-permute-start(bf16[4,8,1,256]{3,1,0,2:T(8,128)(2,1)S(1)} %pad_maximum_fusion.3), channel_id=1, source_target_pairs={{0,1},{1,2},{2,3},{3,4},{4,5},{5,6},{6,7},{8,9},{9,10},{10,11},{11... | collective-permute-start | bytes 49160 | tf_op jit(solution)/shard_map/ppermute | solution.py:26
  196.5 2.7 %collective-permute-done.15 = bf16[4,8,1,256]{3,1,0,2:T(8,128)(2,1)S(1)} collective-permute-done((bf16[4,8,1,256]{3,1,0,2:T(8,128)(2,1)S(1)}, bf16[4,8,1,256]{3,1,0,2:T(8,128)(2,1)S(1)}, u32[]{:S(2)}, u32[]{:S(2)}) %collective-permute-start.15) | collective-permute-done | bytes 16416 | tf_op jit(solution)/shard_map/ppermute | solution.py:27
  215.4 3.3 %fusion.15 = bf16[2,8,1,1024]{3,1,0,2:T(8,128)(2,1)} fusion(bf16[16,27,256]{2,0,1:T(8,128)(2,1)} %constant_dynamic-update-slice_fusion.81, bf16[27,256,256]{2,1,0:T(8,128)(2,1)S(1)} %bitcast.558, bf16[1024,256]{1,0:T(8,128)(2,1)} %param.15), kind=kOutput, calls=%fused_computation.12 | convolution fusion | flops 65032192 | bytes 4317184 | tf_op jit(solution)/shard_map/ztxc,dc->ztxd/dot_general | solution.py:172
  218.7 1.4 copy.78
  220.1 4.8 %all-to-all-start.2 = ((bf16[2,8,1,1024]{3,0,2,1:T(2,128)(2,1)}), bf16[2,8,1,1024]{3,0,2,1:T(2,128)(2,1)}, u32[]{:S(2)}, u32[]{:S(2)}) async-start(bf16[2,8,1,1024]{3,0,2,1:T(2,128)(2,1)} %copy.78), calls=%async_computation.2 | async-start | bytes 65536 | tf_op jit(solution)/shard_map/all_to_all | solution.py:175
  226.1 4.5 %all-to-all-done.2 = bf16[2,8,1,1024]{3,0,2,1:T(2,128)(2,1)} async-done(((bf16[2,8,1,1024]{3,0,2,1:T(2,128)(2,1)}), bf16[2,8,1,1024]{3,0,2,1:T(2,128)(2,1)}, u32[]{:S(2)}, u32[]{:S(2)}) %all-to-all-start.2) | async-done | bytes 32800 | tf_op jit(solution)/shard_map/all_to_all | solution.py:175
  230.7 1.4 copy.80
  (170 shorter events, 47.7 us)
Async XLA Ops:
  7.2 79.8 %copy-start = (bf16[3,3,3,256,256]{4,3,2,1,0:T(8,128)(2,1)S(1)}, bf16[3,3,3,256,256]{4,3,2,1,0:T(8,128)(2,1)}, u32[]{:S(2)}) copy-start(bf16[3,3,3,256,256]{4,3,2,1,0:T(8,128)(2,1)} %param.16) | copy-start | bytes 10616836
  7.2 53.5 %all-gather.2.cloned.1.call-start = ((), (), s32[]{:S(2)}) async-start(), calls=%async_computation.3 | async-start | bytes 2621440 | tf_op jit(solution)/shard_map/all_gather | solution.py:128
  60.7 43.3 %copy-start.2 = (s32[2,8,1]{1,2,0:T(1,128)S(1)}, s32[2,8,1]{1,2,0:T(1,128)}, u32[]{:S(2)}) copy-start(s32[2,8,1]{1,2,0:T(1,128)} %param.19) | copy-start | bytes 196
  60.7 44.0 %copy-start.4 = (bf16[256]{0:T(256)(128)(2,1)S(1)}, bf16[256]{0:T(256)(128)(2,1)}, u32[]{:S(2)}) copy-start(bf16[256]{0:T(256)(128)(2,1)} %param.18) | copy-start | bytes 1540
  62.7 24.3 %copy-start.1 = (bf16[2,1,8,1024]{3,2,0,1:T(8,128)(2,1)}, bf16[2,1,8,1024]{3,2,0,1:T(8,128)(2,1)S(1)}, u32[]{:S(2)}) copy-start(bf16[2,1,8,1024]{3,2,0,1:T(8,128)(2,1)S(1)} %fusion.12) | copy-start | bytes 98308
  74.2 5.9 %collective-permute-start.1 = (bf16[1,8,1,256]{3,1,2,0:T(8,128)(2,1)S(1)}, bf16[1,8,1,256]{3,1,2,0:T(8,128)(2,1)S(1)}, u32[]{:S(2)}, u32[]{:S(2)}) collective-permute-start(bf16[1,8,1,256]{3,1,2,0:T(8,128)(2,1)S(1)} %get-tuple-element.25), channel_id=1, source_target_pairs={{8,0},{16,8},{24,16},{9,1},{17,9},{25,17},{10,2},{18,10},{26,18},{... | collective-permute-start | bytes 12296 | tf_op jit(solution)/shard_map/ppermute | solution.py:27
  75.5 5.9 %collective-permute-start = (bf16[1,8,1,256]{3,1,0,2:T(8,128)(2,1)S(1)}, bf16[1,8,1,256]{3,1,0,2:T(8,128)(2,1)S(1)}, u32[]{:S(2)}, u32[]{:S(2)}) collective-permute-start(bf16[1,8,1,256]{3,1,0,2:T(8,128)(2,1)S(1)} %get-tuple-element.24), channel_id=1, source_target_pairs={{0,8},{8,16},{16,24},{1,9},{9,17},{17,25},{2,10},{10,18},{18,26},{... | collective-permute-start | bytes 12296 | tf_op jit(solution)/shard_map/ppermute | solution.py:26
  81.4 2.6 %collective-permute-start.2 = (bf16[4,8,1,256]{3,1,0,2:T(8,128)(2,1)S(1)}, bf16[4,8,1,256]{3,1,0,2:T(8,128)(2,1)S(1)}, u32[]{:S(2)}, u32[]{:S(2)}) collective-permute-start(bf16[4,8,1,256]{3,1,0,2:T(8,128)(2,1)S(1)} %pad_maximum_fusion), channel_id=1, source_target_pairs={{0,1},{1,2},{2,3},{3,4},{4,5},{5,6},{6,7},{8,9},{9,10},{10,11},{11... | collective-permute-start | bytes 49160 | tf_op jit(solution)/shard_map/ppermute | solution.py:26
  82.6 4.0 %collective-permute-start.3 = (bf16[4,8,1,256]{3,1,0,2:T(8,128)(2,1)S(1)}, bf16[4,8,1,256]{3,1,0,2:T(8,128)(2,1)S(1)}, u32[]{:S(2)}, u32[]{:S(2)}) collective-permute-start(bf16[4,8,1,256]{3,1,0,2:T(8,128)(2,1)S(1)} %pad_maximum_fusion), channel_id=1, source_target_pairs={{1,0},{2,1},{3,2},{4,3},{5,4},{6,5},{7,6},{9,8},{10,9},{11,10},{12... | collective-permute-start | bytes 49160 | tf_op jit(solution)/shard_map/ppermute | solution.py:27
  88.2 5.5 %collective-permute-start.4 = (bf16[1,8,1,256]{3,1,2,0:T(8,128)(2,1)S(1)}, bf16[1,8,1,256]{3,1,2,0:T(8,128)(2,1)S(1)}, u32[]{:S(2)}, u32[]{:S(2)}) collective-permute-start(bf16[1,8,1,256]{3,1,2,0:T(8,128)(2,1)S(1)} %get-tuple-element.22), channel_id=1, source_target_pairs={{0,8},{8,16},{16,24},{1,9},{9,17},{17,25},{2,10},{10,18},{18,26},{... | collective-permute-start | bytes 12296 | tf_op jit(solution)/shard_map/ppermute | solution.py:26
  92.4 5.9 %collective-permute-start.5 = (bf16[1,8,1,256]{3,1,2,0:T(8,128)(2,1)S(1)}, bf16[1,8,1,256]{3,1,2,0:T(8,128)(2,1)S(1)}, u32[]{:S(2)}, u32[]{:S(2)}) collective-permute-start(bf16[1,8,1,256]{3,1,2,0:T(8,128)(2,1)S(1)} %get-tuple-element.23), channel_id=1, source_target_pairs={{8,0},{16,8},{24,16},{9,1},{17,9},{25,17},{10,2},{18,10},{26,18},{... | collective-permute-start | bytes 12296 | tf_op jit(solution)/shard_map/ppermute | solution.py:27
  98.9 8.2 %collective-permute-start.6 = (bf16[4,8,1,256]{3,1,0,2:T(8,128)(2,1)}, bf16[4,8,1,256]{3,1,0,2:T(8,128)(2,1)}, u32[]{:S(2)}, u32[]{:S(2)}) collective-permute-start(bf16[4,8,1,256]{3,1,0,2:T(8,128)(2,1)} %pad_maximum_fusion.1), channel_id=1, source_target_pairs={{0,1},{1,2},{2,3},{3,4},{4,5},{5,6},{6,7},{8,9},{9,10},{10,11},{11... | collective-permute-start | bytes 49160 | tf_op jit(solution)/shard_map/ppermute | solution.py:26
  102.7 4.4 %collective-permute-start.7 = (bf16[4,8,1,256]{3,1,0,2:T(8,128)(2,1)}, bf16[4,8,1,256]{3,1,0,2:T(8,128)(2,1)}, u32[]{:S(2)}, u32[]{:S(2)}) collective-permute-start(bf16[4,8,1,256]{3,1,0,2:T(8,128)(2,1)} %pad_maximum_fusion.1), channel_id=1, source_target_pairs={{1,0},{2,1},{3,2},{4,3},{5,4},{6,5},{7,6},{9,8},{10,9},{11,10},{12... | collective-permute-start | bytes 49160 | tf_op jit(solution)/shard_map/ppermute | solution.py:27
  107.1 7.7 %copy-start.3 = (f32[16]{0:T(128)S(1)}, f32[16]{0:T(128)}, u32[]{:S(2)}) copy-start(f32[16]{0:T(128)} %convert_element_type.63) | copy-start | bytes 196
  107.1 7.7 %copy-start.5 = (bf16[256,1]{0,1:T(2,128)(2,1)S(1)}, bf16[256,1]{0,1:T(2,128)(2,1)}, u32[]{:S(2)}) copy-start(bf16[256,1]{0,1:T(2,128)(2,1)} %reshape.324) | copy-start | bytes 1540
  163.1 6.2 %collective-permute-start.8 = (bf16[1,8,1,256]{3,1,2,0:T(8,128)(2,1)S(1)}, bf16[1,8,1,256]{3,1,2,0:T(8,128)(2,1)S(1)}, u32[]{:S(2)}, u32[]{:S(2)}) collective-permute-start(bf16[1,8,1,256]{3,1,2,0:T(8,128)(2,1)S(1)} %get-tuple-element.20), channel_id=1, source_target_pairs={{0,8},{8,16},{16,24},{1,9},{9,17},{17,25},{2,10},{10,18},{18,26},{... | collective-permute-start | bytes 12296 | tf_op jit(solution)/shard_map/ppermute | solution.py:26
  167.3 5.5 %collective-permute-start.9 = (bf16[1,8,1,256]{3,1,2,0:T(8,128)(2,1)S(1)}, bf16[1,8,1,256]{3,1,2,0:T(8,128)(2,1)S(1)}, u32[]{:S(2)}, u32[]{:S(2)}) collective-permute-start(bf16[1,8,1,256]{3,1,2,0:T(8,128)(2,1)S(1)} %get-tuple-element.21), channel_id=1, source_target_pairs={{8,0},{16,8},{24,16},{9,1},{17,9},{25,17},{10,2},{18,10},{26,18},{... | collective-permute-start | bytes 12296 | tf_op jit(solution)/shard_map/ppermute | solution.py:27
  172.8 2.6 %collective-permute-start.10 = (bf16[4,8,1,256]{3,1,0,2:T(8,128)(2,1)S(1)}, bf16[4,8,1,256]{3,1,0,2:T(8,128)(2,1)S(1)}, u32[]{:S(2)}, u32[]{:S(2)}) collective-permute-start(bf16[4,8,1,256]{3,1,0,2:T(8,128)(2,1)S(1)} %pad_maximum_fusion.2), channel_id=1, source_target_pairs={{0,1},{1,2},{2,3},{3,4},{4,5},{5,6},{6,7},{8,9},{9,10},{10,11},{11... | collective-permute-start | bytes 49160 | tf_op jit(solution)/shard_map/ppermute | solution.py:26
  174.1 4.0 %collective-permute-start.11 = (bf16[4,8,1,256]{3,1,0,2:T(8,128)(2,1)S(1)}, bf16[4,8,1,256]{3,1,0,2:T(8,128)(2,1)S(1)}, u32[]{:S(2)}, u32[]{:S(2)}) collective-permute-start(bf16[4,8,1,256]{3,1,0,2:T(8,128)(2,1)S(1)} %pad_maximum_fusion.2), channel_id=1, source_target_pairs={{1,0},{2,1},{3,2},{4,3},{5,4},{6,5},{7,6},{9,8},{10,9},{11,10},{12... | collective-permute-start | bytes 49160 | tf_op jit(solution)/shard_map/ppermute | solution.py:27
  182.2 5.9 %collective-permute-start.12 = (bf16[1,8,1,256]{3,1,2,0:T(8,128)(2,1)S(1)}, bf16[1,8,1,256]{3,1,2,0:T(8,128)(2,1)S(1)}, u32[]{:S(2)}, u32[]{:S(2)}) collective-permute-start(bf16[1,8,1,256]{3,1,2,0:T(8,128)(2,1)S(1)} %get-tuple-element.18), channel_id=1, source_target_pairs={{0,8},{8,16},{16,24},{1,9},{9,17},{17,25},{2,10},{10,18},{18,26},{... | collective-permute-start | bytes 12296 | tf_op jit(solution)/shard_map/ppermute | solution.py:26
  186.7 5.5 %collective-permute-start.13 = (bf16[1,8,1,256]{3,1,2,0:T(8,128)(2,1)S(1)}, bf16[1,8,1,256]{3,1,2,0:T(8,128)(2,1)S(1)}, u32[]{:S(2)}, u32[]{:S(2)}) collective-permute-start(bf16[1,8,1,256]{3,1,2,0:T(8,128)(2,1)S(1)} %get-tuple-element.19), channel_id=1, source_target_pairs={{8,0},{16,8},{24,16},{9,1},{17,9},{25,17},{10,2},{18,10},{26,18},{... | collective-permute-start | bytes 12296 | tf_op jit(solution)/shard_map/ppermute | solution.py:27
  192.2 4.3 %collective-permute-start.14 = (bf16[4,8,1,256]{3,1,0,2:T(8,128)(2,1)S(1)}, bf16[4,8,1,256]{3,1,0,2:T(8,128)(2,1)S(1)}, u32[]{:S(2)}, u32[]{:S(2)}) collective-permute-start(bf16[4,8,1,256]{3,1,0,2:T(8,128)(2,1)S(1)} %pad_maximum_fusion.3), channel_id=1, source_target_pairs={{0,1},{1,2},{2,3},{3,4},{4,5},{5,6},{6,7},{8,9},{9,10},{10,11},{11... | collective-permute-start | bytes 49160 | tf_op jit(solution)/shard_map/ppermute | solution.py:26
  195.2 4.0 %collective-permute-start.15 = (bf16[4,8,1,256]{3,1,0,2:T(8,128)(2,1)S(1)}, bf16[4,8,1,256]{3,1,0,2:T(8,128)(2,1)S(1)}, u32[]{:S(2)}, u32[]{:S(2)}) collective-permute-start(bf16[4,8,1,256]{3,1,0,2:T(8,128)(2,1)S(1)} %pad_maximum_fusion.3), channel_id=1, source_target_pairs={{1,0},{2,1},{3,2},{4,3},{5,4},{6,5},{7,6},{9,8},{10,9},{11,10},{12... | collective-permute-start | bytes 49160 | tf_op jit(solution)/shard_map/ppermute | solution.py:27
  220.1 10.6 %all-to-all-start.2 = ((bf16[2,8,1,1024]{3,0,2,1:T(2,128)(2,1)}), bf16[2,8,1,1024]{3,0,2,1:T(2,128)(2,1)}, u32[]{:S(2)}, u32[]{:S(2)}) async-start(bf16[2,8,1,1024]{3,0,2,1:T(2,128)(2,1)} %copy.78), calls=%async_computation.2 | async-start | bytes 65536 | tf_op jit(solution)/shard_map/all_to_all | solution.py:175
Sparse Core Ops, SparseCore 0:
  9.9 38.0 all-gather.1
where the time goes:
time: 242 us; the launch traced here: 240 us
  blocking collectives  93.2 us (39%)
  starting transfers between devices  41.9 us (17%)
  local copies, waits for them, and re-layouts  32.6 us (13%)
  waiting for transfers between devices  26.9 us (11%)
  between operations  19.8 us (8%)
  matrix products  17.3 us (7%)
  other arithmetic  8.34 us (3%)
    psum x1, blocking collectives, on_device(): lax.psum((jnp.sum(probability * fault_mask), jnp.sum(probability), jnp.su...  41.7 us
    ppermute x8, starting transfers between devices, padded_2(): before = lax.ppermute(last, axis, up)  26.8 us
    unnamed x109, local copies, waits for them, and re-layouts  20.8 us
    ppermute x8, waiting for transfers between devices, padded_2(): after = lax.ppermute(first, axis, down)  20.4 us
    all_gather x1, blocking collectives, on_device(): lax.all_gather(key_rows, 'tok', axis=0, tiled=True)  17.3 us
    all_gather x1, blocking collectives, on_device(): lax.all_gather(value_rows, 'tok', axis=0, tiled=True)  15.5 us
    ppermute x8, starting transfers between devices, padded_2(): after = lax.ppermute(first, axis, down)  10.3 us
    all_to_all x1, blocking collectives, on_device(): lax.all_to_all(encoded, 'tok', split_axis=2, concat_axis=1, tiled=True)  10.2 us
  transfers between devices with their start and end apart: 18, of which 8 were waited for; matrix products, arithmetic and copies ran while one was open for 6% of the time, Pallas kernels for 0%

commit v1 on v0

--- a/solution.py
+++ b/solution.py
@@ -1,9 +1,15 @@
+import functools
+
 import jax
 import jax.numpy as jnp
 from jax import lax
+from jax.experimental import pallas as pl
+from jax.experimental.pallas import tpu as pltpu
 from jax.sharding import PartitionSpec as P
 
 HD = 64
+F32 = jnp.float32
+BF16 = jnp.bfloat16
 
 
 OFFSETS = [
@@ -84,7 +90,7 @@
     return (new_peak, totals, weighted_sum)
 
 
-def on_device(
+def on_tiles(
     queries, key_rows, value_rows, residual, w_out, w_neck, w_first, w_second, w_class, labels
 ):
     width_here = queries.shape[-1]
@@ -176,6 +182,354 @@
     return (encoded, dice_loss, grad_encoded)
 
 
+def dot(a, b):
+    return jnp.dot(a, b, preferred_element_type=F32)
+
+
+def dot_t(a, b):
+    return lax.dot_general(a, b, (((1,), (1,)), ((), ())), preferred_element_type=F32)
+
+
+def sigma_of(v):
+    return 1.0 / (1.0 + jnp.exp(-v))
+
+
+def slope_of(v):
+    s = sigma_of(v)
+    return s * (1.0 + v * (1.0 - s))
+
+
+def iota(shape, dim):
+    return lax.broadcasted_iota(jnp.int32, shape, dim)
+
+
+def along_inline(value, step, inline):
+    if step == 0:
+        return value
+    rows = value.shape[0]
+    x = iota(value.shape, 0) % inline
+    edge = inline - 1 if step > 0 else 0
+    return jnp.where(x == edge, 0.0, pltpu.roll(value, (-step) % rows, axis=0))
+
+
+def along_rows(value, step):
+    if step == 0:
+        return value
+    zeros = jnp.zeros((abs(step), value.shape[1]), value.dtype)
+    if step > 0:
+        return jnp.concatenate([value[step:], zeros], axis=0)
+    return jnp.concatenate([zeros, value[:step]], axis=0)
+
+
+def pack_kernel(place, q_ref, k_ref, v_ref, r_ref, neck_ref, lab_ref, out_ref):
+    rows = q_ref.shape[1] * q_ref.shape[2]
+    width = q_ref.shape[3]
+    for i, ref in enumerate((q_ref, k_ref, v_ref)):
+        flat = ref[...].astype(F32).reshape(rows, width).astype(BF16)
+        out_ref[i * rows : (i + 1) * rows, :] = flat
+    own = r_ref.shape[0] * r_ref.shape[2]
+    residual = r_ref[...].astype(F32).reshape(own, r_ref.shape[3]).astype(BF16)
+    out_ref[3 * rows : 3 * rows + own, :] = dot(residual, neck_ref[...]).astype(BF16)
+    count = lab_ref.shape[0] * lab_ref.shape[1]
+    labels = lab_ref[...].astype(F32).reshape(count, 1)
+    out_ref[3 * rows + own :, :] = jnp.where(
+        iota((count, width), 1) == place[3], labels, 0.0
+    ).astype(BF16)
+
+
+def attention_kernel(zs, rows, own, *refs):
+    place = refs[0]
+    ours, theirs = refs[1 : 1 + zs], refs[1 + zs : 1 + 2 * zs]
+    out_w, neck_w = refs[1 + 2 * zs : 3 + 2 * zs]
+    part_ref = refs[3 + 2 * zs]
+    enc_refs = refs[4 + 2 * zs : -4]
+    qq, kk, vv, part = refs[-4:]
+    z, core, h = place[0], place[1], place[2]
+    width = qq.shape[1]
+    queries_n, keys_n = qq.shape[0], kk.shape[0]
+    labels = jnp.zeros((ours[0].shape[0] - 3 * rows - own, width), F32)
+    for d in range(zs):
+        qq[d * rows : (d + 1) * rows, :] = ours[d][0:rows, :]
+        for ref, side in ((ours[d], core), (theirs[d], 1 - core)):
+            at = pl.multiple_of((2 * (z ^ d) + side) * rows, rows)
+            kk[pl.ds(at, rows), :] = ref[rows : 2 * rows, :]
+            vv[pl.ds(at, rows), :] = ref[2 * rows : 3 * rows, :]
+            labels = labels + ref[3 * rows + own :, :].astype(F32)
+    heads_here = width // HD
+    scale = HD ** (-0.5)
+    query = qq[...]
+    keys, values = kk[...], vv[...]
+    lane_head = iota((queries_n, width), 1) // HD
+    attended = jnp.zeros((queries_n, width), F32)
+    for head in range(heads_here):
+        mine = lane_head == head
+        scores = dot_t(jnp.where(mine, query, jnp.zeros_like(query)), keys) * scale
+        raw = jnp.exp(scores - jnp.max(scores, axis=1, keepdims=True))
+        total = jnp.sum(raw, axis=1, keepdims=True)
+        mixed = dot(raw.astype(BF16), values)
+        attended = jnp.where(mine, mixed / total, attended)
+    product = dot(attended.astype(BF16), out_w[...])
+    part[...] = dot(product.astype(BF16), neck_w[...])
+    for d in range(zs):
+        at = pl.multiple_of(d * rows + h * own, own)
+        part[pl.ds(at, own), :] += ours[d][3 * rows : 3 * rows + own, :].astype(F32)
+    part_ref[0:queries_n, :] = part[...].astype(BF16)
+    part_ref[queries_n:, :] = labels.astype(BF16)
+    first = product[0:rows, :]
+    blocks = [first[i * own : (i + 1) * own, :] for i in range(rows // own)]
+    for d, ref in enumerate(enc_refs):
+        picked = blocks[0]
+        for i in range(1, len(blocks)):
+            picked = jnp.where((h ^ d) == i, blocks[i], picked)
+        ref[...] = picked.astype(BF16)
+
+
+def decoder_kernel(sizes, place, ours, theirs, first_w, second_w, class_w, neck_w, loss_ref, grad_ref, *scratch):
+    nc, nt, ni, own_c, zs = sizes
+    grid, cols, slope1, grad2, cols3, w1, w2, sems = scratch
+    channels = grid.shape[2]
+    slab = nt * ni
+    rows = nc * ni
+    cells = nc * slab
+    z, core, h, tslab = place[0], place[1], place[2], place[4]
+    taps = 9
+    copies = []
+    for i, (src, dst) in enumerate(((first_w, w1), (second_w, w2))):
+        for a in range(3):
+            copies.append(pltpu.make_async_copy(src.at[a], dst.at[a], sems.at[3 * i + a]))
+            copies[-1].start()
+
+    for d in range(zs):
+        for ref, side in ((ours, core), (theirs, 1 - core)):
+            block = ref[d * rows : (d + 1) * rows, :].astype(F32)
+            at = pl.multiple_of((2 * (z ^ d) + side) * ni, ni)
+            for c in range(nc):
+                grid[c, pl.ds(at, ni), :] = block[c * ni : (c + 1) * ni, :]
+
+    slope1[...] = jnp.zeros_like(slope1)
+    grad2[...] = jnp.zeros_like(grad2)
+    edge = jnp.zeros((slab, taps * channels), BF16)
+    cols[0:slab, :] = edge
+    cols[(nc + 1) * slab :, :] = edge
+
+    def spread(value, c):
+        for e in range(3):
+            moved = along_inline(value, e - 1, ni)
+            for b in range(3):
+                lane = (b * 3 + e) * channels
+                cols[(c + 1) * slab : (c + 2) * slab, lane : lane + channels] = along_rows(
+                    moved, (b - 1) * ni
+                ).astype(BF16)
+
+    def conv(weights, base):
+        total = None
+        for a in range(3):
+            if base is not None:
+                copies[base + a].wait()
+            matrix = weights[a].reshape(taps * channels, channels)
+            term = dot(cols[a * slab : a * slab + cells, :], matrix)
+            total = term if total is None else total + term
+        return total
+
+    for c in range(nc):
+        spread(grid[c], c)
+    hidden_one = conv(w1, 0)
+    for c in range(nc):
+        v = hidden_one[c * slab : (c + 1) * slab, :]
+        s = sigma_of(v)
+        slope1[c + 1, ni : ni + slab, :] = s * (1.0 + v * (1.0 - s))
+        spread((v * s).astype(BF16).astype(F32), c)
+    hidden_two = conv(w2, 3)
+    sigma_two = sigma_of(hidden_two)
+    active_two = (hidden_two * sigma_two).astype(BF16)
+    class_row = class_w[...].astype(F32)
+    logits = dot_t(active_two, jnp.broadcast_to(class_row, (128, channels)).astype(BF16))
+    probability = sigma_of(logits)
+    lab_rows = ours.shape[0] - rows * zs
+    lab = ours[rows * zs :, 0:128].astype(F32).reshape(own_c, nt, 1, 128)
+    spread_lab = jnp.broadcast_to(lab[None], (nc // own_c, own_c, nt, ni, 128)).reshape(cells, 128)
+    row = iota((cells, 128), 0)
+    wanted = (row // (slab * own_c)) * nt + row % ni
+    picked = jnp.where(iota((cells, 128), 1) == wanted, spread_lab, 0.0).astype(BF16)
+    mask = dot(picked, jnp.ones((128, 128), BF16))
+    intersection = jnp.sum(probability * mask, axis=0, keepdims=True)
+    total_prob = jnp.sum(probability, axis=0, keepdims=True)
+    total_fault = jnp.sum(mask, axis=0, keepdims=True)
+    denominator = total_prob + total_fault
+    loss_ref[...] = 1.0 - 2.0 * intersection / denominator
+    grad_logits = (
+        LOSS_SCALE
+        * float(cells)
+        * -2.0
+        * (mask * denominator - intersection)
+        / (denominator * denominator)
+        * probability
+        * (1.0 - probability)
+    )
+    wide = jnp.concatenate([grad_logits] * (channels // 128), axis=1)
+    slope_two = sigma_two * (1.0 + hidden_two * (1.0 - sigma_two))
+    g2 = wide * class_row * slope_two
+    for c in range(nc):
+        grad2[c + 2, 2 * ni : 2 * ni + slab, :] = g2[c * slab : (c + 1) * slab, :]
+
+    band = 4 * ni
+    c0 = h * own_c
+    t0 = pl.multiple_of(tslab * ni, ni)
+    for i in range(own_c + 4):
+        region = grad2[c0 + i, pl.ds(t0, band + 2 * ni), :]
+        for e in range(3):
+            moved = along_inline(region, 1 - e, ni)
+            for b in range(3):
+                lane = (b * 3 + e) * channels
+                cols3[i * band : (i + 1) * band, lane : lane + channels] = moved[
+                    (2 - b) * ni : (2 - b) * ni + band, :
+                ].astype(BF16)
+    out3 = (own_c + 2) * band
+    total = jnp.zeros((out3, channels), F32)
+    for a in range(3):
+        for b in range(3):
+            for e in range(3):
+                lane = (b * 3 + e) * channels
+                piece = cols3[(2 - a) * band : (2 - a) * band + out3, lane : lane + channels]
+                total = total + dot_t(piece, w2[a, b, e])
+    slopes = [slope1[c0 + i, pl.ds(t0, band), :] for i in range(own_c + 2)]
+    g1 = (total * jnp.concatenate(slopes, axis=0)).astype(BF16).astype(F32)
+    shifted = [along_inline(g1, 1 - e, ni) for e in range(3)]
+    total = jnp.zeros((own_c * ni, channels), F32)
+    for a in range(3):
+        for b in range(3):
+            for e in range(3):
+                cells_in = [
+                    shifted[e][(i + 2 - a) * band + (2 - b) * ni : (i + 2 - a) * band + (3 - b) * ni, :]
+                    for i in range(own_c)
+                ]
+                piece = jnp.concatenate(cells_in, axis=0).astype(BF16)
+                total = total + dot_t(piece, w1[a, b, e])
+    grad = dot_t(total.astype(BF16), neck_w[...])
+    grad_ref[...] = grad.reshape(grad_ref.shape).astype(BF16)
+
+
+def vmem():
+    return pl.BlockSpec(memory_space=pltpu.VMEM)
+
+
+def smem():
+    return pl.BlockSpec(memory_space=pltpu.SMEM)
+
+
+def whole_grid(
+    queries, key_rows, value_rows, residual, w_out, w_neck, w_first, w_second, w_class, labels
+):
+    heads_n, tok_n = lax.axis_size("heads"), lax.axis_size("tok")
+    zs = tok_n // 2
+    _, nc, ni, width = queries.shape
+    own_c = residual.shape[0]
+    nt = labels.shape[1]
+    channels = w_neck.shape[1]
+    rows, own, lab = nc * ni, own_c * ni, own_c * nt
+    h, t = lax.axis_index("heads"), lax.axis_index("tok")
+    place = jnp.stack([t // 2, t % 2, h, h * tok_n + t, t]).astype(jnp.int32)
+
+    def swap_tok(value, bits):
+        return lax.ppermute(value, "tok", [(i, i ^ bits) for i in range(tok_n)])
+
+    def swap_heads(value, bits):
+        return lax.ppermute(value, "heads", [(i, i ^ bits) for i in range(heads_n)])
+
+    packed = pl.pallas_call(
+        pack_kernel,
+        out_shape=jax.ShapeDtypeStruct((3 * rows + own + lab, width), BF16),
+        in_specs=[smem()] + [vmem()] * 6,
+        out_specs=vmem(),
+    )(place, queries, key_rows, value_rows, residual, w_neck, labels)
+    ours = [packed] + [swap_tok(packed, 2 * d) for d in range(1, zs)]
+    theirs = [swap_tok(value, 1) for value in ours]
+    enc_shape = jax.ShapeDtypeStruct((own, residual.shape[3]), BF16)
+    queries_n, keys_n = rows * zs, rows * tok_n
+    out = pl.pallas_call(
+        functools.partial(attention_kernel, zs, rows, own),
+        out_shape=[jax.ShapeDtypeStruct((queries_n + lab, channels), BF16)] + [enc_shape] * heads_n,
+        in_specs=[smem()] + [vmem()] * (2 * zs + 2),
+        out_specs=[vmem()] * (1 + heads_n),
+        scratch_shapes=[
+            pltpu.VMEM((queries_n, width), BF16),
+            pltpu.VMEM((keys_n, width), BF16),
+            pltpu.VMEM((keys_n, width), BF16),
+            pltpu.VMEM((queries_n, channels), F32),
+        ],
+        compiler_params=pltpu.CompilerParams(vmem_limit_bytes=32 * 2**20),
+    )(place, *ours, *theirs, w_out, w_neck)
+    parts = [out[0]] + [swap_heads(out[0], d) for d in range(1, heads_n)]
+    pieces = [out[1]] + [swap_heads(out[1 + d], d) for d in range(1, heads_n)]
+
+    def pairwise(values):
+        values = [v.astype(F32) for v in values]
+        while len(values) > 1:
+            values = [values[i] + values[i + 1] for i in range(0, len(values), 2)]
+        return values[0]
+
+    half = pairwise(parts).astype(BF16)
+    other = swap_tok(half, 1)
+    encoded = (residual.astype(F32) + pairwise(pieces).reshape(residual.shape)).astype(BF16)
+
+    slab = nt * ni
+    loss, grad = pl.pallas_call(
+        functools.partial(decoder_kernel, (nc, nt, ni, own_c, zs)),
+        out_shape=[
+            jax.ShapeDtypeStruct((1, 128), F32),
+            jax.ShapeDtypeStruct(residual.shape, BF16),
+        ],
+        in_specs=[smem(), vmem(), vmem()]
+        + [pl.BlockSpec(memory_space=pl.ANY)] * 2
+        + [vmem(), vmem()],
+        out_specs=[vmem(), vmem()],
+        scratch_shapes=[
+            pltpu.VMEM((nc, slab, channels), F32),
+            pltpu.VMEM(((nc + 2) * slab, 9 * channels), BF16),
+            pltpu.VMEM((nc + 2, (nt + 4) * ni, channels), F32),
+            pltpu.VMEM((nc + 4, (nt + 6) * ni, channels), F32),
+            pltpu.VMEM(((own_c + 4) * 4 * ni, 9 * channels), BF16),
+            pltpu.VMEM(w_first.shape, BF16),
+            pltpu.VMEM(w_second.shape, BF16),
+            pltpu.SemaphoreType.DMA((6,)),
+        ],
+        compiler_params=pltpu.CompilerParams(vmem_limit_bytes=40 * 2**20),
+    )(place, half, other, w_first, w_second, w_class.reshape(1, channels), w_neck)
+    return (encoded, loss[0, 0], grad)
+
+
+def power_of_two(n):
+    return n > 0 and n & (n - 1) == 0
+
+
+def fits_whole(queries, residual, w_neck, labels):
+    heads_n, tok_n = lax.axis_size("heads"), lax.axis_size("tok")
+    slabs, nc, ni, width = queries.shape
+    nt = labels.shape[1]
+    return (
+        slabs == 1
+        and labels.shape[2] == 1
+        and ni == 8
+        and nt == tok_n
+        and tok_n >= 4
+        and power_of_two(tok_n)
+        and power_of_two(heads_n)
+        and heads_n * tok_n <= 128
+        and nc * nt * ni <= 1024
+        and width % 128 == 0
+        and w_neck.shape[1] == width
+        and (residual.shape[0] * ni) % 16 == 0
+        and (residual.shape[0] * nt) % 16 == 0
+    )
+
+
+def on_device(*arguments):
+    queries, residual, w_neck, labels = (arguments[i] for i in (0, 3, 5, 9))
+    if fits_whole(queries, residual, w_neck, labels):
+        return whole_grid(*arguments)
+    return on_tiles(*arguments)
+
+
 def solution(mesh):
     placed = (
         P("tok", None, None, "heads"),

time: 242 us -> 59.4 us (0.25)
  blocking collectives: 93.2 us -> 0 us
  starting transfers between devices: 41.9 us -> 14.6 us
  local copies, waits for them, and re-layouts: 32.6 us -> 10.4 us
  Pallas kernels: 0 us -> 19.4 us
  between operations: 19.8 us -> 0.73 us
  matrix products: 17.3 us -> 0 us
  waiting for transfers between devices: 26.9 us -> 13.1 us
  other arithmetic: 8.34 us -> 0.72 us
    psum x1 -> x0, blocking collectives: 41.7 us -> none  [on_device(): lax.psum((jnp.sum(probability * fault_mask), jnp.sum(probability), jnp.su...]
    all_gather x2 -> x0, blocking collectives: 32.8 us -> none  [the longest x1 17.3 us: on_device(): lax.all_gather(key_rows, 'tok', axis=0, tiled=True)]
    ppermute x16 -> x14, starting transfers between devices: 37.1 us -> 14.6 us  [the longest x6 8.37 us: swap_heads(): return lax.ppermute(value, 'heads', [(i, i ^ bits) for i in range(heads_n)])]
    pallas_call x0 -> x3, Pallas kernels: none -> 19.4 us  [the longest x1 15.3 us: whole_grid(): pl.pallas_call(functools.partial(decoder_kernel, (nc, nt, ni, own_c, zs))...]
    all_to_all x2 -> x0, blocking collectives: 18.7 us -> none  [the longest x1 10.2 us: on_device(): lax.all_to_all(encoded, 'tok', split_axis=2, concat_axis=1, tiled=True)]
    dot_general x9 -> x0, matrix products: 17.3 us -> none  [the longest x3 6.73 us: conv_apply(): lax.dot_general(columns, kernel, contraction, preferred_element_type=jnp....]
    unnamed x109 -> x19, local copies, waits for them, and re-layouts: 20.8 us -> 9.09 us
    ppermute x16 -> x14, waiting for transfers between devices: 21.7 us -> 13.1 us  [the longest x8 10.3 us: swap_tok(): return lax.ppermute(value, 'tok', [(i, i ^ bits) for i in range(tok_n)])]
  transfers between devices with their start and end apart: 18 -> 14, of which waited for: 8 -> 8; matrix products, arithmetic and copies ran while one was open for 6% -> 2% of each run, Pallas kernels for 0% -> 0%
where the time goes in v1:
time: 59.4 us; the launch traced here: 59 us
  Pallas kernels  19.4 us (33%)
  starting transfers between devices  14.6 us (25%)
  waiting for transfers between devices  13.1 us (22%)
  local copies, waits for them, and re-layouts  10.4 us (18%)
  between operations  0.73 us (1%)
  other arithmetic  0.72 us (1%)
    pallas_call x1, Pallas kernels, whole_grid(): pl.pallas_call(functools.partial(decoder_kernel, (nc, nt, ni, own_c, zs))...  15.3 us
    ppermute x8, waiting for transfers between devices, swap_tok(): return lax.ppermute(value, 'tok', [(i, i ^ bits) for i in range(tok_n)])  10.3 us
    unnamed x19, local copies, waits for them, and re-layouts  9.09 us
    ppermute x6, starting transfers between devices, swap_heads(): return lax.ppermute(value, 'heads', [(i, i ^ bits) for i in range(heads_n)])  8.37 us
    ppermute x8, starting transfers between devices, swap_tok(): return lax.ppermute(value, 'tok', [(i, i ^ bits) for i in range(tok_n)])  6.2 us
    ppermute x6, waiting for transfers between devices, swap_heads(): return lax.ppermute(value, 'heads', [(i, i ^ bits) for i in range(heads_n)])  2.87 us
    pallas_call x1, Pallas kernels, whole_grid(): pl.pallas_call(functools.partial(attention_kernel, zs, rows, own), out_sh...  2.12 us
    pallas_call x1, Pallas kernels, whole_grid(): pl.pallas_call(pack_kernel, out_shape=jax.ShapeDtypeStruct((3 * rows + ow...  1.96 us
  transfers between devices with their start and end apart: 14, of which 8 were waited for; matrix products, arithmetic and copies ran while one was open for 2% of the time, Pallas kernels for 0%

profile of v1, /device:TPU:0, one launch (start us, length us, event | category | flops | bytes accessed | tf_op | source)
XLA Modules:
  0.0 59.0 jit_solution(18025571358054436435)
XLA Ops:
  0.7 1.4 %copy.13.lab_ref = s32[2,8,1]{2,1,0:T(8,128)} copy(s32[2,8,1]{1,2,0:T(1,128)} %param.19) | data formatting | bytes 128 | tf_op args[9]
  2.1 0.7 %stack.23.place.refs_0_ = s32[5]{0:T(128)} concatenate(s32[1]{0:T(128)} %bitcast, s32[1]{0:T(128)} %bitcast.1, s32[1]{0:T(128)} %bitcast.2, s32[1]{0:T(128)} %bitcast.3, s32[1]{0:T(128)} %bitcast.4), dimensions={0} | concatenate | bytes 40 | tf_op jit(solution)/shard_map/stack | solution.py:431
  2.8 2.0 %shard_map.121.refs_1_ = bf16[224,256]{1,0:T(8,128)(2,1)} custom-call(s32[5]{0:T(128)} %stack.23.place.refs_0_, bf16[1,8,8,256]{3,2,1,0:T(8,128)(2,1)} %q_ref.1, bf16[1,8,8,256]{3,2,1,0:T(8,128)(2,1)} %k_ref.1, bf16[1,8,8,256]{3,2,1,0:T(8,128)(2,1)} %v_ref.1, bf16[2,1,8,1024]{3,2,1,0:T(8,128)(2,1)} %r_ref.1, bf16[1024,256]{1,0:T(8,128)(2,1)} %neck_w.1, ...), custom_call_target="tpu_custom_call" | custom-call | tf_op jit(solution)/shard_map/pallas_call | solution.py:439
  4.7 3.0 %collective-permute-start = (bf16[224,256]{1,0:T(8,128)(2,1)}, bf16[224,256]{1,0:T(8,128)(2,1)S(1)}, u32[]{:S(2)}, u32[]{:S(2)}) collective-permute-start(bf16[224,256]{1,0:T(8,128)(2,1)} %shard_map.121.refs_1_), channel_id=1, source_target_pairs={{0,2},{1,3},{2,0},{3,1},{4,6},{5,7},{6,4},{7,5},{8,10},{9,11},{10,... | collective-permute-start | bytes 344072 | tf_op jit(solution)/shard_map/ppermute | solution.py:434
  7.8 2.6 %collective-permute-start.1 = (bf16[224,256]{1,0:T(8,128)(2,1)}, bf16[224,256]{1,0:T(8,128)(2,1)S(1)}, u32[]{:S(2)}, u32[]{:S(2)}) collective-permute-start(bf16[224,256]{1,0:T(8,128)(2,1)} %shard_map.121.refs_1_), channel_id=1, source_target_pairs={{0,4},{1,5},{2,6},{3,7},{4,0},{5,1},{6,2},{7,3},{8,12},{9,13},{10,... | collective-permute-start | bytes 344072 | tf_op jit(solution)/shard_map/ppermute | solution.py:434
  10.3 0.8 %collective-permute-done.refs_2_ = bf16[224,256]{1,0:T(8,128)(2,1)S(1)} collective-permute-done((bf16[224,256]{1,0:T(8,128)(2,1)}, bf16[224,256]{1,0:T(8,128)(2,1)S(1)}, u32[]{:S(2)}, u32[]{:S(2)}) %collective-permute-start) | collective-permute-done | bytes 114720 | tf_op jit(solution)/shard_map/ppermute | solution.py:434
  11.1 8.5 %collective-permute-done.1.refs_3_ = bf16[224,256]{1,0:T(8,128)(2,1)S(1)} collective-permute-done((bf16[224,256]{1,0:T(8,128)(2,1)}, bf16[224,256]{1,0:T(8,128)(2,1)S(1)}, u32[]{:S(2)}, u32[]{:S(2)}) %collective-permute-start.1) | collective-permute-done | bytes 114720 | tf_op jit(solution)/shard_map/ppermute | solution.py:434
  19.7 0.5 collective-permute-start.6
  20.2 0.8 %collective-permute-done.5.refs_7_ = bf16[224,256]{1,0:T(8,128)(2,1)S(1)} collective-permute-done((bf16[224,256]{1,0:T(8,128)(2,1)S(1)}, bf16[224,256]{1,0:T(8,128)(2,1)S(1)}, u32[]{:S(2)}, u32[]{:S(2)}) %collective-permute-start.5) | collective-permute-done | bytes 114720 | tf_op jit(solution)/shard_map/ppermute | solution.py:434
  21.0 0.2 collective-permute-done.6.refs_8_
  21.1 1.0 %copy-done = bf16[1024,256]{1,0:T(8,128)(2,1)S(1)} copy-done((bf16[1024,256]{1,0:T(8,128)(2,1)S(1)}, bf16[1024,256]{1,0:T(8,128)(2,1)}, u32[]{:S(2)}) %copy-start) | copy-done | bytes 524312
  22.2 1.0 %copy-done.4 = bf16[256,1024]{1,0:T(8,128)(2,1)S(1)} copy-done((bf16[256,1024]{1,0:T(8,128)(2,1)S(1)}, bf16[256,1024]{1,0:T(8,128)(2,1)}, u32[]{:S(2)}) %copy-start.4) | copy-done | bytes 524312
  23.2 0.9 %copy-done.5 = bf16[224,256]{1,0:T(8,128)(2,1)S(1)} copy-done((bf16[224,256]{1,0:T(8,128)(2,1)S(1)}, bf16[224,256]{1,0:T(8,128)(2,1)}, u32[]{:S(2)}) %copy-start.5) | copy-done | bytes 114712
  24.1 0.7 %copy-done.6 = s32[5]{0:T(128)S(1)} copy-done((s32[5]{0:T(128)S(1)}, s32[5]{0:T(128)}, u32[]{:S(2)}) %copy-start.6) | copy-done | bytes 44
  24.8 2.1 %shard_map.122 = (bf16[272,256]{1,0:T(8,128)(2,1)S(1)}, bf16[16,1024]{1,0:T(8,128)(2,1)S(1)}, bf16[16,1024]{1,0:T(8,128)(2,1)S(1)}, bf16[16,1024]{1,0:T(8,128)(2,1)S(1)}, bf16[16,1024]{1,0:T(8,128)(2,1)S(1)}) custom-call(s32[5]{0:T(128)S(1)} %copy-done.6, bf16[224,256]{1,0:T(8,128)(2,1)S(1)} %copy-done.5, bf16[224,256]{1,0:T(8,128)(2,1)S(1)} %collective-permute-done.refs_2_, ...), custom_call_target="tpu_custom_call" | custom-call | tf_op jit(solution)/shard_map/pallas_call | solution.py:449
  26.9 1.6 %collective-permute-start.10 = (bf16[272,256]{1,0:T(8,128)(2,1)S(1)}, bf16[272,256]{1,0:T(8,128)(2,1)S(1)}, u32[]{:S(2)}, u32[]{:S(2)}) collective-permute-start(bf16[272,256]{1,0:T(8,128)(2,1)S(1)} %get-tuple-element.14), channel_id=1, source_target_pairs={{0,8},{8,0},{16,24},{24,16},{1,9},{9,1},{17,25},{25,17},{2,10},{10... | collective-permute-start | bytes 417800 | tf_op jit(solution)/shard_map/ppermute | solution.py:437
  28.5 1.5 %collective-permute-start.11 = (bf16[272,256]{1,0:T(8,128)(2,1)S(1)}, bf16[272,256]{1,0:T(8,128)(2,1)S(1)}, u32[]{:S(2)}, u32[]{:S(2)}) collective-permute-start(bf16[272,256]{1,0:T(8,128)(2,1)S(1)} %get-tuple-element.14), channel_id=1, source_target_pairs={{0,16},{8,24},{16,0},{24,8},{1,17},{9,25},{17,1},{25,9},{2,18},{10... | collective-permute-start | bytes 417800 | tf_op jit(solution)/shard_map/ppermute | solution.py:437
  30.0 0.5 collective-permute-start.12
  30.5 0.7 %reshape.13.class_w = bf16[1,256]{1,0:T(2,128)(2,1)S(1)} reshape(bf16[256]{0:T(256)(128)(2,1)} %param.18) | data formatting | bytes 1024 | tf_op jit(solution)/shard_map/reshape | solution.py:497
  31.1 1.5 %collective-permute-start.7 = (bf16[16,1024]{1,0:T(8,128)(2,1)S(1)}, bf16[16,1024]{1,0:T(8,128)(2,1)S(1)}, u32[]{:S(2)}, u32[]{:S(2)}) collective-permute-start(bf16[16,1024]{1,0:T(8,128)(2,1)S(1)} %get-tuple-element.11), channel_id=1, source_target_pairs={{0,8},{8,0},{16,24},{24,16},{1,9},{9,1},{17,25},{25,17},{2,10},{10... | collective-permute-start | bytes 98312 | tf_op jit(solution)/shard_map/ppermute | solution.py:437
  32.7 1.5 %collective-permute-start.8 = (bf16[16,1024]{1,0:T(8,128)(2,1)S(1)}, bf16[16,1024]{1,0:T(8,128)(2,1)S(1)}, u32[]{:S(2)}, u32[]{:S(2)}) collective-permute-start(bf16[16,1024]{1,0:T(8,128)(2,1)S(1)} %get-tuple-element.12), channel_id=1, source_target_pairs={{0,16},{8,24},{16,0},{24,8},{1,17},{9,25},{17,1},{25,9},{2,18},{10... | collective-permute-start | bytes 98312 | tf_op jit(solution)/shard_map/ppermute | solution.py:437
  34.2 1.8 %collective-permute-start.9 = (bf16[16,1024]{1,0:T(8,128)(2,1)S(1)}, bf16[16,1024]{1,0:T(8,128)(2,1)S(1)}, u32[]{:S(2)}, u32[]{:S(2)}) collective-permute-start(bf16[16,1024]{1,0:T(8,128)(2,1)S(1)} %get-tuple-element.13), channel_id=1, source_target_pairs={{0,24},{8,16},{16,8},{24,0},{1,25},{9,17},{17,9},{25,1},{2,26},{10... | collective-permute-start | bytes 98312 | tf_op jit(solution)/shard_map/ppermute | solution.py:437
  36.0 1.4 %collective-permute-done.11 = bf16[272,256]{1,0:T(8,128)(2,1)S(1)} collective-permute-done((bf16[272,256]{1,0:T(8,128)(2,1)S(1)}, bf16[272,256]{1,0:T(8,128)(2,1)S(1)}, u32[]{:S(2)}, u32[]{:S(2)}) %collective-permute-start.11) | collective-permute-done | bytes 139296 | tf_op jit(solution)/shard_map/ppermute | solution.py:437
  37.4 0.3 collective-permute-done.12
  37.6 0.1 add_convert_fusion.ours
  37.7 0.1 collective-permute-start.13
  37.8 0.4 collective-permute-done.8
  38.2 0.8 %collective-permute-done.9 = bf16[16,1024]{1,0:T(8,128)(2,1)S(1)} collective-permute-done((bf16[16,1024]{1,0:T(8,128)(2,1)S(1)}, bf16[16,1024]{1,0:T(8,128)(2,1)S(1)}, u32[]{:S(2)}, u32[]{:S(2)}) %collective-permute-start.9) | collective-permute-done | bytes 32800 | tf_op jit(solution)/shard_map/ppermute | solution.py:437
  39.0 0.6 %fusion = bf16[2,1,8,1024]{3,2,1,0:T(8,128)(2,1)} fusion(bf16[16,1024]{1,0:T(8,128)(2,1)S(1)} %collective-permute-done.9, bf16[16,1024]{1,0:T(8,128)(2,1)S(1)} %collective-permute-done.8, bf16[16,1024]{1,0:T(8,128)(2,1)S(1)} %collective-permute-done.7, bf16[16,1024]{1,0:T(8,128)(2,1)S(1)} %get-tuple-element.10, bf16[2,1,8,1024]{3,2,1,0:T(8,128)(2,1)S(1)} %copy-done.8), kind=kLoop, calls=%fused_computation.2 | loop fusion | flops 163840 | bytes 196608 | tf_op jit(solution)/shard_map/convert_element_type | solution.py:473
  39.7 2.0 %copy-done.2 = bf16[3,3,3,256,256]{4,3,2,1,0:T(8,128)(2,1)S(1)} copy-done((bf16[3,3,3,256,256]{4,3,2,1,0:T(8,128)(2,1)S(1)}, bf16[3,3,3,256,256]{4,3,2,1,0:T(8,128)(2,1)}, u32[]{:S(2)}) %copy-start.2) | copy-done | bytes 3538968
  41.7 2.0 %copy-done.3 = bf16[3,3,3,256,256]{4,3,2,1,0:T(8,128)(2,1)S(1)} copy-done((bf16[3,3,3,256,256]{4,3,2,1,0:T(8,128)(2,1)S(1)}, bf16[3,3,3,256,256]{4,3,2,1,0:T(8,128)(2,1)}, u32[]{:S(2)}) %copy-start.3) | copy-done | bytes 3538968
  43.7 15.3 %shard_map.123 = (f32[1,128]{1,0:T(1,128)}, bf16[2,1,8,1024]{3,2,1,0:T(8,128)(2,1)}) custom-call(s32[5]{0:T(128)S(1)} %copy-done.7, bf16[272,256]{1,0:T(8,128)(2,1)S(1)} %add_convert_fusion.ours, bf16[272,256]{1,0:T(8,128)(2,1)S(1)} %collective-permute-done.13.theirs, bf16[3,3,3,256,256]{4,3,2,1,0:T(8,128)(2,1)S(1)} %copy-done.2, ...), custom_call_target="tpu_custom_call" | custom-call | tf_op jit(solution)/shard_map/pallas_call | solution.py:476
  (22 shorter events, 0.1 us)
Async XLA Ops:
  0.6 38.4 %copy-start.8 = (bf16[2,1,8,1024]{3,2,1,0:T(8,128)(2,1)S(1)}, bf16[2,1,8,1024]{3,2,1,0:T(8,128)(2,1)}, u32[]{:S(2)}) copy-start(bf16[2,1,8,1024]{3,2,1,0:T(8,128)(2,1)} %r_ref.1) | copy-start | bytes 98308
  0.6 39.0 %copy-start.1 = (bf16[1024,256]{1,0:T(8,128)(2,1)S(1)}, bf16[1024,256]{1,0:T(8,128)(2,1)}, u32[]{:S(2)}) copy-start(bf16[1024,256]{1,0:T(8,128)(2,1)} %neck_w.1) | copy-start | bytes 1572868
  2.8 36.9 %copy-start.7 = (s32[5]{0:T(128)S(1)}, s32[5]{0:T(128)}, u32[]{:S(2)}) copy-start(s32[5]{0:T(128)} %stack.23.place.refs_0_) | copy-start | bytes 64
  4.7 6.4 %collective-permute-start = (bf16[224,256]{1,0:T(8,128)(2,1)}, bf16[224,256]{1,0:T(8,128)(2,1)S(1)}, u32[]{:S(2)}, u32[]{:S(2)}) collective-permute-start(bf16[224,256]{1,0:T(8,128)(2,1)} %shard_map.121.refs_1_), channel_id=1, source_target_pairs={{0,2},{1,3},{2,0},{3,1},{4,6},{5,7},{6,4},{7,5},{8,10},{9,11},{10,... | collective-permute-start | bytes 344072 | tf_op jit(solution)/shard_map/ppermute | solution.py:434
  7.8 11.9 %collective-permute-start.1 = (bf16[224,256]{1,0:T(8,128)(2,1)}, bf16[224,256]{1,0:T(8,128)(2,1)S(1)}, u32[]{:S(2)}, u32[]{:S(2)}) collective-permute-start(bf16[224,256]{1,0:T(8,128)(2,1)} %shard_map.121.refs_1_), channel_id=1, source_target_pairs={{0,4},{1,5},{2,6},{3,7},{4,0},{5,1},{6,2},{7,3},{8,12},{9,13},{10,... | collective-permute-start | bytes 344072 | tf_op jit(solution)/shard_map/ppermute | solution.py:434
  10.3 9.3 %collective-permute-start.2 = (bf16[224,256]{1,0:T(8,128)(2,1)}, bf16[224,256]{1,0:T(8,128)(2,1)S(1)}, u32[]{:S(2)}, u32[]{:S(2)}) collective-permute-start(bf16[224,256]{1,0:T(8,128)(2,1)} %shard_map.121.refs_1_), channel_id=1, source_target_pairs={{0,6},{1,7},{2,4},{3,5},{4,2},{5,3},{6,0},{7,1},{8,14},{9,15},{10,... | collective-permute-start | bytes 344072 | tf_op jit(solution)/shard_map/ppermute | solution.py:434
  10.3 9.8 %collective-permute-start.3 = (bf16[224,256]{1,0:T(8,128)(2,1)}, bf16[224,256]{1,0:T(8,128)(2,1)S(1)}, u32[]{:S(2)}, u32[]{:S(2)}) collective-permute-start(bf16[224,256]{1,0:T(8,128)(2,1)} %shard_map.121.refs_1_), channel_id=1, source_target_pairs={{0,1},{1,0},{2,3},{3,2},{4,5},{5,4},{6,7},{7,6},{8,9},{9,8},{10,11... | collective-permute-start | bytes 344072 | tf_op jit(solution)/shard_map/ppermute | solution.py:434
  11.1 9.1 %collective-permute-start.4 = (bf16[224,256]{1,0:T(8,128)(2,1)S(1)}, bf16[224,256]{1,0:T(8,128)(2,1)S(1)}, u32[]{:S(2)}, u32[]{:S(2)}) collective-permute-start(bf16[224,256]{1,0:T(8,128)(2,1)S(1)} %collective-permute-done.refs_2_), channel_id=1, source_target_pairs={{0,1},{1,0},{2,3},{3,2},{4,5},{5,4},{6,7},{7,6},{8,9},{9,8},{10,11... | collective-permute-start | bytes 344072 | tf_op jit(solution)/shard_map/ppermute | solution.py:434
  19.7 1.3 %collective-permute-start.5 = (bf16[224,256]{1,0:T(8,128)(2,1)S(1)}, bf16[224,256]{1,0:T(8,128)(2,1)S(1)}, u32[]{:S(2)}, u32[]{:S(2)}) collective-permute-start(bf16[224,256]{1,0:T(8,128)(2,1)S(1)} %collective-permute-done.1.refs_3_), channel_id=1, source_target_pairs={{0,1},{1,0},{2,3},{3,2},{4,5},{5,4},{6,7},{7,6},{8,9},{9,8},{10,11... | collective-permute-start | bytes 344072 | tf_op jit(solution)/shard_map/ppermute | solution.py:434
  19.7 1.5 %collective-permute-start.6 = (bf16[224,256]{1,0:T(8,128)(2,1)S(1)}, bf16[224,256]{1,0:T(8,128)(2,1)S(1)}, u32[]{:S(2)}, u32[]{:S(2)}) collective-permute-start(bf16[224,256]{1,0:T(8,128)(2,1)S(1)} %collective-permute-done.2.refs_4_), channel_id=1, source_target_pairs={{0,1},{1,0},{2,3},{3,2},{4,5},{5,4},{6,7},{7,6},{8,9},{9,8},{10,11... | collective-permute-start | bytes 344072 | tf_op jit(solution)/shard_map/ppermute | solution.py:434
  21.1 1.0 %copy-start = (bf16[1024,256]{1,0:T(8,128)(2,1)S(1)}, bf16[1024,256]{1,0:T(8,128)(2,1)}, u32[]{:S(2)}) copy-start(bf16[1024,256]{1,0:T(8,128)(2,1)} %neck_w.1) | copy-start | bytes 1572868
  22.2 1.0 %copy-start.4 = (bf16[256,1024]{1,0:T(8,128)(2,1)S(1)}, bf16[256,1024]{1,0:T(8,128)(2,1)}, u32[]{:S(2)}) copy-start(bf16[256,1024]{1,0:T(8,128)(2,1)} %refs_9_.1) | copy-start | bytes 1572868
  23.2 0.9 %copy-start.5 = (bf16[224,256]{1,0:T(8,128)(2,1)S(1)}, bf16[224,256]{1,0:T(8,128)(2,1)}, u32[]{:S(2)}) copy-start(bf16[224,256]{1,0:T(8,128)(2,1)} %shard_map.121.refs_1_) | copy-start | bytes 344068
  24.1 0.7 %copy-start.6 = (s32[5]{0:T(128)S(1)}, s32[5]{0:T(128)}, u32[]{:S(2)}) copy-start(s32[5]{0:T(128)} %stack.23.place.refs_0_) | copy-start | bytes 64
  26.9 7.3 %collective-permute-start.10 = (bf16[272,256]{1,0:T(8,128)(2,1)S(1)}, bf16[272,256]{1,0:T(8,128)(2,1)S(1)}, u32[]{:S(2)}, u32[]{:S(2)}) collective-permute-start(bf16[272,256]{1,0:T(8,128)(2,1)S(1)} %get-tuple-element.14), channel_id=1, source_target_pairs={{0,8},{8,0},{16,24},{24,16},{1,9},{9,1},{17,25},{25,17},{2,10},{10... | collective-permute-start | bytes 417800 | tf_op jit(solution)/shard_map/ppermute | solution.py:437
  28.5 8.8 %collective-permute-start.11 = (bf16[272,256]{1,0:T(8,128)(2,1)S(1)}, bf16[272,256]{1,0:T(8,128)(2,1)S(1)}, u32[]{:S(2)}, u32[]{:S(2)}) collective-permute-start(bf16[272,256]{1,0:T(8,128)(2,1)S(1)} %get-tuple-element.14), channel_id=1, source_target_pairs={{0,16},{8,24},{16,0},{24,8},{1,17},{9,25},{17,1},{25,9},{2,18},{10... | collective-permute-start | bytes 417800 | tf_op jit(solution)/shard_map/ppermute | solution.py:437
  30.0 7.6 %collective-permute-start.12 = (bf16[272,256]{1,0:T(8,128)(2,1)S(1)}, bf16[272,256]{1,0:T(8,128)(2,1)S(1)}, u32[]{:S(2)}, u32[]{:S(2)}) collective-permute-start(bf16[272,256]{1,0:T(8,128)(2,1)S(1)} %get-tuple-element.14), channel_id=1, source_target_pairs={{0,24},{8,16},{16,8},{24,0},{1,25},{9,17},{17,9},{25,1},{2,26},{10... | collective-permute-start | bytes 417800 | tf_op jit(solution)/shard_map/ppermute | solution.py:437
  31.1 6.7 %collective-permute-start.7 = (bf16[16,1024]{1,0:T(8,128)(2,1)S(1)}, bf16[16,1024]{1,0:T(8,128)(2,1)S(1)}, u32[]{:S(2)}, u32[]{:S(2)}) collective-permute-start(bf16[16,1024]{1,0:T(8,128)(2,1)S(1)} %get-tuple-element.11), channel_id=1, source_target_pairs={{0,8},{8,0},{16,24},{24,16},{1,9},{9,1},{17,25},{25,17},{2,10},{10... | collective-permute-start | bytes 98312 | tf_op jit(solution)/shard_map/ppermute | solution.py:437
  32.7 5.5 %collective-permute-start.8 = (bf16[16,1024]{1,0:T(8,128)(2,1)S(1)}, bf16[16,1024]{1,0:T(8,128)(2,1)S(1)}, u32[]{:S(2)}, u32[]{:S(2)}) collective-permute-start(bf16[16,1024]{1,0:T(8,128)(2,1)S(1)} %get-tuple-element.12), channel_id=1, source_target_pairs={{0,16},{8,24},{16,0},{24,8},{1,17},{9,25},{17,1},{25,9},{2,18},{10... | collective-permute-start | bytes 98312 | tf_op jit(solution)/shard_map/ppermute | solution.py:437
  34.2 4.8 %collective-permute-start.9 = (bf16[16,1024]{1,0:T(8,128)(2,1)S(1)}, bf16[16,1024]{1,0:T(8,128)(2,1)S(1)}, u32[]{:S(2)}, u32[]{:S(2)}) collective-permute-start(bf16[16,1024]{1,0:T(8,128)(2,1)S(1)} %get-tuple-element.13), channel_id=1, source_target_pairs={{0,24},{8,16},{16,8},{24,0},{1,25},{9,17},{17,9},{25,1},{2,26},{10... | collective-permute-start | bytes 98312 | tf_op jit(solution)/shard_map/ppermute | solution.py:437
  37.7 1.9 %collective-permute-start.13 = (bf16[272,256]{1,0:T(8,128)(2,1)S(1)}, bf16[272,256]{1,0:T(8,128)(2,1)S(1)}, u32[]{:S(2)}, u32[]{:S(2)}) collective-permute-start(bf16[272,256]{1,0:T(8,128)(2,1)S(1)} %add_convert_fusion.ours), channel_id=1, source_target_pairs={{0,1},{1,0},{2,3},{3,2},{4,5},{5,4},{6,7},{7,6},{8,9},{9,8},{10,11... | collective-permute-start | bytes 417800 | tf_op jit(solution)/shard_map/ppermute | solution.py:434
  39.7 2.0 %copy-start.2 = (bf16[3,3,3,256,256]{4,3,2,1,0:T(8,128)(2,1)S(1)}, bf16[3,3,3,256,256]{4,3,2,1,0:T(8,128)(2,1)}, u32[]{:S(2)}) copy-start(bf16[3,3,3,256,256]{4,3,2,1,0:T(8,128)(2,1)} %first_w.1) | copy-start | bytes 10616836
  41.7 2.0 %copy-start.3 = (bf16[3,3,3,256,256]{4,3,2,1,0:T(8,128)(2,1)S(1)}, bf16[3,3,3,256,256]{4,3,2,1,0:T(8,128)(2,1)}, u32[]{:S(2)}) copy-start(bf16[3,3,3,256,256]{4,3,2,1,0:T(8,128)(2,1)} %second_w.1) | copy-start | bytes 10616836

commit v2 on v1

--- a/solution.py
+++ b/solution.py
@@ -10,6 +10,7 @@
 HD = 64
 F32 = jnp.float32
 BF16 = jnp.bfloat16
+LABEL_ROWS = 16
 
 
 OFFSETS = [
@@ -221,7 +222,13 @@
     return jnp.concatenate([zeros, value[:step]], axis=0)
 
 
-def pack_kernel(place, q_ref, k_ref, v_ref, r_ref, neck_ref, lab_ref, out_ref):
+def place_of(tok_n):
+    h, t = lax.axis_index("heads"), lax.axis_index("tok")
+    return h, t // 2, t % 2, t
+
+
+def pack_kernel(tok_n, q_ref, k_ref, v_ref, r_ref, neck_ref, lab_ref, out_ref):
+    h, _, _, t = place_of(tok_n)
     rows = q_ref.shape[1] * q_ref.shape[2]
     width = q_ref.shape[3]
     for i, ref in enumerate((q_ref, k_ref, v_ref)):
@@ -230,24 +237,51 @@
     own = r_ref.shape[0] * r_ref.shape[2]
     residual = r_ref[...].astype(F32).reshape(own, r_ref.shape[3]).astype(BF16)
     out_ref[3 * rows : 3 * rows + own, :] = dot(residual, neck_ref[...]).astype(BF16)
-    count = lab_ref.shape[0] * lab_ref.shape[1]
-    labels = lab_ref[...].astype(F32).reshape(count, 1)
+    own_c, _, nt = lab_ref.shape
+    spread = jnp.zeros((LABEL_ROWS, width), F32)
+    for c in range(own_c):
+        row = jnp.broadcast_to(lab_ref[c].astype(F32), (LABEL_ROWS, nt)).astype(BF16)
+        at = (h * own_c + c) * nt + iota((nt, width), 0)
+        spread = spread + dot(row, (iota((nt, width), 1) == at).astype(F32).astype(BF16))
     out_ref[3 * rows + own :, :] = jnp.where(
-        iota((count, width), 1) == place[3], labels, 0.0
+        iota((LABEL_ROWS, width), 0) == t, spread, 0.0
     ).astype(BF16)
 
 
-def attention_kernel(zs, rows, own, *refs):
-    place = refs[0]
-    ours, theirs = refs[1 : 1 + zs], refs[1 + zs : 1 + 2 * zs]
-    out_w, neck_w = refs[1 + 2 * zs : 3 + 2 * zs]
-    part_ref = refs[3 + 2 * zs]
-    enc_refs = refs[4 + 2 * zs : -4]
+def weights_kernel(first_ref, second_ref, out_ref, neck_ref, packed_ref, *refs):
+    first_in, second_in, first_t, second_t, joint, again, out_w, neck_w, sems = refs
+    small = [
+        pltpu.make_async_copy(out_ref, out_w, sems.at[6]),
+        pltpu.make_async_copy(neck_ref, neck_w, sems.at[7]),
+    ]
+    for copy in small:
+        copy.start()
+    copies = []
+    for i, (src, dst) in enumerate(((first_ref, first_in), (second_ref, second_in))):
+        for a in range(3):
+            copies.append(pltpu.make_async_copy(src.at[a], dst.at[a], sems.at[3 * i + a]))
+            copies[-1].start()
+    again[...] = packed_ref[...]
+    for copy in small:
+        copy.wait()
+    joint[...] = dot(out_w[...], neck_w[...]).astype(BF16)
+    for i, (src, dst) in enumerate(((first_in, first_t), (second_in, second_t))):
+        for a in range(3):
+            copies[3 * i + a].wait()
+            for b in range(3):
+                for e in range(3):
+                    dst[a, b, e] = src[a, b, e].T
+
+
+def attention_kernel(tok_n, zs, rows, own, *refs):
+    ours, theirs = refs[:zs], refs[zs : 2 * zs]
+    out_w, joint_w = refs[2 * zs : 2 + 2 * zs]
+    part_refs = refs[2 + 2 * zs : -4]
     qq, kk, vv, part = refs[-4:]
-    z, core, h = place[0], place[1], place[2]
+    h, z, core, _ = place_of(tok_n)
     width = qq.shape[1]
-    queries_n, keys_n = qq.shape[0], kk.shape[0]
-    labels = jnp.zeros((ours[0].shape[0] - 3 * rows - own, width), F32)
+    queries_n = qq.shape[0]
+    labels = jnp.zeros((LABEL_ROWS, width), F32)
     for d in range(zs):
         qq[d * rows : (d + 1) * rows, :] = ours[d][0:rows, :]
         for ref, side in ((ours[d], core), (theirs[d], 1 - core)):
@@ -268,37 +302,37 @@
         total = jnp.sum(raw, axis=1, keepdims=True)
         mixed = dot(raw.astype(BF16), values)
         attended = jnp.where(mine, mixed / total, attended)
-    product = dot(attended.astype(BF16), out_w[...])
-    part[...] = dot(product.astype(BF16), neck_w[...])
+    attended = attended.astype(BF16)
+    part[...] = dot(attended, joint_w[...])
     for d in range(zs):
         at = pl.multiple_of(d * rows + h * own, own)
         part[pl.ds(at, own), :] += ours[d][3 * rows : 3 * rows + own, :].astype(F32)
-    part_ref[0:queries_n, :] = part[...].astype(BF16)
-    part_ref[queries_n:, :] = labels.astype(BF16)
-    first = product[0:rows, :]
+    partial = part[...].astype(BF16)
+    labels = labels.astype(BF16)
+    first = dot(attended[0:rows, :], out_w[...])
     blocks = [first[i * own : (i + 1) * own, :] for i in range(rows // own)]
-    for d, ref in enumerate(enc_refs):
+    for d, ref in enumerate(part_refs):
+        ref[0:queries_n, :] = partial
+        ref[queries_n : queries_n + LABEL_ROWS, :] = labels
         picked = blocks[0]
         for i in range(1, len(blocks)):
             picked = jnp.where((h ^ d) == i, blocks[i], picked)
-        ref[...] = picked.astype(BF16)
-
-
-def decoder_kernel(sizes, place, ours, theirs, first_w, second_w, class_w, neck_w, loss_ref, grad_ref, *scratch):
-    nc, nt, ni, own_c, zs = sizes
-    grid, cols, slope1, grad2, cols3, w1, w2, sems = scratch
+        for i in range(picked.shape[1] // width):
+            at = queries_n + LABEL_ROWS + i * own
+            ref[at : at + own, :] = picked[:, i * width : (i + 1) * width].astype(BF16)
+
+
+def decoder_kernel(sizes, *refs):
+    nc, nt, ni, own_c, zs, tok_n, parts_n = sizes
+    ours, theirs, r_ref, w1, w2, w1_t, w2_t, class_w, neck_w = refs[:9]
+    parts = refs[9 : 9 + parts_n]
+    encoded_ref, loss_ref, grad_ref, grid, cols, slope1, grad2, cols3 = refs[9 + parts_n :]
     channels = grid.shape[2]
     slab = nt * ni
     rows = nc * ni
     cells = nc * slab
-    z, core, h, tslab = place[0], place[1], place[2], place[4]
+    h, z, core, tslab = place_of(tok_n)
     taps = 9
-    copies = []
-    for i, (src, dst) in enumerate(((first_w, w1), (second_w, w2))):
-        for a in range(3):
-            copies.append(pltpu.make_async_copy(src.at[a], dst.at[a], sems.at[3 * i + a]))
-            copies[-1].start()
-
     for d in range(zs):
         for ref, side in ((ours, core), (theirs, 1 - core)):
             block = ref[d * rows : (d + 1) * rows, :].astype(F32)
@@ -321,11 +355,9 @@
                     moved, (b - 1) * ni
                 ).astype(BF16)
 
-    def conv(weights, base):
+    def conv(weights):
         total = None
         for a in range(3):
-            if base is not None:
-                copies[base + a].wait()
             matrix = weights[a].reshape(taps * channels, channels)
             term = dot(cols[a * slab : a * slab + cells, :], matrix)
             total = term if total is None else total + term
@@ -333,23 +365,21 @@
 
     for c in range(nc):
         spread(grid[c], c)
-    hidden_one = conv(w1, 0)
+    hidden_one = conv(w1)
     for c in range(nc):
         v = hidden_one[c * slab : (c + 1) * slab, :]
         s = sigma_of(v)
         slope1[c + 1, ni : ni + slab, :] = s * (1.0 + v * (1.0 - s))
         spread((v * s).astype(BF16).astype(F32), c)
-    hidden_two = conv(w2, 3)
+    hidden_two = conv(w2)
     sigma_two = sigma_of(hidden_two)
     active_two = (hidden_two * sigma_two).astype(BF16)
-    class_row = class_w[...].astype(F32)
+    class_row = class_w[...].astype(F32).reshape(1, channels)
     logits = dot_t(active_two, jnp.broadcast_to(class_row, (128, channels)).astype(BF16))
     probability = sigma_of(logits)
-    lab_rows = ours.shape[0] - rows * zs
-    lab = ours[rows * zs :, 0:128].astype(F32).reshape(own_c, nt, 1, 128)
-    spread_lab = jnp.broadcast_to(lab[None], (nc // own_c, own_c, nt, ni, 128)).reshape(cells, 128)
-    row = iota((cells, 128), 0)
-    wanted = (row // (slab * own_c)) * nt + row % ni
+    lab = ours[rows * zs : rows * zs + ni, 0:128].astype(F32)
+    spread_lab = jnp.broadcast_to(lab[None], (cells // ni, ni, 128)).reshape(cells, 128)
+    wanted = iota((cells, 128), 0) // ni
     picked = jnp.where(iota((cells, 128), 1) == wanted, spread_lab, 0.0).astype(BF16)
     mask = dot(picked, jnp.ones((128, 128), BF16))
     intersection = jnp.sum(probability * mask, axis=0, keepdims=True)
@@ -391,7 +421,7 @@
             for e in range(3):
                 lane = (b * 3 + e) * channels
                 piece = cols3[(2 - a) * band : (2 - a) * band + out3, lane : lane + channels]
-                total = total + dot_t(piece, w2[a, b, e])
+                total = total + dot(piece, w2_t[a, b, e])
     slopes = [slope1[c0 + i, pl.ds(t0, band), :] for i in range(own_c + 2)]
     g1 = (total * jnp.concatenate(slopes, axis=0)).astype(BF16).astype(F32)
     shifted = [along_inline(g1, 1 - e, ni) for e in range(3)]
@@ -404,17 +434,32 @@
                     for i in range(own_c)
                 ]
                 piece = jnp.concatenate(cells_in, axis=0).astype(BF16)
-                total = total + dot_t(piece, w1[a, b, e])
+                total = total + dot(piece, w1_t[a, b, e])
     grad = dot_t(total.astype(BF16), neck_w[...])
     grad_ref[...] = grad.reshape(grad_ref.shape).astype(BF16)
 
+    own = own_c * ni
+    width = parts[0].shape[1]
+    base = rows * zs + LABEL_ROWS
+    for i in range(r_ref.shape[3] // width):
+        terms = [ref[base + i * own : base + (i + 1) * own, :].astype(F32) for ref in parts]
+        total = pairwise(terms).reshape(own_c, 1, ni, width)
+        lanes = slice(i * width, (i + 1) * width)
+        encoded_ref[:, :, :, lanes] = (r_ref[:, :, :, lanes].astype(F32) + total).astype(BF16)
+
+
+def pairwise(values):
+    while len(values) > 1:
+        values = [values[i] + values[i + 1] for i in range(0, len(values), 2)]
+    return values[0]
+
 
 def vmem():
     return pl.BlockSpec(memory_space=pltpu.VMEM)
 
 
-def smem():
-    return pl.BlockSpec(memory_space=pltpu.SMEM)
+def hbm():
+    return pl.BlockSpec(memory_space=pltpu.HBM)
 
 
 def whole_grid(
@@ -426,9 +471,7 @@
     own_c = residual.shape[0]
     nt = labels.shape[1]
     channels = w_neck.shape[1]
-    rows, own, lab = nc * ni, own_c * ni, own_c * nt
-    h, t = lax.axis_index("heads"), lax.axis_index("tok")
-    place = jnp.stack([t // 2, t % 2, h, h * tok_n + t, t]).astype(jnp.int32)
+    rows, own = nc * ni, own_c * ni
 
     def swap_tok(value, bits):
         return lax.ppermute(value, "tok", [(i, i ^ bits) for i in range(tok_n)])
@@ -437,65 +480,70 @@
         return lax.ppermute(value, "heads", [(i, i ^ bits) for i in range(heads_n)])
 
     packed = pl.pallas_call(
-        pack_kernel,
-        out_shape=jax.ShapeDtypeStruct((3 * rows + own + lab, width), BF16),
-        in_specs=[smem()] + [vmem()] * 6,
+        functools.partial(pack_kernel, tok_n),
+        out_shape=pltpu.VMEM((3 * rows + own + LABEL_ROWS, width), BF16),
+        in_specs=[vmem()] * 6,
         out_specs=vmem(),
-    )(place, queries, key_rows, value_rows, residual, w_neck, labels)
+    )(queries, key_rows, value_rows, residual, w_neck, labels.transpose(0, 2, 1))
     ours = [packed] + [swap_tok(packed, 2 * d) for d in range(1, zs)]
-    theirs = [swap_tok(value, 1) for value in ours]
-    enc_shape = jax.ShapeDtypeStruct((own, residual.shape[3]), BF16)
+    kept = [pltpu.with_memory_space_constraint(w, pltpu.HBM) for w in (w_first, w_second, w_out, w_neck)]
+    first_in, second_in, first_t, second_t, joint, again, out_w, neck_w = pl.pallas_call(
+        weights_kernel,
+        out_shape=[pltpu.VMEM(w_first.shape, BF16)] * 4
+        + [
+            pltpu.VMEM((width, channels), BF16),
+            pltpu.VMEM(packed.shape, BF16),
+            pltpu.VMEM(w_out.shape, BF16),
+            pltpu.VMEM(w_neck.shape, BF16),
+        ],
+        in_specs=[hbm()] * 4 + [vmem()],
+        out_specs=[vmem()] * 8,
+        scratch_shapes=[pltpu.SemaphoreType.DMA((8,))],
+        compiler_params=pltpu.CompilerParams(vmem_limit_bytes=24 * 2**20),
+        cost_estimate=pl.CostEstimate(flops=0, bytes_accessed=28 * 2**20, transcendentals=0),
+    )(*kept, packed)
+    theirs = [swap_tok(value, 1) for value in [again] + ours[1:]]
     queries_n, keys_n = rows * zs, rows * tok_n
-    out = pl.pallas_call(
-        functools.partial(attention_kernel, zs, rows, own),
-        out_shape=[jax.ShapeDtypeStruct((queries_n + lab, channels), BF16)] + [enc_shape] * heads_n,
-        in_specs=[smem()] + [vmem()] * (2 * zs + 2),
-        out_specs=[vmem()] * (1 + heads_n),
+    enc_rows = own * residual.shape[3] // width
+    part_shape = pltpu.VMEM((queries_n + LABEL_ROWS + enc_rows, channels), BF16)
+    sent = pl.pallas_call(
+        functools.partial(attention_kernel, tok_n, zs, rows, own),
+        out_shape=[part_shape] * heads_n,
+        in_specs=[vmem()] * (2 * zs + 2),
+        out_specs=[vmem()] * heads_n,
         scratch_shapes=[
             pltpu.VMEM((queries_n, width), BF16),
             pltpu.VMEM((keys_n, width), BF16),
             pltpu.VMEM((keys_n, width), BF16),
             pltpu.VMEM((queries_n, channels), F32),
         ],
-        compiler_params=pltpu.CompilerParams(vmem_limit_bytes=32 * 2**20),
-    )(place, *ours, *theirs, w_out, w_neck)
-    parts = [out[0]] + [swap_heads(out[0], d) for d in range(1, heads_n)]
-    pieces = [out[1]] + [swap_heads(out[1 + d], d) for d in range(1, heads_n)]
-
-    def pairwise(values):
-        values = [v.astype(F32) for v in values]
-        while len(values) > 1:
-            values = [values[i] + values[i + 1] for i in range(0, len(values), 2)]
-        return values[0]
-
-    half = pairwise(parts).astype(BF16)
+        compiler_params=pltpu.CompilerParams(vmem_limit_bytes=16 * 2**20),
+    )(*ours, *theirs, out_w, joint)
+    parts = [sent[0]] + [swap_heads(sent[d], d) for d in range(1, heads_n)]
+    used = queries_n + LABEL_ROWS
+    half = pairwise([part[:used].astype(F32) for part in parts]).astype(BF16)
     other = swap_tok(half, 1)
-    encoded = (residual.astype(F32) + pairwise(pieces).reshape(residual.shape)).astype(BF16)
-
     slab = nt * ni
-    loss, grad = pl.pallas_call(
-        functools.partial(decoder_kernel, (nc, nt, ni, own_c, zs)),
-        out_shape=[
-            jax.ShapeDtypeStruct((1, 128), F32),
-            jax.ShapeDtypeStruct(residual.shape, BF16),
-        ],
-        in_specs=[smem(), vmem(), vmem()]
-        + [pl.BlockSpec(memory_space=pl.ANY)] * 2
-        + [vmem(), vmem()],
-        out_specs=[vmem(), vmem()],
-        scratch_shapes=[
-            pltpu.VMEM((nc, slab, channels), F32),
-            pltpu.VMEM(((nc + 2) * slab, 9 * channels), BF16),
-            pltpu.VMEM((nc + 2, (nt + 4) * ni, channels), F32),
-            pltpu.VMEM((nc + 4, (nt + 6) * ni, channels), F32),
-            pltpu.VMEM(((own_c + 4) * 4 * ni, 9 * channels), BF16),
-            pltpu.VMEM(w_first.shape, BF16),
-            pltpu.VMEM(w_second.shape, BF16),
-            pltpu.SemaphoreType.DMA((6,)),
-        ],
-        compiler_params=pltpu.CompilerParams(vmem_limit_bytes=40 * 2**20),
-    )(place, half, other, w_first, w_second, w_class.reshape(1, channels), w_neck)
-    return (encoded, loss[0, 0], grad)
+    return tuple(
+        pl.pallas_call(
+            functools.partial(decoder_kernel, (nc, nt, ni, own_c, zs, tok_n, heads_n)),
+            out_shape=[
+                jax.ShapeDtypeStruct(residual.shape, BF16),
+                jax.ShapeDtypeStruct((1, 128), F32),
+                jax.ShapeDtypeStruct(residual.shape, BF16),
+            ],
+            in_specs=[vmem()] * (9 + heads_n),
+            out_specs=[vmem()] * 3,
+            scratch_shapes=[
+                pltpu.VMEM((nc, slab, channels), F32),
+                pltpu.VMEM(((nc + 2) * slab, 9 * channels), BF16),
+                pltpu.VMEM((nc + 2, (nt + 4) * ni, channels), F32),
+                pltpu.VMEM((nc + 4, (nt + 6) * ni, channels), F32),
+                pltpu.VMEM(((own_c + 4) * 4 * ni, 9 * channels), BF16),
+            ],
+            compiler_params=pltpu.CompilerParams(vmem_limit_bytes=36 * 2**20),
+        )(half, other, residual, first_in, second_in, first_t, second_t, w_class, neck_w, *parts)
+    )
 
 
 def power_of_two(n):
@@ -508,25 +556,26 @@
     nt = labels.shape[1]
     return (
         slabs == 1
+        and nc * nt <= 128
         and labels.shape[2] == 1
         and ni == 8
         and nt == tok_n
         and tok_n >= 4
         and power_of_two(tok_n)
         and power_of_two(heads_n)
-        and heads_n * tok_n <= 128
+        and residual.shape[0] * heads_n == nc
         and nc * nt * ni <= 1024
         and width % 128 == 0
         and w_neck.shape[1] == width
         and (residual.shape[0] * ni) % 16 == 0
-        and (residual.shape[0] * nt) % 16 == 0
     )
 
 
 def on_device(*arguments):
     queries, residual, w_neck, labels = (arguments[i] for i in (0, 3, 5, 9))
     if fits_whole(queries, residual, w_neck, labels):
-        return whole_grid(*arguments)
+        encoded, loss, grad = whole_grid(*arguments)
+        return (encoded, loss[0, 0], grad)
     return on_tiles(*arguments)
 
 

time: 59.4 us -> 43.6 us (0.73)
  local copies, waits for them, and re-layouts: 10.4 us -> 0.01 us
  starting transfers between devices: 14.6 us -> 10.5 us
  Pallas kernels: 19.4 us -> 17.2 us
  waiting for transfers between devices: 13.1 us -> 15 us
  other arithmetic: 0.72 us -> 0.08 us
    unnamed x19 -> x4, local copies, waits for them, and re-layouts: 9.09 us -> 0.01 us
    ppermute x6 -> x3, waiting for transfers between devices: 2.87 us -> 8.04 us  [swap_heads(): return lax.ppermute(value, 'heads', [(i, i ^ bits) for i in range(heads_n)])]
    ppermute x6 -> x3, starting transfers between devices: 8.37 us -> 3.55 us  [swap_heads(): return lax.ppermute(value, 'heads', [(i, i ^ bits) for i in range(heads_n)])]
    ppermute x8, waiting for transfers between devices: 10.3 us -> 6.94 us  [swap_tok(): return lax.ppermute(value, 'tok', [(i, i ^ bits) for i in range(tok_n)])]
    pallas_call x3 -> x4, Pallas kernels: 19.4 us -> 17.2 us  [the longest x1 10.8 us: whole_grid(): pl.pallas_call(functools.partial(decoder_kernel, (nc, nt, ni, own_c, zs,...]
    ppermute x8, starting transfers between devices: 6.2 us -> 6.9 us  [swap_tok(): return lax.ppermute(value, 'tok', [(i, i ^ bits) for i in range(tok_n)])]
    another operation x1 -> x0, local copies, waits for them, and re-layouts: 0.68 us -> none  [whole_grid(): place = jnp.stack([t // 2, t % 2, h, h * tok_n + t, t]).astype(jnp.int32)]
    reshape x1 -> x0, local copies, waits for them, and re-layouts: 0.66 us -> none  [whole_grid(): w_class.reshape(1, channels)]
  transfers between devices with their start and end apart: 14 -> 11, of which waited for: 8 -> 6; matrix products, arithmetic and copies ran while one was open for 2% -> 0% of each run, Pallas kernels for 0% -> 9%
where the time goes in v2:
time: 43.6 us; the launch traced here: 43.4 us
  Pallas kernels  17.2 us (39%)
  waiting for transfers between devices  15 us (34%)
  starting transfers between devices  10.5 us (24%)
  between operations  0.71 us (2%)
    pallas_call x1, Pallas kernels, whole_grid(): pl.pallas_call(functools.partial(decoder_kernel, (nc, nt, ni, own_c, zs,...  10.8 us
    ppermute x3, waiting for transfers between devices, swap_heads(): return lax.ppermute(value, 'heads', [(i, i ^ bits) for i in range(heads_n)])  8.04 us
    ppermute x8, waiting for transfers between devices, swap_tok(): return lax.ppermute(value, 'tok', [(i, i ^ bits) for i in range(tok_n)])  6.94 us
    ppermute x8, starting transfers between devices, swap_tok(): return lax.ppermute(value, 'tok', [(i, i ^ bits) for i in range(tok_n)])  6.9 us
    pallas_call x1, Pallas kernels, whole_grid(): pl.pallas_call(weights_kernel, out_shape=[pltpu.VMEM(w_first.shape, BF16)...  3.82 us
    ppermute x3, starting transfers between devices, swap_heads(): return lax.ppermute(value, 'heads', [(i, i ^ bits) for i in range(heads_n)])  3.55 us
    pallas_call x1, Pallas kernels, whole_grid(): pl.pallas_call(functools.partial(pack_kernel, tok_n), out_shape=pltpu.VME...  1.32 us
    pallas_call x1, Pallas kernels, whole_grid(): pl.pallas_call(functools.partial(attention_kernel, tok_n, zs, rows, own),...  1.31 us
  transfers between devices with their start and end apart: 11, of which 6 were waited for; matrix products, arithmetic and copies ran while one was open for 0% of the time, Pallas kernels for 9%

profile of v2, /device:TPU:0, one launch (start us, length us, event | category | flops | bytes accessed | tf_op | source)
XLA Modules:
  0.0 43.4 jit_solution(5331167283241281516)
XLA Ops:
  0.6 1.3 %shard_map.121.packed_ref.refs_0_ = bf16[224,256]{1,0:T(8,128)(2,1)S(1)} custom-call(bf16[1,8,8,256]{3,2,1,0:T(8,128)(2,1)} %q_ref.1, bf16[1,8,8,256]{3,2,1,0:T(8,128)(2,1)} %k_ref.1, bf16[1,8,8,256]{3,2,1,0:T(8,128)(2,1)} %v_ref.1, bf16[2,1,8,1024]{3,2,1,0:T(8,128)(2,1)} %refs_2_.1, bf16[1024,256]{1,0:T(8,128)(2,1)} %neck_ref.3, s32[2,1,8]{2,1,0:T(1,128)} %bitcast.5), custom_call_target="tpu_custom_call" | custom-call | tf_op jit(solution)/shard_map/pallas_call | solution.py:482
  2.0 0.0 copy-start
  2.0 0.0 copy-start.1
  2.0 5.1 %collective-permute-start.2 = (bf16[224,256]{1,0:T(8,128)(2,1)S(1)}, bf16[224,256]{1,0:T(8,128)(2,1)S(1)}, u32[]{:S(2)}, u32[]{:S(2)}) collective-permute-start(bf16[224,256]{1,0:T(8,128)(2,1)S(1)} %shard_map.121.packed_ref.refs_0_), channel_id=1, source_target_pairs={{0,6},{1,7},{2,4},{3,5},{4,2},{5,3},{6,0},{7,1},{8,14},{9,15},{10,... | collective-permute-start | bytes 344072 | tf_op jit(solution)/shard_map/ppermute | solution.py:477
  7.1 0.0 collective-permute-start.1
  7.1 0.6 %collective-permute-start = (bf16[224,256]{1,0:T(8,128)(2,1)S(1)}, bf16[224,256]{1,0:T(8,128)(2,1)S(1)}, u32[]{:S(2)}, u32[]{:S(2)}) collective-permute-start(bf16[224,256]{1,0:T(8,128)(2,1)S(1)} %shard_map.121.packed_ref.refs_0_), channel_id=1, source_target_pairs={{0,2},{1,3},{2,0},{3,1},{4,6},{5,7},{6,4},{7,5},{8,10},{9,11},{10,... | collective-permute-start | bytes 344072 | tf_op jit(solution)/shard_map/ppermute | solution.py:477
  7.7 3.8 %shard_map.122 = (bf16[3,3,3,256,256]{4,3,2,1,0:T(8,128)(2,1)S(1)}, bf16[3,3,3,256,256]{4,3,2,1,0:T(8,128)(2,1)S(1)}, bf16[3,3,3,256,256]{4,3,2,1,0:T(8,128)(2,1...) custom-call(bf16[3,3,3,256,256]{4,3,2,1,0:T(8,128)(2,1)} %first_ref., ...), custom_call_target="tpu_custom_call" | custom-call | bytes 29360128 | tf_op jit(solution)/shard_map/pallas_call | solution.py:490
  11.6 0.1 collective-permute-start.3
  11.6 0.0 collective-permute-done.2.refs_3_
  11.7 0.5 %collective-permute-start.6 = (bf16[224,256]{1,0:T(8,128)(2,1)S(1)}, bf16[224,256]{1,0:T(8,128)(2,1)S(1)}, u32[]{:S(2)}, u32[]{:S(2)}) collective-permute-start(bf16[224,256]{1,0:T(8,128)(2,1)S(1)} %collective-permute-done.2.refs_3_), channel_id=1, source_target_pairs={{0,1},{1,0},{2,3},{3,2},{4,5},{5,4},{6,7},{7,6},{8,9},{9,8},{10,11... | collective-permute-start | bytes 344072 | tf_op jit(solution)/shard_map/ppermute | solution.py:477
  12.2 4.6 %collective-permute-done.1.refs_2_ = bf16[224,256]{1,0:T(8,128)(2,1)S(1)} collective-permute-done((bf16[224,256]{1,0:T(8,128)(2,1)S(1)}, bf16[224,256]{1,0:T(8,128)(2,1)S(1)}, u32[]{:S(2)}, u32[]{:S(2)}) %collective-permute-start.1) | collective-permute-done | bytes 114720 | tf_op jit(solution)/shard_map/ppermute | solution.py:477
  16.8 0.0 collective-permute-start.5
  16.8 0.0 collective-permute-done.refs_1_
  16.8 0.5 %collective-permute-start.4 = (bf16[224,256]{1,0:T(8,128)(2,1)S(1)}, bf16[224,256]{1,0:T(8,128)(2,1)S(1)}, u32[]{:S(2)}, u32[]{:S(2)}) collective-permute-start(bf16[224,256]{1,0:T(8,128)(2,1)S(1)} %collective-permute-done.refs_1_), channel_id=1, source_target_pairs={{0,1},{1,0},{2,3},{3,2},{4,5},{5,4},{6,7},{7,6},{8,9},{9,8},{10,11... | collective-permute-start | bytes 344072 | tf_op jit(solution)/shard_map/ppermute | solution.py:477
  17.3 0.0 collective-permute-done.3.refs_4_
  17.3 0.0 collective-permute-done.6.refs_7_
  17.3 0.8 %collective-permute-done.5.refs_6_ = bf16[224,256]{1,0:T(8,128)(2,1)S(1)} collective-permute-done((bf16[224,256]{1,0:T(8,128)(2,1)S(1)}, bf16[224,256]{1,0:T(8,128)(2,1)S(1)}, u32[]{:S(2)}, u32[]{:S(2)}) %collective-permute-start.5) | collective-permute-done | bytes 114720 | tf_op jit(solution)/shard_map/ppermute | solution.py:477
  18.1 0.2 collective-permute-done.4.refs_5_
  18.3 1.3 %shard_map.123 = (bf16[336,256]{1,0:T(8,128)(2,1)S(1)}, bf16[336,256]{1,0:T(8,128)(2,1)S(1)}, bf16[336,256]{1,0:T(8,128)(2,1)S(1)}, bf16[336,256]{1,0:T(8,128)(2,1)S(1)}) custom-call(bf16[224,256]{1,0:T(8,128)(2,1)S(1)} %shard_map.121.packed_ref.refs_0_, bf16[224,256]{1,0:T(8,128)(2,1)S(1)} %collective-permute-done.refs_1_, ...), custom_call_target="tpu_custom_call" | custom-call | tf_op jit(solution)/shard_map/pallas_call | solution.py:509
  19.6 1.6 %collective-permute-start.7 = (bf16[336,256]{1,0:T(8,128)(2,1)S(1)}, bf16[336,256]{1,0:T(8,128)(2,1)S(1)}, u32[]{:S(2)}, u32[]{:S(2)}) collective-permute-start(bf16[336,256]{1,0:T(8,128)(2,1)S(1)} %get-tuple-element.22), channel_id=1, source_target_pairs={{0,8},{8,0},{16,24},{24,16},{1,9},{9,1},{17,25},{25,17},{2,10},{10... | collective-permute-start | bytes 516104 | tf_op jit(solution)/shard_map/ppermute | solution.py:480
  21.1 1.5 %collective-permute-start.8 = (bf16[336,256]{1,0:T(8,128)(2,1)S(1)}, bf16[336,256]{1,0:T(8,128)(2,1)S(1)}, u32[]{:S(2)}, u32[]{:S(2)}) collective-permute-start(bf16[336,256]{1,0:T(8,128)(2,1)S(1)} %get-tuple-element.23), channel_id=1, source_target_pairs={{0,16},{8,24},{16,0},{24,8},{1,17},{9,25},{17,1},{25,9},{2,18},{10... | collective-permute-start | bytes 516104 | tf_op jit(solution)/shard_map/ppermute | solution.py:480
  22.6 0.5 %collective-permute-start.9 = (bf16[336,256]{1,0:T(8,128)(2,1)S(1)}, bf16[336,256]{1,0:T(8,128)(2,1)S(1)}, u32[]{:S(2)}, u32[]{:S(2)}) collective-permute-start(bf16[336,256]{1,0:T(8,128)(2,1)S(1)} %get-tuple-element.24), channel_id=1, source_target_pairs={{0,24},{8,16},{16,8},{24,0},{1,25},{9,17},{17,9},{25,1},{2,26},{10... | collective-permute-start | bytes 516104 | tf_op jit(solution)/shard_map/ppermute | solution.py:480
  23.1 3.7 %collective-permute-done.7.refs_10_ = bf16[336,256]{1,0:T(8,128)(2,1)S(1)} collective-permute-done((bf16[336,256]{1,0:T(8,128)(2,1)S(1)}, bf16[336,256]{1,0:T(8,128)(2,1)S(1)}, u32[]{:S(2)}, u32[]{:S(2)}) %collective-permute-start.7) | collective-permute-done | bytes 172064 | tf_op jit(solution)/shard_map/ppermute | solution.py:480
  26.8 4.3 %collective-permute-done.8.refs_11_ = bf16[336,256]{1,0:T(8,128)(2,1)S(1)} collective-permute-done((bf16[336,256]{1,0:T(8,128)(2,1)S(1)}, bf16[336,256]{1,0:T(8,128)(2,1)S(1)}, u32[]{:S(2)}, u32[]{:S(2)}) %collective-permute-start.8) | collective-permute-done | bytes 172064 | tf_op jit(solution)/shard_map/ppermute | solution.py:480
  31.2 0.0 collective-permute-done.9.refs_12_
  31.2 0.1 add_convert_fusion.refs_0_
  31.2 0.1 collective-permute-start.10
  31.3 1.3 %collective-permute-done.10.refs_1_ = bf16[272,256]{1,0:T(8,128)(2,1)S(1)} collective-permute-done((bf16[272,256]{1,0:T(8,128)(2,1)S(1)}, bf16[272,256]{1,0:T(8,128)(2,1)S(1)}, u32[]{:S(2)}, u32[]{:S(2)}) %collective-permute-start.10) | collective-permute-done | bytes 139296 | tf_op jit(solution)/shard_map/ppermute | solution.py:477
  32.7 0.0 copy-done
  32.7 0.0 copy-done.1
  32.7 10.8 %shard_map.124 = (bf16[2,1,8,1024]{3,2,1,0:T(8,128)(2,1)}, f32[1,128]{1,0:T(1,128)}, bf16[2,1,8,1024]{3,2,1,0:T(8,128)(2,1)}) custom-call(bf16[272,256]{1,0:T(8,128)(2,1)S(1)} %add_convert_fusion.refs_0_, bf16[272,256]{1,0:T(8,128)(2,1)S(1)} %collective-permute-done.10.refs_1_, bf16[2,1,8,1024]{3,2,1,0:T(8,128)(2,1)S(1)} %copy-done, ...), custom_call_target="tpu_custom_call" | custom-call | tf_op jit(solution)/shard_map/pallas_call | solution.py:528
Async XLA Ops:
  2.0 30.7 %copy-start = (bf16[2,1,8,1024]{3,2,1,0:T(8,128)(2,1)S(1)}, bf16[2,1,8,1024]{3,2,1,0:T(8,128)(2,1)}, u32[]{:S(2)}) copy-start(bf16[2,1,8,1024]{3,2,1,0:T(8,128)(2,1)} %refs_2_.1) | copy-start | bytes 98308
  2.0 30.7 %copy-start.1 = (bf16[256]{0:T(256)(128)(2,1)S(1)}, bf16[256]{0:T(256)(128)(2,1)}, u32[]{:S(2)}) copy-start(bf16[256]{0:T(256)(128)(2,1)} %refs_7_.1) | copy-start | bytes 1540
  2.0 9.7 %collective-permute-start.2 = (bf16[224,256]{1,0:T(8,128)(2,1)S(1)}, bf16[224,256]{1,0:T(8,128)(2,1)S(1)}, u32[]{:S(2)}, u32[]{:S(2)}) collective-permute-start(bf16[224,256]{1,0:T(8,128)(2,1)S(1)} %shard_map.121.packed_ref.refs_0_), channel_id=1, source_target_pairs={{0,6},{1,7},{2,4},{3,5},{4,2},{5,3},{6,0},{7,1},{8,14},{9,15},{10,... | collective-permute-start | bytes 344072 | tf_op jit(solution)/shard_map/ppermute | solution.py:477
  7.1 9.7 %collective-permute-start.1 = (bf16[224,256]{1,0:T(8,128)(2,1)S(1)}, bf16[224,256]{1,0:T(8,128)(2,1)S(1)}, u32[]{:S(2)}, u32[]{:S(2)}) collective-permute-start(bf16[224,256]{1,0:T(8,128)(2,1)S(1)} %shard_map.121.packed_ref.refs_0_), channel_id=1, source_target_pairs={{0,4},{1,5},{2,6},{3,7},{4,0},{5,1},{6,2},{7,3},{8,12},{9,13},{10,... | collective-permute-start | bytes 344072 | tf_op jit(solution)/shard_map/ppermute | solution.py:477
  7.1 9.7 %collective-permute-start = (bf16[224,256]{1,0:T(8,128)(2,1)S(1)}, bf16[224,256]{1,0:T(8,128)(2,1)S(1)}, u32[]{:S(2)}, u32[]{:S(2)}) collective-permute-start(bf16[224,256]{1,0:T(8,128)(2,1)S(1)} %shard_map.121.packed_ref.refs_0_), channel_id=1, source_target_pairs={{0,2},{1,3},{2,0},{3,1},{4,6},{5,7},{6,4},{7,5},{8,10},{9,11},{10,... | collective-permute-start | bytes 344072 | tf_op jit(solution)/shard_map/ppermute | solution.py:477
  11.6 5.7 %collective-permute-start.3 = (bf16[224,256]{1,0:T(8,128)(2,1)S(1)}, bf16[224,256]{1,0:T(8,128)(2,1)S(1)}, u32[]{:S(2)}, u32[]{:S(2)}) collective-permute-start(bf16[224,256]{1,0:T(8,128)(2,1)S(1)} %get-tuple-element.18), channel_id=1, source_target_pairs={{0,1},{1,0},{2,3},{3,2},{4,5},{5,4},{6,7},{7,6},{8,9},{9,8},{10,11... | collective-permute-start | bytes 344072 | tf_op jit(solution)/shard_map/ppermute | solution.py:477
  11.7 5.6 %collective-permute-start.6 = (bf16[224,256]{1,0:T(8,128)(2,1)S(1)}, bf16[224,256]{1,0:T(8,128)(2,1)S(1)}, u32[]{:S(2)}, u32[]{:S(2)}) collective-permute-start(bf16[224,256]{1,0:T(8,128)(2,1)S(1)} %collective-permute-done.2.refs_3_), channel_id=1, source_target_pairs={{0,1},{1,0},{2,3},{3,2},{4,5},{5,4},{6,7},{7,6},{8,9},{9,8},{10,11... | collective-permute-start | bytes 344072 | tf_op jit(solution)/shard_map/ppermute | solution.py:477
  16.8 1.3 %collective-permute-start.5 = (bf16[224,256]{1,0:T(8,128)(2,1)S(1)}, bf16[224,256]{1,0:T(8,128)(2,1)S(1)}, u32[]{:S(2)}, u32[]{:S(2)}) collective-permute-start(bf16[224,256]{1,0:T(8,128)(2,1)S(1)} %collective-permute-done.1.refs_2_), channel_id=1, source_target_pairs={{0,1},{1,0},{2,3},{3,2},{4,5},{5,4},{6,7},{7,6},{8,9},{9,8},{10,11... | collective-permute-start | bytes 344072 | tf_op jit(solution)/shard_map/ppermute | solution.py:477
  16.8 1.5 %collective-permute-start.4 = (bf16[224,256]{1,0:T(8,128)(2,1)S(1)}, bf16[224,256]{1,0:T(8,128)(2,1)S(1)}, u32[]{:S(2)}, u32[]{:S(2)}) collective-permute-start(bf16[224,256]{1,0:T(8,128)(2,1)S(1)} %collective-permute-done.refs_1_), channel_id=1, source_target_pairs={{0,1},{1,0},{2,3},{3,2},{4,5},{5,4},{6,7},{7,6},{8,9},{9,8},{10,11... | collective-permute-start | bytes 344072 | tf_op jit(solution)/shard_map/ppermute | solution.py:477
  19.6 7.3 %collective-permute-start.7 = (bf16[336,256]{1,0:T(8,128)(2,1)S(1)}, bf16[336,256]{1,0:T(8,128)(2,1)S(1)}, u32[]{:S(2)}, u32[]{:S(2)}) collective-permute-start(bf16[336,256]{1,0:T(8,128)(2,1)S(1)} %get-tuple-element.22), channel_id=1, source_target_pairs={{0,8},{8,0},{16,24},{24,16},{1,9},{9,1},{17,25},{25,17},{2,10},{10... | collective-permute-start | bytes 516104 | tf_op jit(solution)/shard_map/ppermute | solution.py:480
  21.1 10.0 %collective-permute-start.8 = (bf16[336,256]{1,0:T(8,128)(2,1)S(1)}, bf16[336,256]{1,0:T(8,128)(2,1)S(1)}, u32[]{:S(2)}, u32[]{:S(2)}) collective-permute-start(bf16[336,256]{1,0:T(8,128)(2,1)S(1)} %get-tuple-element.23), channel_id=1, source_target_pairs={{0,16},{8,24},{16,0},{24,8},{1,17},{9,25},{17,1},{25,9},{2,18},{10... | collective-permute-start | bytes 516104 | tf_op jit(solution)/shard_map/ppermute | solution.py:480
  22.6 8.5 %collective-permute-start.9 = (bf16[336,256]{1,0:T(8,128)(2,1)S(1)}, bf16[336,256]{1,0:T(8,128)(2,1)S(1)}, u32[]{:S(2)}, u32[]{:S(2)}) collective-permute-start(bf16[336,256]{1,0:T(8,128)(2,1)S(1)} %get-tuple-element.24), channel_id=1, source_target_pairs={{0,24},{8,16},{16,8},{24,0},{1,25},{9,17},{17,9},{25,1},{2,26},{10... | collective-permute-start | bytes 516104 | tf_op jit(solution)/shard_map/ppermute | solution.py:480
  31.2 1.4 %collective-permute-start.10 = (bf16[272,256]{1,0:T(8,128)(2,1)S(1)}, bf16[272,256]{1,0:T(8,128)(2,1)S(1)}, u32[]{:S(2)}, u32[]{:S(2)}) collective-permute-start(bf16[272,256]{1,0:T(8,128)(2,1)S(1)} %add_convert_fusion.refs_0_), channel_id=1, source_target_pairs={{0,1},{1,0},{2,3},{3,2},{4,5},{5,4},{6,7},{7,6},{8,9},{9,8},{10,11... | collective-permute-start | bytes 417800 | tf_op jit(solution)/shard_map/ppermute | solution.py:477

commit v3 on v2

--- a/solution.py
+++ b/solution.py
@@ -11,6 +11,7 @@
 F32 = jnp.float32
 BF16 = jnp.bfloat16
 LABEL_ROWS = 16
+TILE = 128
 
 
 OFFSETS = [
@@ -326,7 +327,7 @@
     nc, nt, ni, own_c, zs, tok_n, parts_n = sizes
     ours, theirs, r_ref, w1, w2, w1_t, w2_t, class_w, neck_w = refs[:9]
     parts = refs[9 : 9 + parts_n]
-    encoded_ref, loss_ref, grad_ref, grid, cols, slope1, grad2, cols3 = refs[9 + parts_n :]
+    encoded_ref, loss_ref, grad_ref, grid, cols, slope1, grad2, cols3, hid1, hid2 = refs[9 + parts_n :]
     channels = grid.shape[2]
     slab = nt * ni
     rows = nc * ni
@@ -355,23 +356,25 @@
                     moved, (b - 1) * ni
                 ).astype(BF16)
 
-    def conv(weights):
-        total = None
-        for a in range(3):
-            matrix = weights[a].reshape(taps * channels, channels)
-            term = dot(cols[a * slab : a * slab + cells, :], matrix)
-            total = term if total is None else total + term
-        return total
+    def conv(weights, out):
+        for m in range(0, cells, TILE):
+            total = None
+            for a in range(3):
+                matrix = weights[a].reshape(taps * channels, channels)
+                term = dot(cols[a * slab + m : a * slab + m + TILE, :], matrix)
+                total = term if total is None else total + term
+            out[m : m + TILE, :] = total
 
     for c in range(nc):
         spread(grid[c], c)
-    hidden_one = conv(w1)
+    conv(w1, hid1)
     for c in range(nc):
-        v = hidden_one[c * slab : (c + 1) * slab, :]
+        v = hid1[c * slab : (c + 1) * slab, :]
         s = sigma_of(v)
         slope1[c + 1, ni : ni + slab, :] = s * (1.0 + v * (1.0 - s))
         spread((v * s).astype(BF16).astype(F32), c)
-    hidden_two = conv(w2)
+    conv(w2, hid2)
+    hidden_two = hid2[...]
     sigma_two = sigma_of(hidden_two)
     active_two = (hidden_two * sigma_two).astype(BF16)
     class_row = class_w[...].astype(F32).reshape(1, channels)
@@ -427,14 +430,16 @@
     shifted = [along_inline(g1, 1 - e, ni) for e in range(3)]
     total = jnp.zeros((own_c * ni, channels), F32)
     for a in range(3):
+        pieces = []
         for b in range(3):
             for e in range(3):
                 cells_in = [
                     shifted[e][(i + 2 - a) * band + (2 - b) * ni : (i + 2 - a) * band + (3 - b) * ni, :]
                     for i in range(own_c)
                 ]
-                piece = jnp.concatenate(cells_in, axis=0).astype(BF16)
-                total = total + dot(piece, w1_t[a, b, e])
+                pieces.append(jnp.concatenate(cells_in, axis=0).astype(BF16))
+        matrix = w1_t[a].reshape(taps * channels, channels)
+        total = total + dot(jnp.concatenate(pieces, axis=1), matrix)
     grad = dot_t(total.astype(BF16), neck_w[...])
     grad_ref[...] = grad.reshape(grad_ref.shape).astype(BF16)
 
@@ -540,6 +545,8 @@
                 pltpu.VMEM((nc + 2, (nt + 4) * ni, channels), F32),
                 pltpu.VMEM((nc + 4, (nt + 6) * ni, channels), F32),
                 pltpu.VMEM(((own_c + 4) * 4 * ni, 9 * channels), BF16),
+                pltpu.VMEM((nc * slab, channels), F32),
+                pltpu.VMEM((nc * slab, channels), F32),
             ],
             compiler_params=pltpu.CompilerParams(vmem_limit_bytes=36 * 2**20),
         )(half, other, residual, first_in, second_in, first_t, second_t, w_class, neck_w, *parts)
@@ -565,6 +572,7 @@
         and power_of_two(heads_n)
         and residual.shape[0] * heads_n == nc
         and nc * nt * ni <= 1024
+        and (nc * nt * ni) % TILE == 0
         and width % 128 == 0
         and w_neck.shape[1] == width
         and (residual.shape[0] * ni) % 16 == 0

time: 43.6 us -> 40.2 us (0.922)
  Pallas kernels: 17.2 us -> 13.8 us
    pallas_call x1, Pallas kernels: 10.8 us -> 7.33 us  [whole_grid(): pl.pallas_call(functools.partial(decoder_kernel, (nc, nt, ni, own_c, zs,...]
  transfers between devices with their start and end apart: 11 -> 11, of which waited for: 6 -> 6; matrix products, arithmetic and copies ran while one was open for 0% -> 0% of each run, Pallas kernels for 9% -> 10%
where the time goes in v3:
time: 40.2 us; the launch traced here: 40 us
  waiting for transfers between devices  15 us (37%)
  Pallas kernels  13.8 us (34%)
  starting transfers between devices  10.5 us (26%)
  between operations  0.71 us (2%)
    ppermute x3, waiting for transfers between devices, swap_heads(): return lax.ppermute(value, 'heads', [(i, i ^ bits) for i in range(heads_n)])  8.04 us
    pallas_call x1, Pallas kernels, whole_grid(): pl.pallas_call(functools.partial(decoder_kernel, (nc, nt, ni, own_c, zs,...  7.33 us
    ppermute x8, waiting for transfers between devices, swap_tok(): return lax.ppermute(value, 'tok', [(i, i ^ bits) for i in range(tok_n)])  6.94 us
    ppermute x8, starting transfers between devices, swap_tok(): return lax.ppermute(value, 'tok', [(i, i ^ bits) for i in range(tok_n)])  6.9 us
    pallas_call x1, Pallas kernels, whole_grid(): pl.pallas_call(weights_kernel, out_shape=[pltpu.VMEM(w_first.shape, BF16)...  3.82 us
    ppermute x3, starting transfers between devices, swap_heads(): return lax.ppermute(value, 'heads', [(i, i ^ bits) for i in range(heads_n)])  3.55 us
    pallas_call x1, Pallas kernels, whole_grid(): pl.pallas_call(functools.partial(pack_kernel, tok_n), out_shape=pltpu.VME...  1.32 us
    pallas_call x1, Pallas kernels, whole_grid(): pl.pallas_call(functools.partial(attention_kernel, tok_n, zs, rows, own),...  1.31 us
  transfers between devices with their start and end apart: 11, of which 6 were waited for; matrix products, arithmetic and copies ran while one was open for 0% of the time, Pallas kernels for 10%

profile of v3, /device:TPU:0, one launch (start us, length us, event | category | flops | bytes accessed | tf_op | source)
XLA Modules:
  0.0 40.0 jit_solution(14201609645127611991)
XLA Ops:
  0.6 1.3 %shard_map.121.packed_ref.refs_0_ = bf16[224,256]{1,0:T(8,128)(2,1)S(1)} custom-call(bf16[1,8,8,256]{3,2,1,0:T(8,128)(2,1)} %q_ref.1, bf16[1,8,8,256]{3,2,1,0:T(8,128)(2,1)} %k_ref.1, bf16[1,8,8,256]{3,2,1,0:T(8,128)(2,1)} %v_ref.1, bf16[2,1,8,1024]{3,2,1,0:T(8,128)(2,1)} %refs_2_.1, bf16[1024,256]{1,0:T(8,128)(2,1)} %neck_ref.3, s32[2,1,8]{2,1,0:T(1,128)} %bitcast.5), custom_call_target="tpu_custom_call" | custom-call | tf_op jit(solution)/shard_map/pallas_call | solution.py:487
  2.0 0.0 copy-start
  2.0 0.0 copy-start.1
  2.0 5.1 %collective-permute-start.2 = (bf16[224,256]{1,0:T(8,128)(2,1)S(1)}, bf16[224,256]{1,0:T(8,128)(2,1)S(1)}, u32[]{:S(2)}, u32[]{:S(2)}) collective-permute-start(bf16[224,256]{1,0:T(8,128)(2,1)S(1)} %shard_map.121.packed_ref.refs_0_), channel_id=1, source_target_pairs={{0,6},{1,7},{2,4},{3,5},{4,2},{5,3},{6,0},{7,1},{8,14},{9,15},{10,... | collective-permute-start | bytes 344072 | tf_op jit(solution)/shard_map/ppermute | solution.py:482
  7.1 0.0 collective-permute-start.1
  7.1 0.6 %collective-permute-start = (bf16[224,256]{1,0:T(8,128)(2,1)S(1)}, bf16[224,256]{1,0:T(8,128)(2,1)S(1)}, u32[]{:S(2)}, u32[]{:S(2)}) collective-permute-start(bf16[224,256]{1,0:T(8,128)(2,1)S(1)} %shard_map.121.packed_ref.refs_0_), channel_id=1, source_target_pairs={{0,2},{1,3},{2,0},{3,1},{4,6},{5,7},{6,4},{7,5},{8,10},{9,11},{10,... | collective-permute-start | bytes 344072 | tf_op jit(solution)/shard_map/ppermute | solution.py:482
  7.7 3.8 %shard_map.122 = (bf16[3,3,3,256,256]{4,3,2,1,0:T(8,128)(2,1)S(1)}, bf16[3,3,3,256,256]{4,3,2,1,0:T(8,128)(2,1)S(1)}, bf16[3,3,3,256,256]{4,3,2,1,0:T(8,128)(2,1...) custom-call(bf16[3,3,3,256,256]{4,3,2,1,0:T(8,128)(2,1)} %first_ref., ...), custom_call_target="tpu_custom_call" | custom-call | bytes 29360128 | tf_op jit(solution)/shard_map/pallas_call | solution.py:495
  11.6 0.1 collective-permute-start.3
  11.6 0.0 collective-permute-done.2.refs_3_
  11.7 0.5 %collective-permute-start.6 = (bf16[224,256]{1,0:T(8,128)(2,1)S(1)}, bf16[224,256]{1,0:T(8,128)(2,1)S(1)}, u32[]{:S(2)}, u32[]{:S(2)}) collective-permute-start(bf16[224,256]{1,0:T(8,128)(2,1)S(1)} %collective-permute-done.2.refs_3_), channel_id=1, source_target_pairs={{0,1},{1,0},{2,3},{3,2},{4,5},{5,4},{6,7},{7,6},{8,9},{9,8},{10,11... | collective-permute-start | bytes 344072 | tf_op jit(solution)/shard_map/ppermute | solution.py:482
  12.2 4.6 %collective-permute-done.1.refs_2_ = bf16[224,256]{1,0:T(8,128)(2,1)S(1)} collective-permute-done((bf16[224,256]{1,0:T(8,128)(2,1)S(1)}, bf16[224,256]{1,0:T(8,128)(2,1)S(1)}, u32[]{:S(2)}, u32[]{:S(2)}) %collective-permute-start.1) | collective-permute-done | bytes 114720 | tf_op jit(solution)/shard_map/ppermute | solution.py:482
  16.8 0.0 collective-permute-start.5
  16.8 0.0 collective-permute-done.refs_1_
  16.8 0.5 %collective-permute-start.4 = (bf16[224,256]{1,0:T(8,128)(2,1)S(1)}, bf16[224,256]{1,0:T(8,128)(2,1)S(1)}, u32[]{:S(2)}, u32[]{:S(2)}) collective-permute-start(bf16[224,256]{1,0:T(8,128)(2,1)S(1)} %collective-permute-done.refs_1_), channel_id=1, source_target_pairs={{0,1},{1,0},{2,3},{3,2},{4,5},{5,4},{6,7},{7,6},{8,9},{9,8},{10,11... | collective-permute-start | bytes 344072 | tf_op jit(solution)/shard_map/ppermute | solution.py:482
  17.3 0.0 collective-permute-done.3.refs_4_
  17.3 0.0 collective-permute-done.6.refs_7_
  17.3 0.8 %collective-permute-done.5.refs_6_ = bf16[224,256]{1,0:T(8,128)(2,1)S(1)} collective-permute-done((bf16[224,256]{1,0:T(8,128)(2,1)S(1)}, bf16[224,256]{1,0:T(8,128)(2,1)S(1)}, u32[]{:S(2)}, u32[]{:S(2)}) %collective-permute-start.5) | collective-permute-done | bytes 114720 | tf_op jit(solution)/shard_map/ppermute | solution.py:482
  18.1 0.2 collective-permute-done.4.refs_5_
  18.3 1.3 %shard_map.123 = (bf16[336,256]{1,0:T(8,128)(2,1)S(1)}, bf16[336,256]{1,0:T(8,128)(2,1)S(1)}, bf16[336,256]{1,0:T(8,128)(2,1)S(1)}, bf16[336,256]{1,0:T(8,128)(2,1)S(1)}) custom-call(bf16[224,256]{1,0:T(8,128)(2,1)S(1)} %shard_map.121.packed_ref.refs_0_, bf16[224,256]{1,0:T(8,128)(2,1)S(1)} %collective-permute-done.refs_1_, ...), custom_call_target="tpu_custom_call" | custom-call | tf_op jit(solution)/shard_map/pallas_call | solution.py:514
  19.6 1.6 %collective-permute-start.7 = (bf16[336,256]{1,0:T(8,128)(2,1)S(1)}, bf16[336,256]{1,0:T(8,128)(2,1)S(1)}, u32[]{:S(2)}, u32[]{:S(2)}) collective-permute-start(bf16[336,256]{1,0:T(8,128)(2,1)S(1)} %get-tuple-element.22), channel_id=1, source_target_pairs={{0,8},{8,0},{16,24},{24,16},{1,9},{9,1},{17,25},{25,17},{2,10},{10... | collective-permute-start | bytes 516104 | tf_op jit(solution)/shard_map/ppermute | solution.py:485
  21.1 1.5 %collective-permute-start.8 = (bf16[336,256]{1,0:T(8,128)(2,1)S(1)}, bf16[336,256]{1,0:T(8,128)(2,1)S(1)}, u32[]{:S(2)}, u32[]{:S(2)}) collective-permute-start(bf16[336,256]{1,0:T(8,128)(2,1)S(1)} %get-tuple-element.23), channel_id=1, source_target_pairs={{0,16},{8,24},{16,0},{24,8},{1,17},{9,25},{17,1},{25,9},{2,18},{10... | collective-permute-start | bytes 516104 | tf_op jit(solution)/shard_map/ppermute | solution.py:485
  22.6 0.5 %collective-permute-start.9 = (bf16[336,256]{1,0:T(8,128)(2,1)S(1)}, bf16[336,256]{1,0:T(8,128)(2,1)S(1)}, u32[]{:S(2)}, u32[]{:S(2)}) collective-permute-start(bf16[336,256]{1,0:T(8,128)(2,1)S(1)} %get-tuple-element.24), channel_id=1, source_target_pairs={{0,24},{8,16},{16,8},{24,0},{1,25},{9,17},{17,9},{25,1},{2,26},{10... | collective-permute-start | bytes 516104 | tf_op jit(solution)/shard_map/ppermute | solution.py:485
  23.1 3.7 %collective-permute-done.7.refs_10_ = bf16[336,256]{1,0:T(8,128)(2,1)S(1)} collective-permute-done((bf16[336,256]{1,0:T(8,128)(2,1)S(1)}, bf16[336,256]{1,0:T(8,128)(2,1)S(1)}, u32[]{:S(2)}, u32[]{:S(2)}) %collective-permute-start.7) | collective-permute-done | bytes 172064 | tf_op jit(solution)/shard_map/ppermute | solution.py:485
  26.8 4.3 %collective-permute-done.8.refs_11_ = bf16[336,256]{1,0:T(8,128)(2,1)S(1)} collective-permute-done((bf16[336,256]{1,0:T(8,128)(2,1)S(1)}, bf16[336,256]{1,0:T(8,128)(2,1)S(1)}, u32[]{:S(2)}, u32[]{:S(2)}) %collective-permute-start.8) | collective-permute-done | bytes 172064 | tf_op jit(solution)/shard_map/ppermute | solution.py:485
  31.2 0.0 collective-permute-done.9.refs_12_
  31.2 0.1 add_convert_fusion.refs_0_
  31.2 0.1 collective-permute-start.10
  31.3 1.3 %collective-permute-done.10.refs_1_ = bf16[272,256]{1,0:T(8,128)(2,1)S(1)} collective-permute-done((bf16[272,256]{1,0:T(8,128)(2,1)S(1)}, bf16[272,256]{1,0:T(8,128)(2,1)S(1)}, u32[]{:S(2)}, u32[]{:S(2)}) %collective-permute-start.10) | collective-permute-done | bytes 139296 | tf_op jit(solution)/shard_map/ppermute | solution.py:482
  32.7 0.0 copy-done
  32.7 0.0 copy-done.1
  32.7 7.3 %shard_map.124 = (bf16[2,1,8,1024]{3,2,1,0:T(8,128)(2,1)}, f32[1,128]{1,0:T(1,128)}, bf16[2,1,8,1024]{3,2,1,0:T(8,128)(2,1)}) custom-call(bf16[272,256]{1,0:T(8,128)(2,1)S(1)} %add_convert_fusion.refs_0_, bf16[272,256]{1,0:T(8,128)(2,1)S(1)} %collective-permute-done.10.refs_1_, bf16[2,1,8,1024]{3,2,1,0:T(8,128)(2,1)S(1)} %copy-done, ...), custom_call_target="tpu_custom_call" | custom-call | tf_op jit(solution)/shard_map/pallas_call | solution.py:533
Async XLA Ops:
  2.0 30.7 %copy-start = (bf16[2,1,8,1024]{3,2,1,0:T(8,128)(2,1)S(1)}, bf16[2,1,8,1024]{3,2,1,0:T(8,128)(2,1)}, u32[]{:S(2)}) copy-start(bf16[2,1,8,1024]{3,2,1,0:T(8,128)(2,1)} %refs_2_.1) | copy-start | bytes 98308
  2.0 30.7 %copy-start.1 = (bf16[256]{0:T(256)(128)(2,1)S(1)}, bf16[256]{0:T(256)(128)(2,1)}, u32[]{:S(2)}) copy-start(bf16[256]{0:T(256)(128)(2,1)} %refs_7_.1) | copy-start | bytes 1540
  2.0 9.7 %collective-permute-start.2 = (bf16[224,256]{1,0:T(8,128)(2,1)S(1)}, bf16[224,256]{1,0:T(8,128)(2,1)S(1)}, u32[]{:S(2)}, u32[]{:S(2)}) collective-permute-start(bf16[224,256]{1,0:T(8,128)(2,1)S(1)} %shard_map.121.packed_ref.refs_0_), channel_id=1, source_target_pairs={{0,6},{1,7},{2,4},{3,5},{4,2},{5,3},{6,0},{7,1},{8,14},{9,15},{10,... | collective-permute-start | bytes 344072 | tf_op jit(solution)/shard_map/ppermute | solution.py:482
  7.1 9.7 %collective-permute-start.1 = (bf16[224,256]{1,0:T(8,128)(2,1)S(1)}, bf16[224,256]{1,0:T(8,128)(2,1)S(1)}, u32[]{:S(2)}, u32[]{:S(2)}) collective-permute-start(bf16[224,256]{1,0:T(8,128)(2,1)S(1)} %shard_map.121.packed_ref.refs_0_), channel_id=1, source_target_pairs={{0,4},{1,5},{2,6},{3,7},{4,0},{5,1},{6,2},{7,3},{8,12},{9,13},{10,... | collective-permute-start | bytes 344072 | tf_op jit(solution)/shard_map/ppermute | solution.py:482
  7.1 9.7 %collective-permute-start = (bf16[224,256]{1,0:T(8,128)(2,1)S(1)}, bf16[224,256]{1,0:T(8,128)(2,1)S(1)}, u32[]{:S(2)}, u32[]{:S(2)}) collective-permute-start(bf16[224,256]{1,0:T(8,128)(2,1)S(1)} %shard_map.121.packed_ref.refs_0_), channel_id=1, source_target_pairs={{0,2},{1,3},{2,0},{3,1},{4,6},{5,7},{6,4},{7,5},{8,10},{9,11},{10,... | collective-permute-start | bytes 344072 | tf_op jit(solution)/shard_map/ppermute | solution.py:482
  11.6 5.7 %collective-permute-start.3 = (bf16[224,256]{1,0:T(8,128)(2,1)S(1)}, bf16[224,256]{1,0:T(8,128)(2,1)S(1)}, u32[]{:S(2)}, u32[]{:S(2)}) collective-permute-start(bf16[224,256]{1,0:T(8,128)(2,1)S(1)} %get-tuple-element.18), channel_id=1, source_target_pairs={{0,1},{1,0},{2,3},{3,2},{4,5},{5,4},{6,7},{7,6},{8,9},{9,8},{10,11... | collective-permute-start | bytes 344072 | tf_op jit(solution)/shard_map/ppermute | solution.py:482
  11.7 5.6 %collective-permute-start.6 = (bf16[224,256]{1,0:T(8,128)(2,1)S(1)}, bf16[224,256]{1,0:T(8,128)(2,1)S(1)}, u32[]{:S(2)}, u32[]{:S(2)}) collective-permute-start(bf16[224,256]{1,0:T(8,128)(2,1)S(1)} %collective-permute-done.2.refs_3_), channel_id=1, source_target_pairs={{0,1},{1,0},{2,3},{3,2},{4,5},{5,4},{6,7},{7,6},{8,9},{9,8},{10,11... | collective-permute-start | bytes 344072 | tf_op jit(solution)/shard_map/ppermute | solution.py:482
  16.8 1.3 %collective-permute-start.5 = (bf16[224,256]{1,0:T(8,128)(2,1)S(1)}, bf16[224,256]{1,0:T(8,128)(2,1)S(1)}, u32[]{:S(2)}, u32[]{:S(2)}) collective-permute-start(bf16[224,256]{1,0:T(8,128)(2,1)S(1)} %collective-permute-done.1.refs_2_), channel_id=1, source_target_pairs={{0,1},{1,0},{2,3},{3,2},{4,5},{5,4},{6,7},{7,6},{8,9},{9,8},{10,11... | collective-permute-start | bytes 344072 | tf_op jit(solution)/shard_map/ppermute | solution.py:482
  16.8 1.5 %collective-permute-start.4 = (bf16[224,256]{1,0:T(8,128)(2,1)S(1)}, bf16[224,256]{1,0:T(8,128)(2,1)S(1)}, u32[]{:S(2)}, u32[]{:S(2)}) collective-permute-start(bf16[224,256]{1,0:T(8,128)(2,1)S(1)} %collective-permute-done.refs_1_), channel_id=1, source_target_pairs={{0,1},{1,0},{2,3},{3,2},{4,5},{5,4},{6,7},{7,6},{8,9},{9,8},{10,11... | collective-permute-start | bytes 344072 | tf_op jit(solution)/shard_map/ppermute | solution.py:482
  19.6 7.3 %collective-permute-start.7 = (bf16[336,256]{1,0:T(8,128)(2,1)S(1)}, bf16[336,256]{1,0:T(8,128)(2,1)S(1)}, u32[]{:S(2)}, u32[]{:S(2)}) collective-permute-start(bf16[336,256]{1,0:T(8,128)(2,1)S(1)} %get-tuple-element.22), channel_id=1, source_target_pairs={{0,8},{8,0},{16,24},{24,16},{1,9},{9,1},{17,25},{25,17},{2,10},{10... | collective-permute-start | bytes 516104 | tf_op jit(solution)/shard_map/ppermute | solution.py:485
  21.1 10.0 %collective-permute-start.8 = (bf16[336,256]{1,0:T(8,128)(2,1)S(1)}, bf16[336,256]{1,0:T(8,128)(2,1)S(1)}, u32[]{:S(2)}, u32[]{:S(2)}) collective-permute-start(bf16[336,256]{1,0:T(8,128)(2,1)S(1)} %get-tuple-element.23), channel_id=1, source_target_pairs={{0,16},{8,24},{16,0},{24,8},{1,17},{9,25},{17,1},{25,9},{2,18},{10... | collective-permute-start | bytes 516104 | tf_op jit(solution)/shard_map/ppermute | solution.py:485
  22.6 8.5 %collective-permute-start.9 = (bf16[336,256]{1,0:T(8,128)(2,1)S(1)}, bf16[336,256]{1,0:T(8,128)(2,1)S(1)}, u32[]{:S(2)}, u32[]{:S(2)}) collective-permute-start(bf16[336,256]{1,0:T(8,128)(2,1)S(1)} %get-tuple-element.24), channel_id=1, source_target_pairs={{0,24},{8,16},{16,8},{24,0},{1,25},{9,17},{17,9},{25,1},{2,26},{10... | collective-permute-start | bytes 516104 | tf_op jit(solution)/shard_map/ppermute | solution.py:485
  31.2 1.4 %collective-permute-start.10 = (bf16[272,256]{1,0:T(8,128)(2,1)S(1)}, bf16[272,256]{1,0:T(8,128)(2,1)S(1)}, u32[]{:S(2)}, u32[]{:S(2)}) collective-permute-start(bf16[272,256]{1,0:T(8,128)(2,1)S(1)} %add_convert_fusion.refs_0_), channel_id=1, source_target_pairs={{0,1},{1,0},{2,3},{3,2},{4,5},{5,4},{6,7},{7,6},{8,9},{9,8},{10,11... | collective-permute-start | bytes 417800 | tf_op jit(solution)/shard_map/ppermute | solution.py:482

commit v4 on v3

--- a/solution.py
+++ b/solution.py
@@ -274,8 +274,14 @@
                     dst[a, b, e] = src[a, b, e].T
 
 
+def far_first(zs):
+    return [0, 1] + list(range(zs - 1, 1, -1))
+
+
 def attention_kernel(tok_n, zs, rows, own, *refs):
-    ours, theirs = refs[:zs], refs[zs : 2 * zs]
+    order = far_first(zs)
+    ours = [refs[order.index(d)] for d in range(zs)]
+    theirs = [refs[zs + order.index(d)] for d in range(zs)]
     out_w, joint_w = refs[2 * zs : 2 + 2 * zs]
     part_refs = refs[2 + 2 * zs : -4]
     qq, kk, vv, part = refs[-4:]
@@ -508,6 +514,7 @@
         cost_estimate=pl.CostEstimate(flops=0, bytes_accessed=28 * 2**20, transcendentals=0),
     )(*kept, packed)
     theirs = [swap_tok(value, 1) for value in [again] + ours[1:]]
+    order = far_first(zs)
     queries_n, keys_n = rows * zs, rows * tok_n
     enc_rows = own * residual.shape[3] // width
     part_shape = pltpu.VMEM((queries_n + LABEL_ROWS + enc_rows, channels), BF16)
@@ -523,8 +530,8 @@
             pltpu.VMEM((queries_n, channels), F32),
         ],
         compiler_params=pltpu.CompilerParams(vmem_limit_bytes=16 * 2**20),
-    )(*ours, *theirs, out_w, joint)
-    parts = [sent[0]] + [swap_heads(sent[d], d) for d in range(1, heads_n)]
+    )(*[ours[d] for d in order], *[theirs[d] for d in order], out_w, joint)
+    parts = [swap_heads(sent[d], d) for d in range(heads_n - 1, 0, -1)] + [sent[0]]
     used = queries_n + LABEL_ROWS
     half = pairwise([part[:used].astype(F32) for part in parts]).astype(BF16)
     other = swap_tok(half, 1)

time: 40.2 us -> 38.7 us (0.963)
  waiting for transfers between devices: 15 us -> 14 us
  starting transfers between devices: 10.5 us -> 9.96 us
    ppermute x8, waiting for transfers between devices: 6.94 us -> 6.05 us  [swap_tok(): return lax.ppermute(value, 'tok', [(i, i ^ bits) for i in range(tok_n)])]
    ppermute x8, starting transfers between devices: 6.9 us -> 6.4 us  [swap_tok(): return lax.ppermute(value, 'tok', [(i, i ^ bits) for i in range(tok_n)])]
  transfers between devices with their start and end apart: 11 -> 11, of which waited for: 6 -> 8; matrix products, arithmetic and copies ran while one was open for 0% -> 0% of each run, Pallas kernels for 10% -> 10%
where the time goes in v4:
time: 38.7 us; the launch traced here: 38.5 us
  waiting for transfers between devices  14 us (36%)
  Pallas kernels  13.8 us (36%)
  starting transfers between devices  9.96 us (26%)
  between operations  0.7 us (2%)
    ppermute x3, waiting for transfers between devices, swap_heads(): return lax.ppermute(value, 'heads', [(i, i ^ bits) for i in range(heads_n)])  7.98 us
    pallas_call x1, Pallas kernels, whole_grid(): pl.pallas_call(functools.partial(decoder_kernel, (nc, nt, ni, own_c, zs,...  7.33 us
    ppermute x8, starting transfers between devices, swap_tok(): return lax.ppermute(value, 'tok', [(i, i ^ bits) for i in range(tok_n)])  6.4 us
    ppermute x8, waiting for transfers between devices, swap_tok(): return lax.ppermute(value, 'tok', [(i, i ^ bits) for i in range(tok_n)])  6.05 us
    pallas_call x1, Pallas kernels, whole_grid(): pl.pallas_call(weights_kernel, out_shape=[pltpu.VMEM(w_first.shape, BF16)...  3.82 us
    ppermute x3, starting transfers between devices, swap_heads(): return lax.ppermute(value, 'heads', [(i, i ^ bits) for i in range(heads_n)])  3.55 us
    pallas_call x1, Pallas kernels, whole_grid(): pl.pallas_call(functools.partial(pack_kernel, tok_n), out_shape=pltpu.VME...  1.32 us
    pallas_call x1, Pallas kernels, whole_grid(): pl.pallas_call(functools.partial(attention_kernel, tok_n, zs, rows, own),...  1.31 us
  transfers between devices with their start and end apart: 11, of which 8 were waited for; matrix products, arithmetic and copies ran while one was open for 0% of the time, Pallas kernels for 10%

profile of v4, /device:TPU:0, one launch (start us, length us, event | category | flops | bytes accessed | tf_op | source)
XLA Modules:
  0.0 38.5 jit_solution(11400034962550559186)
XLA Ops:
  0.6 1.3 %shard_map.121.packed_ref.refs_0_ = bf16[224,256]{1,0:T(8,128)(2,1)S(1)} custom-call(bf16[1,8,8,256]{3,2,1,0:T(8,128)(2,1)} %q_ref.1, bf16[1,8,8,256]{3,2,1,0:T(8,128)(2,1)} %k_ref.1, bf16[1,8,8,256]{3,2,1,0:T(8,128)(2,1)} %v_ref.1, bf16[2,1,8,1024]{3,2,1,0:T(8,128)(2,1)} %refs_2_.1, bf16[1024,256]{1,0:T(8,128)(2,1)} %neck_ref.3, s32[2,1,8]{2,1,0:T(1,128)} %bitcast.5), custom_call_target="tpu_custom_call" | custom-call | tf_op jit(solution)/shard_map/pallas_call | solution.py:493
  2.0 0.0 copy-start
  2.0 0.0 copy-start.1
  2.0 4.1 %collective-permute-start.2 = (bf16[224,256]{1,0:T(8,128)(2,1)S(1)}, bf16[224,256]{1,0:T(8,128)(2,1)S(1)}, u32[]{:S(2)}, u32[]{:S(2)}) collective-permute-start(bf16[224,256]{1,0:T(8,128)(2,1)S(1)} %shard_map.121.packed_ref.refs_0_), channel_id=1, source_target_pairs={{0,4},{1,5},{2,6},{3,7},{4,0},{5,1},{6,2},{7,3},{8,12},{9,13},{10,... | collective-permute-start | bytes 344072 | tf_op jit(solution)/shard_map/ppermute | solution.py:488
  6.1 1.3 %collective-permute-start.1 = (bf16[224,256]{1,0:T(8,128)(2,1)S(1)}, bf16[224,256]{1,0:T(8,128)(2,1)S(1)}, u32[]{:S(2)}, u32[]{:S(2)}) collective-permute-start(bf16[224,256]{1,0:T(8,128)(2,1)S(1)} %shard_map.121.packed_ref.refs_0_), channel_id=1, source_target_pairs={{0,6},{1,7},{2,4},{3,5},{4,2},{5,3},{6,0},{7,1},{8,14},{9,15},{10,... | collective-permute-start | bytes 344072 | tf_op jit(solution)/shard_map/ppermute | solution.py:488
  7.4 0.2 collective-permute-start
  7.7 3.8 %shard_map.122 = (bf16[3,3,3,256,256]{4,3,2,1,0:T(8,128)(2,1)S(1)}, bf16[3,3,3,256,256]{4,3,2,1,0:T(8,128)(2,1)S(1)}, bf16[3,3,3,256,256]{4,3,2,1,0:T(8,128)(2,1...) custom-call(bf16[3,3,3,256,256]{4,3,2,1,0:T(8,128)(2,1)} %first_ref., ...), custom_call_target="tpu_custom_call" | custom-call | bytes 29360128 | tf_op jit(solution)/shard_map/pallas_call | solution.py:501
  11.5 0.1 collective-permute-start.3
  11.6 3.4 %collective-permute-done.2.refs_3_ = bf16[224,256]{1,0:T(8,128)(2,1)S(1)} collective-permute-done((bf16[224,256]{1,0:T(8,128)(2,1)S(1)}, bf16[224,256]{1,0:T(8,128)(2,1)S(1)}, u32[]{:S(2)}, u32[]{:S(2)}) %collective-permute-start.2) | collective-permute-done | bytes 114720 | tf_op jit(solution)/shard_map/ppermute | solution.py:488
  15.0 0.0 collective-permute-start.6
  15.0 0.0 collective-permute-done.1.refs_2_
  15.0 0.5 %collective-permute-start.5 = (bf16[224,256]{1,0:T(8,128)(2,1)S(1)}, bf16[224,256]{1,0:T(8,128)(2,1)S(1)}, u32[]{:S(2)}, u32[]{:S(2)}) collective-permute-start(bf16[224,256]{1,0:T(8,128)(2,1)S(1)} %collective-permute-done.1.refs_2_), channel_id=1, source_target_pairs={{0,1},{1,0},{2,3},{3,2},{4,5},{5,4},{6,7},{7,6},{8,9},{9,8},{10,11... | collective-permute-start | bytes 344072 | tf_op jit(solution)/shard_map/ppermute | solution.py:488
  15.5 0.0 collective-permute-done.refs_1_
  15.5 0.1 collective-permute-start.4
  15.6 0.0 collective-permute-done.3.refs_4_
  15.6 0.7 %collective-permute-done.6.refs_7_ = bf16[224,256]{1,0:T(8,128)(2,1)S(1)} collective-permute-done((bf16[224,256]{1,0:T(8,128)(2,1)S(1)}, bf16[224,256]{1,0:T(8,128)(2,1)S(1)}, u32[]{:S(2)}, u32[]{:S(2)}) %collective-permute-start.6) | collective-permute-done | bytes 114720 | tf_op jit(solution)/shard_map/ppermute | solution.py:488
  16.3 0.2 collective-permute-done.5.refs_6_
  16.5 0.4 collective-permute-done.4.refs_5_
  16.9 1.3 %shard_map.123 = (bf16[336,256]{1,0:T(8,128)(2,1)S(1)}, bf16[336,256]{1,0:T(8,128)(2,1)S(1)}, bf16[336,256]{1,0:T(8,128)(2,1)S(1)}, bf16[336,256]{1,0:T(8,128)(2,1)S(1)}) custom-call(bf16[224,256]{1,0:T(8,128)(2,1)S(1)} %shard_map.121.packed_ref.refs_0_, bf16[224,256]{1,0:T(8,128)(2,1)S(1)} %collective-permute-done.refs_1_, ...), custom_call_target="tpu_custom_call" | custom-call | tf_op jit(solution)/shard_map/pallas_call | solution.py:521
  18.2 2.9 %collective-permute-start.7 = (bf16[336,256]{1,0:T(8,128)(2,1)S(1)}, bf16[336,256]{1,0:T(8,128)(2,1)S(1)}, u32[]{:S(2)}, u32[]{:S(2)}) collective-permute-start(bf16[336,256]{1,0:T(8,128)(2,1)S(1)} %get-tuple-element.21), channel_id=1, source_target_pairs={{0,24},{8,16},{16,8},{24,0},{1,25},{9,17},{17,9},{25,1},{2,26},{10... | collective-permute-start | bytes 516104 | tf_op jit(solution)/shard_map/ppermute | solution.py:491
  21.0 0.5 %collective-permute-start.8 = (bf16[336,256]{1,0:T(8,128)(2,1)S(1)}, bf16[336,256]{1,0:T(8,128)(2,1)S(1)}, u32[]{:S(2)}, u32[]{:S(2)}) collective-permute-start(bf16[336,256]{1,0:T(8,128)(2,1)S(1)} %get-tuple-element.22), channel_id=1, source_target_pairs={{0,16},{8,24},{16,0},{24,8},{1,17},{9,25},{17,1},{25,9},{2,18},{10... | collective-permute-start | bytes 516104 | tf_op jit(solution)/shard_map/ppermute | solution.py:491
  21.5 0.2 collective-permute-start.9
  21.7 4.6 %collective-permute-done.7.refs_9_ = bf16[336,256]{1,0:T(8,128)(2,1)S(1)} collective-permute-done((bf16[336,256]{1,0:T(8,128)(2,1)S(1)}, bf16[336,256]{1,0:T(8,128)(2,1)S(1)}, u32[]{:S(2)}, u32[]{:S(2)}) %collective-permute-start.7) | collective-permute-done | bytes 172064 | tf_op jit(solution)/shard_map/ppermute | solution.py:491
  26.4 3.1 %collective-permute-done.8.refs_10_ = bf16[336,256]{1,0:T(8,128)(2,1)S(1)} collective-permute-done((bf16[336,256]{1,0:T(8,128)(2,1)S(1)}, bf16[336,256]{1,0:T(8,128)(2,1)S(1)}, u32[]{:S(2)}, u32[]{:S(2)}) %collective-permute-start.8) | collective-permute-done | bytes 172064 | tf_op jit(solution)/shard_map/ppermute | solution.py:491
  29.4 0.3 collective-permute-done.9.refs_11_
  29.7 0.1 add_convert_fusion.refs_0_
  29.8 0.1 collective-permute-start.10
  29.9 1.3 %collective-permute-done.10.refs_1_ = bf16[272,256]{1,0:T(8,128)(2,1)S(1)} collective-permute-done((bf16[272,256]{1,0:T(8,128)(2,1)S(1)}, bf16[272,256]{1,0:T(8,128)(2,1)S(1)}, u32[]{:S(2)}, u32[]{:S(2)}) %collective-permute-start.10) | collective-permute-done | bytes 139296 | tf_op jit(solution)/shard_map/ppermute | solution.py:488
  31.2 0.0 copy-done
  31.2 0.0 copy-done.1
  31.2 7.3 %shard_map.124 = (bf16[2,1,8,1024]{3,2,1,0:T(8,128)(2,1)}, f32[1,128]{1,0:T(1,128)}, bf16[2,1,8,1024]{3,2,1,0:T(8,128)(2,1)}) custom-call(bf16[272,256]{1,0:T(8,128)(2,1)S(1)} %add_convert_fusion.refs_0_, bf16[272,256]{1,0:T(8,128)(2,1)S(1)} %collective-permute-done.10.refs_1_, bf16[2,1,8,1024]{3,2,1,0:T(8,128)(2,1)S(1)} %copy-done, ...), custom_call_target="tpu_custom_call" | custom-call | tf_op jit(solution)/shard_map/pallas_call | solution.py:540
Async XLA Ops:
  2.0 29.3 %copy-start = (bf16[2,1,8,1024]{3,2,1,0:T(8,128)(2,1)S(1)}, bf16[2,1,8,1024]{3,2,1,0:T(8,128)(2,1)}, u32[]{:S(2)}) copy-start(bf16[2,1,8,1024]{3,2,1,0:T(8,128)(2,1)} %refs_2_.1) | copy-start | bytes 98308
  2.0 29.3 %copy-start.1 = (bf16[256]{0:T(256)(128)(2,1)S(1)}, bf16[256]{0:T(256)(128)(2,1)}, u32[]{:S(2)}) copy-start(bf16[256]{0:T(256)(128)(2,1)} %refs_7_.1) | copy-start | bytes 1540
  2.0 13.0 %collective-permute-start.2 = (bf16[224,256]{1,0:T(8,128)(2,1)S(1)}, bf16[224,256]{1,0:T(8,128)(2,1)S(1)}, u32[]{:S(2)}, u32[]{:S(2)}) collective-permute-start(bf16[224,256]{1,0:T(8,128)(2,1)S(1)} %shard_map.121.packed_ref.refs_0_), channel_id=1, source_target_pairs={{0,4},{1,5},{2,6},{3,7},{4,0},{5,1},{6,2},{7,3},{8,12},{9,13},{10,... | collective-permute-start | bytes 344072 | tf_op jit(solution)/shard_map/ppermute | solution.py:488
  6.1 8.9 %collective-permute-start.1 = (bf16[224,256]{1,0:T(8,128)(2,1)S(1)}, bf16[224,256]{1,0:T(8,128)(2,1)S(1)}, u32[]{:S(2)}, u32[]{:S(2)}) collective-permute-start(bf16[224,256]{1,0:T(8,128)(2,1)S(1)} %shard_map.121.packed_ref.refs_0_), channel_id=1, source_target_pairs={{0,6},{1,7},{2,4},{3,5},{4,2},{5,3},{6,0},{7,1},{8,14},{9,15},{10,... | collective-permute-start | bytes 344072 | tf_op jit(solution)/shard_map/ppermute | solution.py:488
  7.4 8.1 %collective-permute-start = (bf16[224,256]{1,0:T(8,128)(2,1)S(1)}, bf16[224,256]{1,0:T(8,128)(2,1)S(1)}, u32[]{:S(2)}, u32[]{:S(2)}) collective-permute-start(bf16[224,256]{1,0:T(8,128)(2,1)S(1)} %shard_map.121.packed_ref.refs_0_), channel_id=1, source_target_pairs={{0,2},{1,3},{2,0},{3,1},{4,6},{5,7},{6,4},{7,5},{8,10},{9,11},{10,... | collective-permute-start | bytes 344072 | tf_op jit(solution)/shard_map/ppermute | solution.py:488
  11.5 4.1 %collective-permute-start.3 = (bf16[224,256]{1,0:T(8,128)(2,1)S(1)}, bf16[224,256]{1,0:T(8,128)(2,1)S(1)}, u32[]{:S(2)}, u32[]{:S(2)}) collective-permute-start(bf16[224,256]{1,0:T(8,128)(2,1)S(1)} %get-tuple-element.18), channel_id=1, source_target_pairs={{0,1},{1,0},{2,3},{3,2},{4,5},{5,4},{6,7},{7,6},{8,9},{9,8},{10,11... | collective-permute-start | bytes 344072 | tf_op jit(solution)/shard_map/ppermute | solution.py:488
  15.0 1.3 %collective-permute-start.6 = (bf16[224,256]{1,0:T(8,128)(2,1)S(1)}, bf16[224,256]{1,0:T(8,128)(2,1)S(1)}, u32[]{:S(2)}, u32[]{:S(2)}) collective-permute-start(bf16[224,256]{1,0:T(8,128)(2,1)S(1)} %collective-permute-done.2.refs_3_), channel_id=1, source_target_pairs={{0,1},{1,0},{2,3},{3,2},{4,5},{5,4},{6,7},{7,6},{8,9},{9,8},{10,11... | collective-permute-start | bytes 344072 | tf_op jit(solution)/shard_map/ppermute | solution.py:488
  15.0 1.5 %collective-permute-start.5 = (bf16[224,256]{1,0:T(8,128)(2,1)S(1)}, bf16[224,256]{1,0:T(8,128)(2,1)S(1)}, u32[]{:S(2)}, u32[]{:S(2)}) collective-permute-start(bf16[224,256]{1,0:T(8,128)(2,1)S(1)} %collective-permute-done.1.refs_2_), channel_id=1, source_target_pairs={{0,1},{1,0},{2,3},{3,2},{4,5},{5,4},{6,7},{7,6},{8,9},{9,8},{10,11... | collective-permute-start | bytes 344072 | tf_op jit(solution)/shard_map/ppermute | solution.py:488
  15.5 1.3 %collective-permute-start.4 = (bf16[224,256]{1,0:T(8,128)(2,1)S(1)}, bf16[224,256]{1,0:T(8,128)(2,1)S(1)}, u32[]{:S(2)}, u32[]{:S(2)}) collective-permute-start(bf16[224,256]{1,0:T(8,128)(2,1)S(1)} %collective-permute-done.refs_1_), channel_id=1, source_target_pairs={{0,1},{1,0},{2,3},{3,2},{4,5},{5,4},{6,7},{7,6},{8,9},{9,8},{10,11... | collective-permute-start | bytes 344072 | tf_op jit(solution)/shard_map/ppermute | solution.py:488
  18.2 8.2 %collective-permute-start.7 = (bf16[336,256]{1,0:T(8,128)(2,1)S(1)}, bf16[336,256]{1,0:T(8,128)(2,1)S(1)}, u32[]{:S(2)}, u32[]{:S(2)}) collective-permute-start(bf16[336,256]{1,0:T(8,128)(2,1)S(1)} %get-tuple-element.21), channel_id=1, source_target_pairs={{0,24},{8,16},{16,8},{24,0},{1,25},{9,17},{17,9},{25,1},{2,26},{10... | collective-permute-start | bytes 516104 | tf_op jit(solution)/shard_map/ppermute | solution.py:491
  21.0 8.4 %collective-permute-start.8 = (bf16[336,256]{1,0:T(8,128)(2,1)S(1)}, bf16[336,256]{1,0:T(8,128)(2,1)S(1)}, u32[]{:S(2)}, u32[]{:S(2)}) collective-permute-start(bf16[336,256]{1,0:T(8,128)(2,1)S(1)} %get-tuple-element.22), channel_id=1, source_target_pairs={{0,16},{8,24},{16,0},{24,8},{1,17},{9,25},{17,1},{25,9},{2,18},{10... | collective-permute-start | bytes 516104 | tf_op jit(solution)/shard_map/ppermute | solution.py:491
  21.5 8.2 %collective-permute-start.9 = (bf16[336,256]{1,0:T(8,128)(2,1)S(1)}, bf16[336,256]{1,0:T(8,128)(2,1)S(1)}, u32[]{:S(2)}, u32[]{:S(2)}) collective-permute-start(bf16[336,256]{1,0:T(8,128)(2,1)S(1)} %get-tuple-element.23), channel_id=1, source_target_pairs={{0,8},{8,0},{16,24},{24,16},{1,9},{9,1},{17,25},{25,17},{2,10},{10... | collective-permute-start | bytes 516104 | tf_op jit(solution)/shard_map/ppermute | solution.py:491
  29.8 1.4 %collective-permute-start.10 = (bf16[272,256]{1,0:T(8,128)(2,1)S(1)}, bf16[272,256]{1,0:T(8,128)(2,1)S(1)}, u32[]{:S(2)}, u32[]{:S(2)}) collective-permute-start(bf16[272,256]{1,0:T(8,128)(2,1)S(1)} %add_convert_fusion.refs_0_), channel_id=1, source_target_pairs={{0,1},{1,0},{2,3},{3,2},{4,5},{5,4},{6,7},{7,6},{8,9},{9,8},{10,11... | collective-permute-start | bytes 417800 | tf_op jit(solution)/shard_map/ppermute | solution.py:488

commit v5 on v4

--- a/solution.py
+++ b/solution.py
@@ -11,7 +11,7 @@
 F32 = jnp.float32
 BF16 = jnp.bfloat16
 LABEL_ROWS = 16
-TILE = 128
+TILE = 256
 
 
 OFFSETS = [
@@ -250,28 +250,38 @@
 
 
 def weights_kernel(first_ref, second_ref, out_ref, neck_ref, packed_ref, *refs):
-    first_in, second_in, first_t, second_t, joint, again, out_w, neck_w, sems = refs
+    first_in, second_in, first_t, second_t, joint, again, out_w, neck_w = refs[:8]
+    first_mid, second_mid, sems = refs[8:]
     small = [
         pltpu.make_async_copy(out_ref, out_w, sems.at[6]),
         pltpu.make_async_copy(neck_ref, neck_w, sems.at[7]),
     ]
     for copy in small:
         copy.start()
+    sets = (
+        (first_ref, first_in, first_mid, first_t),
+        (second_ref, second_in, second_mid, second_t),
+    )
     copies = []
-    for i, (src, dst) in enumerate(((first_ref, first_in), (second_ref, second_in))):
-        for a in range(3):
-            copies.append(pltpu.make_async_copy(src.at[a], dst.at[a], sems.at[3 * i + a]))
+    for i, (src, dst, mid, _) in enumerate(sets):
+        for a, place in enumerate((dst.at[0], mid, dst.at[3])):
+            copies.append(pltpu.make_async_copy(src.at[a], place, sems.at[3 * i + a]))
             copies[-1].start()
     again[...] = packed_ref[...]
     for copy in small:
         copy.wait()
     joint[...] = dot(out_w[...], neck_w[...]).astype(BF16)
-    for i, (src, dst) in enumerate(((first_in, first_t), (second_in, second_t))):
+    for i, (_, dst, mid, flipped) in enumerate(sets):
         for a in range(3):
             copies[3 * i + a].wait()
-            for b in range(3):
-                for e in range(3):
-                    dst[a, b, e] = src[a, b, e].T
+        for b in range(3):
+            for e in range(3):
+                taps = (dst[0, b, e], mid[b, e], dst[3, b, e])
+                for a in range(3):
+                    flipped[a, b, e] = taps[a].T
+                g0, g1, g2 = (tap.astype(F32) * 0.5 for tap in taps)
+                dst[1, b, e] = (g0 + g2 + g1).astype(BF16)
+                dst[2, b, e] = (g0 + g2 - g1).astype(BF16)
 
 
 def far_first(zs):
@@ -333,7 +343,7 @@
     nc, nt, ni, own_c, zs, tok_n, parts_n = sizes
     ours, theirs, r_ref, w1, w2, w1_t, w2_t, class_w, neck_w = refs[:9]
     parts = refs[9 : 9 + parts_n]
-    encoded_ref, loss_ref, grad_ref, grid, cols, slope1, grad2, cols3, hid1, hid2 = refs[9 + parts_n :]
+    encoded_ref, loss_ref, grad_ref, grid, cols, slope1, grad2, cols3, hid1, hid2, parts_out = refs[9 + parts_n :]
     channels = grid.shape[2]
     slab = nt * ni
     rows = nc * ni
@@ -349,36 +359,44 @@
 
     slope1[...] = jnp.zeros_like(slope1)
     grad2[...] = jnp.zeros_like(grad2)
-    edge = jnp.zeros((slab, taps * channels), BF16)
-    cols[0:slab, :] = edge
-    cols[(nc + 1) * slab :, :] = edge
-
-    def spread(value, c):
+    def spread(value, k, i):
         for e in range(3):
             moved = along_inline(value, e - 1, ni)
             for b in range(3):
                 lane = (b * 3 + e) * channels
-                cols[(c + 1) * slab : (c + 2) * slab, lane : lane + channels] = along_rows(
+                cols[k, i * slab : (i + 1) * slab, lane : lane + channels] = along_rows(
                     moved, (b - 1) * ni
                 ).astype(BF16)
 
+    def spread_all(volume):
+        empty = jnp.zeros((slab, channels), F32)
+        for i in range(nc // 2):
+            d0 = volume[2 * i - 1] if i > 0 else empty
+            d1, d2 = volume[2 * i], volume[2 * i + 1]
+            d3 = volume[2 * i + 2] if 2 * i + 2 < nc else empty
+            for k, value in enumerate((d0 - d2, d1 + d2, d2 - d1, d1 - d3)):
+                spread(value, k, i)
+
+    half_cells = cells // 2
+
     def conv(weights, out):
-        for m in range(0, cells, TILE):
-            total = None
-            for a in range(3):
-                matrix = weights[a].reshape(taps * channels, channels)
-                term = dot(cols[a * slab + m : a * slab + m + TILE, :], matrix)
-                total = term if total is None else total + term
-            out[m : m + TILE, :] = total
-
-    for c in range(nc):
-        spread(grid[c], c)
+        for k in range(4):
+            matrix = weights[k].reshape(taps * channels, channels)
+            for m in range(0, half_cells, TILE):
+                parts_out[k, m : m + TILE, :] = dot(cols[k, m : m + TILE, :], matrix)
+        for i in range(nc // 2):
+            m0, m1, m2, m3 = (parts_out[k, i * slab : (i + 1) * slab, :] for k in range(4))
+            out[2 * i * slab : (2 * i + 1) * slab, :] = m0 + m1 + m2
+            out[(2 * i + 1) * slab : (2 * i + 2) * slab, :] = m1 - m2 - m3
+
+    spread_all([grid[c] for c in range(nc)])
     conv(w1, hid1)
     for c in range(nc):
         v = hid1[c * slab : (c + 1) * slab, :]
         s = sigma_of(v)
         slope1[c + 1, ni : ni + slab, :] = s * (1.0 + v * (1.0 - s))
-        spread((v * s).astype(BF16).astype(F32), c)
+        grid[c] = (v * s).astype(BF16).astype(F32)
+    spread_all([grid[c] for c in range(nc)])
     conv(w2, hid2)
     hidden_two = hid2[...]
     sigma_two = sigma_of(hidden_two)
@@ -500,7 +518,8 @@
     kept = [pltpu.with_memory_space_constraint(w, pltpu.HBM) for w in (w_first, w_second, w_out, w_neck)]
     first_in, second_in, first_t, second_t, joint, again, out_w, neck_w = pl.pallas_call(
         weights_kernel,
-        out_shape=[pltpu.VMEM(w_first.shape, BF16)] * 4
+        out_shape=[pltpu.VMEM((4,) + w_first.shape[1:], BF16)] * 2
+        + [pltpu.VMEM(w_first.shape, BF16)] * 2
         + [
             pltpu.VMEM((width, channels), BF16),
             pltpu.VMEM(packed.shape, BF16),
@@ -509,7 +528,7 @@
         ],
         in_specs=[hbm()] * 4 + [vmem()],
         out_specs=[vmem()] * 8,
-        scratch_shapes=[pltpu.SemaphoreType.DMA((8,))],
+        scratch_shapes=[pltpu.VMEM(w_first.shape[1:], BF16)] * 2 + [pltpu.SemaphoreType.DMA((8,))],
         compiler_params=pltpu.CompilerParams(vmem_limit_bytes=24 * 2**20),
         cost_estimate=pl.CostEstimate(flops=0, bytes_accessed=28 * 2**20, transcendentals=0),
     )(*kept, packed)
@@ -548,12 +567,13 @@
             out_specs=[vmem()] * 3,
             scratch_shapes=[
                 pltpu.VMEM((nc, slab, channels), F32),
-                pltpu.VMEM(((nc + 2) * slab, 9 * channels), BF16),
+                pltpu.VMEM((4, nc // 2 * slab, 9 * channels), BF16),
                 pltpu.VMEM((nc + 2, (nt + 4) * ni, channels), F32),
                 pltpu.VMEM((nc + 4, (nt + 6) * ni, channels), F32),
                 pltpu.VMEM(((own_c + 4) * 4 * ni, 9 * channels), BF16),
                 pltpu.VMEM((nc * slab, channels), F32),
                 pltpu.VMEM((nc * slab, channels), F32),
+                pltpu.VMEM((4, nc // 2 * slab, channels), F32),
             ],
             compiler_params=pltpu.CompilerParams(vmem_limit_bytes=36 * 2**20),
         )(half, other, residual, first_in, second_in, first_t, second_t, w_class, neck_w, *parts)
@@ -579,7 +599,8 @@
         and power_of_two(heads_n)
         and residual.shape[0] * heads_n == nc
         and nc * nt * ni <= 1024
-        and (nc * nt * ni) % TILE == 0
+        and (nc // 2 * nt * ni) % TILE == 0
+        and nc % 2 == 0
         and width % 128 == 0
         and w_neck.shape[1] == width
         and (residual.shape[0] * ni) % 16 == 0

time: 38.7 us -> 37.9 us (0.979)
  waiting for transfers between devices: 14 us -> 13.1 us
    ppermute x8, waiting for transfers between devices: 6.05 us -> 5.17 us  [swap_tok(): return lax.ppermute(value, 'tok', [(i, i ^ bits) for i in range(tok_n)])]
    pallas_call x1, Pallas kernels: 3.82 us -> 4.7 us  [whole_grid(): pl.pallas_call(weights_kernel, out_shape=[pltpu.VMEM((4,) + w_first.shape...]
    pallas_call x1, Pallas kernels: 7.33 us -> 6.54 us  [whole_grid(): pl.pallas_call(functools.partial(decoder_kernel, (nc, nt, ni, own_c, zs,...]
  transfers between devices with their start and end apart: 11 -> 11, of which waited for: 8 -> 8; matrix products, arithmetic and copies ran while one was open for 0% -> 0% of each run, Pallas kernels for 10% -> 12%
where the time goes in v5:
time: 37.9 us; the launch traced here: 37.8 us
  Pallas kernels  13.9 us (37%)
  waiting for transfers between devices  13.1 us (35%)
  starting transfers between devices  9.96 us (26%)
  between operations  0.7 us (2%)
    ppermute x3, waiting for transfers between devices, swap_heads(): return lax.ppermute(value, 'heads', [(i, i ^ bits) for i in range(heads_n)])  7.98 us
    pallas_call x1, Pallas kernels, whole_grid(): pl.pallas_call(functools.partial(decoder_kernel, (nc, nt, ni, own_c, zs,...  6.54 us
    ppermute x8, starting transfers between devices, swap_tok(): return lax.ppermute(value, 'tok', [(i, i ^ bits) for i in range(tok_n)])  6.4 us
    ppermute x8, waiting for transfers between devices, swap_tok(): return lax.ppermute(value, 'tok', [(i, i ^ bits) for i in range(tok_n)])  5.17 us
    pallas_call x1, Pallas kernels, whole_grid(): pl.pallas_call(weights_kernel, out_shape=[pltpu.VMEM((4,) + w_first.shape...  4.7 us
    ppermute x3, starting transfers between devices, swap_heads(): return lax.ppermute(value, 'heads', [(i, i ^ bits) for i in range(heads_n)])  3.55 us
    pallas_call x1, Pallas kernels, whole_grid(): pl.pallas_call(functools.partial(pack_kernel, tok_n), out_shape=pltpu.VME...  1.32 us
    pallas_call x1, Pallas kernels, whole_grid(): pl.pallas_call(functools.partial(attention_kernel, tok_n, zs, rows, own),...  1.3 us
  transfers between devices with their start and end apart: 11, of which 8 were waited for; matrix products, arithmetic and copies ran while one was open for 0% of the time, Pallas kernels for 12%

profile of v5, /device:TPU:0, one launch (start us, length us, event | category | flops | bytes accessed | tf_op | source)
XLA Modules:
  0.0 37.8 jit_solution(5549504647368062596)
XLA Ops:
  0.6 1.3 %shard_map.121.packed_ref.refs_0_ = bf16[224,256]{1,0:T(8,128)(2,1)S(1)} custom-call(bf16[1,8,8,256]{3,2,1,0:T(8,128)(2,1)} %q_ref.1, bf16[1,8,8,256]{3,2,1,0:T(8,128)(2,1)} %k_ref.1, bf16[1,8,8,256]{3,2,1,0:T(8,128)(2,1)} %v_ref.1, bf16[2,1,8,1024]{3,2,1,0:T(8,128)(2,1)} %refs_2_.1, bf16[1024,256]{1,0:T(8,128)(2,1)} %neck_ref.3, s32[2,1,8]{2,1,0:T(1,128)} %bitcast.5), custom_call_target="tpu_custom_call" | custom-call | tf_op jit(solution)/shard_map/pallas_call | solution.py:511
  2.0 0.0 copy-start
  2.0 0.0 copy-start.1
  2.0 4.1 %collective-permute-start.2 = (bf16[224,256]{1,0:T(8,128)(2,1)S(1)}, bf16[224,256]{1,0:T(8,128)(2,1)S(1)}, u32[]{:S(2)}, u32[]{:S(2)}) collective-permute-start(bf16[224,256]{1,0:T(8,128)(2,1)S(1)} %shard_map.121.packed_ref.refs_0_), channel_id=1, source_target_pairs={{0,4},{1,5},{2,6},{3,7},{4,0},{5,1},{6,2},{7,3},{8,12},{9,13},{10,... | collective-permute-start | bytes 344072 | tf_op jit(solution)/shard_map/ppermute | solution.py:506
  6.1 1.3 %collective-permute-start.1 = (bf16[224,256]{1,0:T(8,128)(2,1)S(1)}, bf16[224,256]{1,0:T(8,128)(2,1)S(1)}, u32[]{:S(2)}, u32[]{:S(2)}) collective-permute-start(bf16[224,256]{1,0:T(8,128)(2,1)S(1)} %shard_map.121.packed_ref.refs_0_), channel_id=1, source_target_pairs={{0,6},{1,7},{2,4},{3,5},{4,2},{5,3},{6,0},{7,1},{8,14},{9,15},{10,... | collective-permute-start | bytes 344072 | tf_op jit(solution)/shard_map/ppermute | solution.py:506
  7.4 0.2 collective-permute-start
  7.7 4.7 %shard_map.122 = (bf16[4,3,3,256,256]{4,3,2,1,0:T(8,128)(2,1)S(1)}, bf16[4,3,3,256,256]{4,3,2,1,0:T(8,128)(2,1)S(1)}, bf16[3,3,3,256,256]{4,3,2,1,0:T(8,128)(2,1...) custom-call(bf16[3,3,3,256,256]{4,3,2,1,0:T(8,128)(2,1)} %first_ref., ...), custom_call_target="tpu_custom_call" | custom-call | bytes 29360128 | tf_op jit(solution)/shard_map/pallas_call | solution.py:519
  12.4 0.1 collective-permute-start.3
  12.5 2.6 %collective-permute-done.2.refs_3_ = bf16[224,256]{1,0:T(8,128)(2,1)S(1)} collective-permute-done((bf16[224,256]{1,0:T(8,128)(2,1)S(1)}, bf16[224,256]{1,0:T(8,128)(2,1)S(1)}, u32[]{:S(2)}, u32[]{:S(2)}) %collective-permute-start.2) | collective-permute-done | bytes 114720 | tf_op jit(solution)/shard_map/ppermute | solution.py:506
  15.0 0.0 collective-permute-start.6
  15.0 0.0 collective-permute-done.1.refs_2_
  15.0 0.5 %collective-permute-start.5 = (bf16[224,256]{1,0:T(8,128)(2,1)S(1)}, bf16[224,256]{1,0:T(8,128)(2,1)S(1)}, u32[]{:S(2)}, u32[]{:S(2)}) collective-permute-start(bf16[224,256]{1,0:T(8,128)(2,1)S(1)} %collective-permute-done.1.refs_2_), channel_id=1, source_target_pairs={{0,1},{1,0},{2,3},{3,2},{4,5},{5,4},{6,7},{7,6},{8,9},{9,8},{10,11... | collective-permute-start | bytes 344072 | tf_op jit(solution)/shard_map/ppermute | solution.py:506
  15.5 0.0 collective-permute-done.refs_1_
  15.5 0.1 collective-permute-start.4
  15.6 0.0 collective-permute-done.3.refs_4_
  15.6 0.7 %collective-permute-done.6.refs_7_ = bf16[224,256]{1,0:T(8,128)(2,1)S(1)} collective-permute-done((bf16[224,256]{1,0:T(8,128)(2,1)S(1)}, bf16[224,256]{1,0:T(8,128)(2,1)S(1)}, u32[]{:S(2)}, u32[]{:S(2)}) %collective-permute-start.6) | collective-permute-done | bytes 114720 | tf_op jit(solution)/shard_map/ppermute | solution.py:506
  16.3 0.2 collective-permute-done.5.refs_6_
  16.5 0.4 collective-permute-done.4.refs_5_
  16.9 1.3 %shard_map.123 = (bf16[336,256]{1,0:T(8,128)(2,1)S(1)}, bf16[336,256]{1,0:T(8,128)(2,1)S(1)}, bf16[336,256]{1,0:T(8,128)(2,1)S(1)}, bf16[336,256]{1,0:T(8,128)(2,1)S(1)}) custom-call(bf16[224,256]{1,0:T(8,128)(2,1)S(1)} %shard_map.121.packed_ref.refs_0_, bf16[224,256]{1,0:T(8,128)(2,1)S(1)} %collective-permute-done.refs_1_, ...), custom_call_target="tpu_custom_call" | custom-call | tf_op jit(solution)/shard_map/pallas_call | solution.py:540
  18.2 2.9 %collective-permute-start.7 = (bf16[336,256]{1,0:T(8,128)(2,1)S(1)}, bf16[336,256]{1,0:T(8,128)(2,1)S(1)}, u32[]{:S(2)}, u32[]{:S(2)}) collective-permute-start(bf16[336,256]{1,0:T(8,128)(2,1)S(1)} %get-tuple-element.21), channel_id=1, source_target_pairs={{0,24},{8,16},{16,8},{24,0},{1,25},{9,17},{17,9},{25,1},{2,26},{10... | collective-permute-start | bytes 516104 | tf_op jit(solution)/shard_map/ppermute | solution.py:509
  21.0 0.5 %collective-permute-start.8 = (bf16[336,256]{1,0:T(8,128)(2,1)S(1)}, bf16[336,256]{1,0:T(8,128)(2,1)S(1)}, u32[]{:S(2)}, u32[]{:S(2)}) collective-permute-start(bf16[336,256]{1,0:T(8,128)(2,1)S(1)} %get-tuple-element.22), channel_id=1, source_target_pairs={{0,16},{8,24},{16,0},{24,8},{1,17},{9,25},{17,1},{25,9},{2,18},{10... | collective-permute-start | bytes 516104 | tf_op jit(solution)/shard_map/ppermute | solution.py:509
  21.5 0.2 collective-permute-start.9
  21.7 4.6 %collective-permute-done.7.refs_9_ = bf16[336,256]{1,0:T(8,128)(2,1)S(1)} collective-permute-done((bf16[336,256]{1,0:T(8,128)(2,1)S(1)}, bf16[336,256]{1,0:T(8,128)(2,1)S(1)}, u32[]{:S(2)}, u32[]{:S(2)}) %collective-permute-start.7) | collective-permute-done | bytes 172064 | tf_op jit(solution)/shard_map/ppermute | solution.py:509
  26.3 3.1 %collective-permute-done.8.refs_10_ = bf16[336,256]{1,0:T(8,128)(2,1)S(1)} collective-permute-done((bf16[336,256]{1,0:T(8,128)(2,1)S(1)}, bf16[336,256]{1,0:T(8,128)(2,1)S(1)}, u32[]{:S(2)}, u32[]{:S(2)}) %collective-permute-start.8) | collective-permute-done | bytes 172064 | tf_op jit(solution)/shard_map/ppermute | solution.py:509
  29.4 0.3 collective-permute-done.9.refs_11_
  29.7 0.1 add_convert_fusion.refs_0_
  29.8 0.1 collective-permute-start.10
  29.9 1.3 %collective-permute-done.10.refs_1_ = bf16[272,256]{1,0:T(8,128)(2,1)S(1)} collective-permute-done((bf16[272,256]{1,0:T(8,128)(2,1)S(1)}, bf16[272,256]{1,0:T(8,128)(2,1)S(1)}, u32[]{:S(2)}, u32[]{:S(2)}) %collective-permute-start.10) | collective-permute-done | bytes 139296 | tf_op jit(solution)/shard_map/ppermute | solution.py:506
  31.2 0.0 copy-done
  31.2 0.0 copy-done.1
  31.2 6.5 %shard_map.124 = (bf16[2,1,8,1024]{3,2,1,0:T(8,128)(2,1)}, f32[1,128]{1,0:T(1,128)}, bf16[2,1,8,1024]{3,2,1,0:T(8,128)(2,1)}) custom-call(bf16[272,256]{1,0:T(8,128)(2,1)S(1)} %add_convert_fusion.refs_0_, bf16[272,256]{1,0:T(8,128)(2,1)S(1)} %collective-permute-done.10.refs_1_, bf16[2,1,8,1024]{3,2,1,0:T(8,128)(2,1)S(1)} %copy-done, ...), custom_call_target="tpu_custom_call" | custom-call | tf_op jit(solution)/shard_map/pallas_call | solution.py:559
Async XLA Ops:
  2.0 29.3 %copy-start = (bf16[2,1,8,1024]{3,2,1,0:T(8,128)(2,1)S(1)}, bf16[2,1,8,1024]{3,2,1,0:T(8,128)(2,1)}, u32[]{:S(2)}) copy-start(bf16[2,1,8,1024]{3,2,1,0:T(8,128)(2,1)} %refs_2_.1) | copy-start | bytes 98308
  2.0 29.2 %copy-start.1 = (bf16[256]{0:T(256)(128)(2,1)S(1)}, bf16[256]{0:T(256)(128)(2,1)}, u32[]{:S(2)}) copy-start(bf16[256]{0:T(256)(128)(2,1)} %refs_7_.1) | copy-start | bytes 1540
  2.0 13.0 %collective-permute-start.2 = (bf16[224,256]{1,0:T(8,128)(2,1)S(1)}, bf16[224,256]{1,0:T(8,128)(2,1)S(1)}, u32[]{:S(2)}, u32[]{:S(2)}) collective-permute-start(bf16[224,256]{1,0:T(8,128)(2,1)S(1)} %shard_map.121.packed_ref.refs_0_), channel_id=1, source_target_pairs={{0,4},{1,5},{2,6},{3,7},{4,0},{5,1},{6,2},{7,3},{8,12},{9,13},{10,... | collective-permute-start | bytes 344072 | tf_op jit(solution)/shard_map/ppermute | solution.py:506
  6.1 8.9 %collective-permute-start.1 = (bf16[224,256]{1,0:T(8,128)(2,1)S(1)}, bf16[224,256]{1,0:T(8,128)(2,1)S(1)}, u32[]{:S(2)}, u32[]{:S(2)}) collective-permute-start(bf16[224,256]{1,0:T(8,128)(2,1)S(1)} %shard_map.121.packed_ref.refs_0_), channel_id=1, source_target_pairs={{0,6},{1,7},{2,4},{3,5},{4,2},{5,3},{6,0},{7,1},{8,14},{9,15},{10,... | collective-permute-start | bytes 344072 | tf_op jit(solution)/shard_map/ppermute | solution.py:506
  7.4 8.1 %collective-permute-start = (bf16[224,256]{1,0:T(8,128)(2,1)S(1)}, bf16[224,256]{1,0:T(8,128)(2,1)S(1)}, u32[]{:S(2)}, u32[]{:S(2)}) collective-permute-start(bf16[224,256]{1,0:T(8,128)(2,1)S(1)} %shard_map.121.packed_ref.refs_0_), channel_id=1, source_target_pairs={{0,2},{1,3},{2,0},{3,1},{4,6},{5,7},{6,4},{7,5},{8,10},{9,11},{10,... | collective-permute-start | bytes 344072 | tf_op jit(solution)/shard_map/ppermute | solution.py:506
  12.4 3.2 %collective-permute-start.3 = (bf16[224,256]{1,0:T(8,128)(2,1)S(1)}, bf16[224,256]{1,0:T(8,128)(2,1)S(1)}, u32[]{:S(2)}, u32[]{:S(2)}) collective-permute-start(bf16[224,256]{1,0:T(8,128)(2,1)S(1)} %get-tuple-element.18), channel_id=1, source_target_pairs={{0,1},{1,0},{2,3},{3,2},{4,5},{5,4},{6,7},{7,6},{8,9},{9,8},{10,11... | collective-permute-start | bytes 344072 | tf_op jit(solution)/shard_map/ppermute | solution.py:506
  15.0 1.3 %collective-permute-start.6 = (bf16[224,256]{1,0:T(8,128)(2,1)S(1)}, bf16[224,256]{1,0:T(8,128)(2,1)S(1)}, u32[]{:S(2)}, u32[]{:S(2)}) collective-permute-start(bf16[224,256]{1,0:T(8,128)(2,1)S(1)} %collective-permute-done.2.refs_3_), channel_id=1, source_target_pairs={{0,1},{1,0},{2,3},{3,2},{4,5},{5,4},{6,7},{7,6},{8,9},{9,8},{10,11... | collective-permute-start | bytes 344072 | tf_op jit(solution)/shard_map/ppermute | solution.py:506
  15.0 1.5 %collective-permute-start.5 = (bf16[224,256]{1,0:T(8,128)(2,1)S(1)}, bf16[224,256]{1,0:T(8,128)(2,1)S(1)}, u32[]{:S(2)}, u32[]{:S(2)}) collective-permute-start(bf16[224,256]{1,0:T(8,128)(2,1)S(1)} %collective-permute-done.1.refs_2_), channel_id=1, source_target_pairs={{0,1},{1,0},{2,3},{3,2},{4,5},{5,4},{6,7},{7,6},{8,9},{9,8},{10,11... | collective-permute-start | bytes 344072 | tf_op jit(solution)/shard_map/ppermute | solution.py:506
  15.5 1.3 %collective-permute-start.4 = (bf16[224,256]{1,0:T(8,128)(2,1)S(1)}, bf16[224,256]{1,0:T(8,128)(2,1)S(1)}, u32[]{:S(2)}, u32[]{:S(2)}) collective-permute-start(bf16[224,256]{1,0:T(8,128)(2,1)S(1)} %collective-permute-done.refs_1_), channel_id=1, source_target_pairs={{0,1},{1,0},{2,3},{3,2},{4,5},{5,4},{6,7},{7,6},{8,9},{9,8},{10,11... | collective-permute-start | bytes 344072 | tf_op jit(solution)/shard_map/ppermute | solution.py:506
  18.2 8.2 %collective-permute-start.7 = (bf16[336,256]{1,0:T(8,128)(2,1)S(1)}, bf16[336,256]{1,0:T(8,128)(2,1)S(1)}, u32[]{:S(2)}, u32[]{:S(2)}) collective-permute-start(bf16[336,256]{1,0:T(8,128)(2,1)S(1)} %get-tuple-element.21), channel_id=1, source_target_pairs={{0,24},{8,16},{16,8},{24,0},{1,25},{9,17},{17,9},{25,1},{2,26},{10... | collective-permute-start | bytes 516104 | tf_op jit(solution)/shard_map/ppermute | solution.py:509
  21.0 8.4 %collective-permute-start.8 = (bf16[336,256]{1,0:T(8,128)(2,1)S(1)}, bf16[336,256]{1,0:T(8,128)(2,1)S(1)}, u32[]{:S(2)}, u32[]{:S(2)}) collective-permute-start(bf16[336,256]{1,0:T(8,128)(2,1)S(1)} %get-tuple-element.22), channel_id=1, source_target_pairs={{0,16},{8,24},{16,0},{24,8},{1,17},{9,25},{17,1},{25,9},{2,18},{10... | collective-permute-start | bytes 516104 | tf_op jit(solution)/shard_map/ppermute | solution.py:509
  21.5 8.2 %collective-permute-start.9 = (bf16[336,256]{1,0:T(8,128)(2,1)S(1)}, bf16[336,256]{1,0:T(8,128)(2,1)S(1)}, u32[]{:S(2)}, u32[]{:S(2)}) collective-permute-start(bf16[336,256]{1,0:T(8,128)(2,1)S(1)} %get-tuple-element.23), channel_id=1, source_target_pairs={{0,8},{8,0},{16,24},{24,16},{1,9},{9,1},{17,25},{25,17},{2,10},{10... | collective-permute-start | bytes 516104 | tf_op jit(solution)/shard_map/ppermute | solution.py:509
  29.8 1.4 %collective-permute-start.10 = (bf16[272,256]{1,0:T(8,128)(2,1)S(1)}, bf16[272,256]{1,0:T(8,128)(2,1)S(1)}, u32[]{:S(2)}, u32[]{:S(2)}) collective-permute-start(bf16[272,256]{1,0:T(8,128)(2,1)S(1)} %add_convert_fusion.refs_0_), channel_id=1, source_target_pairs={{0,1},{1,0},{2,3},{3,2},{4,5},{5,4},{6,7},{7,6},{8,9},{9,8},{10,11... | collective-permute-start | bytes 417800 | tf_op jit(solution)/shard_map/ppermute | solution.py:506

commit v6 on v5

--- a/solution.py
+++ b/solution.py
@@ -10,7 +10,7 @@
 HD = 64
 F32 = jnp.float32
 BF16 = jnp.bfloat16
-LABEL_ROWS = 16
+LABEL_ROWS = 8
 TILE = 256
 
 
@@ -330,13 +330,13 @@
     blocks = [first[i * own : (i + 1) * own, :] for i in range(rows // own)]
     for d, ref in enumerate(part_refs):
         ref[0:queries_n, :] = partial
-        ref[queries_n : queries_n + LABEL_ROWS, :] = labels
         picked = blocks[0]
         for i in range(1, len(blocks)):
             picked = jnp.where((h ^ d) == i, blocks[i], picked)
         for i in range(picked.shape[1] // width):
-            at = queries_n + LABEL_ROWS + i * own
+            at = queries_n + i * own
             ref[at : at + own, :] = picked[:, i * width : (i + 1) * width].astype(BF16)
+        ref[ref.shape[0] - LABEL_ROWS :, :] = labels
 
 
 def decoder_kernel(sizes, *refs):
@@ -404,7 +404,8 @@
     class_row = class_w[...].astype(F32).reshape(1, channels)
     logits = dot_t(active_two, jnp.broadcast_to(class_row, (128, channels)).astype(BF16))
     probability = sigma_of(logits)
-    lab = ours[rows * zs : rows * zs + ni, 0:128].astype(F32)
+    last = parts[0].shape[0] - LABEL_ROWS
+    lab = pairwise([ref[last : last + ni, 0:128].astype(F32) for ref in parts])
     spread_lab = jnp.broadcast_to(lab[None], (cells // ni, ni, 128)).reshape(cells, 128)
     wanted = iota((cells, 128), 0) // ni
     picked = jnp.where(iota((cells, 128), 1) == wanted, spread_lab, 0.0).astype(BF16)
@@ -469,7 +470,7 @@
 
     own = own_c * ni
     width = parts[0].shape[1]
-    base = rows * zs + LABEL_ROWS
+    base = rows * zs
     for i in range(r_ref.shape[3] // width):
         terms = [ref[base + i * own : base + (i + 1) * own, :].astype(F32) for ref in parts]
         total = pairwise(terms).reshape(own_c, 1, ni, width)
@@ -551,8 +552,7 @@
         compiler_params=pltpu.CompilerParams(vmem_limit_bytes=16 * 2**20),
     )(*[ours[d] for d in order], *[theirs[d] for d in order], out_w, joint)
     parts = [swap_heads(sent[d], d) for d in range(heads_n - 1, 0, -1)] + [sent[0]]
-    used = queries_n + LABEL_ROWS
-    half = pairwise([part[:used].astype(F32) for part in parts]).astype(BF16)
+    half = pairwise([part[:queries_n].astype(F32) for part in parts]).astype(BF16)
     other = swap_tok(half, 1)
     slab = nt * ni
     return tuple(
@@ -592,7 +592,7 @@
         slabs == 1
         and nc * nt <= 128
         and labels.shape[2] == 1
-        and ni == 8
+        and ni == LABEL_ROWS
         and nt == tok_n
         and tok_n >= 4
         and power_of_two(tok_n)

time: 37.9 us -> 37.4 us (0.987)
  waiting for transfers between devices: 13.1 us -> 12.7 us
  transfers between devices with their start and end apart: 11 -> 11, of which waited for: 8 -> 8; matrix products, arithmetic and copies ran while one was open for 0% -> 0% of each run, Pallas kernels for 12% -> 13%
where the time goes in v6:
time: 37.4 us; the launch traced here: 37.3 us
  Pallas kernels  13.9 us (37%)
  waiting for transfers between devices  12.7 us (34%)
  starting transfers between devices  9.96 us (27%)
  between operations  0.7 us (2%)
    ppermute x3, waiting for transfers between devices, swap_heads(): return lax.ppermute(value, 'heads', [(i, i ^ bits) for i in range(heads_n)])  7.8 us
    pallas_call x1, Pallas kernels, whole_grid(): pl.pallas_call(functools.partial(decoder_kernel, (nc, nt, ni, own_c, zs,...  6.53 us
    ppermute x8, starting transfers between devices, swap_tok(): return lax.ppermute(value, 'tok', [(i, i ^ bits) for i in range(tok_n)])  6.4 us
    ppermute x8, waiting for transfers between devices, swap_tok(): return lax.ppermute(value, 'tok', [(i, i ^ bits) for i in range(tok_n)])  4.89 us
    pallas_call x1, Pallas kernels, whole_grid(): pl.pallas_call(weights_kernel, out_shape=[pltpu.VMEM((4,) + w_first.shape...  4.7 us
    ppermute x3, starting transfers between devices, swap_heads(): return lax.ppermute(value, 'heads', [(i, i ^ bits) for i in range(heads_n)])  3.55 us
    pallas_call x1, Pallas kernels, whole_grid(): pl.pallas_call(functools.partial(pack_kernel, tok_n), out_shape=pltpu.VME...  1.31 us
    pallas_call x1, Pallas kernels, whole_grid(): pl.pallas_call(functools.partial(attention_kernel, tok_n, zs, rows, own),...  1.31 us
  transfers between devices with their start and end apart: 11, of which 8 were waited for; matrix products, arithmetic and copies ran while one was open for 0% of the time, Pallas kernels for 13%

profile of v6, /device:TPU:0, one launch (start us, length us, event | category | flops | bytes accessed | tf_op | source)
XLA Modules:
  0.0 37.3 jit_solution(17133429838816913953)
XLA Ops:
  0.6 1.3 %shard_map.121.packed_ref.refs_0_ = bf16[216,256]{1,0:T(8,128)(2,1)S(1)} custom-call(bf16[1,8,8,256]{3,2,1,0:T(8,128)(2,1)} %q_ref.1, bf16[1,8,8,256]{3,2,1,0:T(8,128)(2,1)} %k_ref.1, bf16[1,8,8,256]{3,2,1,0:T(8,128)(2,1)} %v_ref.1, bf16[2,1,8,1024]{3,2,1,0:T(8,128)(2,1)} %refs_2_.1, bf16[1024,256]{1,0:T(8,128)(2,1)} %neck_ref.3, s32[2,1,8]{2,1,0:T(1,128)} %bitcast.5), custom_call_target="tpu_custom_call" | custom-call | tf_op jit(solution)/shard_map/pallas_call | solution.py:512
  2.0 0.0 copy-start
  2.0 0.0 copy-start.1
  2.0 4.1 %collective-permute-start.2 = (bf16[216,256]{1,0:T(8,128)(2,1)S(1)}, bf16[216,256]{1,0:T(8,128)(2,1)S(1)}, u32[]{:S(2)}, u32[]{:S(2)}) collective-permute-start(bf16[216,256]{1,0:T(8,128)(2,1)S(1)} %shard_map.121.packed_ref.refs_0_), channel_id=1, source_target_pairs={{0,4},{1,5},{2,6},{3,7},{4,0},{5,1},{6,2},{7,3},{8,12},{9,13},{10,... | collective-permute-start | bytes 331784 | tf_op jit(solution)/shard_map/ppermute | solution.py:507
  6.1 1.3 %collective-permute-start.1 = (bf16[216,256]{1,0:T(8,128)(2,1)S(1)}, bf16[216,256]{1,0:T(8,128)(2,1)S(1)}, u32[]{:S(2)}, u32[]{:S(2)}) collective-permute-start(bf16[216,256]{1,0:T(8,128)(2,1)S(1)} %shard_map.121.packed_ref.refs_0_), channel_id=1, source_target_pairs={{0,6},{1,7},{2,4},{3,5},{4,2},{5,3},{6,0},{7,1},{8,14},{9,15},{10,... | collective-permute-start | bytes 331784 | tf_op jit(solution)/shard_map/ppermute | solution.py:507
  7.4 0.2 collective-permute-start
  7.7 4.7 %shard_map.122 = (bf16[4,3,3,256,256]{4,3,2,1,0:T(8,128)(2,1)S(1)}, bf16[4,3,3,256,256]{4,3,2,1,0:T(8,128)(2,1)S(1)}, bf16[3,3,3,256,256]{4,3,2,1,0:T(8,128)(2,1...) custom-call(bf16[3,3,3,256,256]{4,3,2,1,0:T(8,128)(2,1)} %first_ref., ...), custom_call_target="tpu_custom_call" | custom-call | bytes 29360128 | tf_op jit(solution)/shard_map/pallas_call | solution.py:520
  12.4 0.1 collective-permute-start.3
  12.5 2.3 %collective-permute-done.2.refs_3_ = bf16[216,256]{1,0:T(8,128)(2,1)S(1)} collective-permute-done((bf16[216,256]{1,0:T(8,128)(2,1)S(1)}, bf16[216,256]{1,0:T(8,128)(2,1)S(1)}, u32[]{:S(2)}, u32[]{:S(2)}) %collective-permute-start.2) | collective-permute-done | bytes 110624 | tf_op jit(solution)/shard_map/ppermute | solution.py:507
  14.8 0.0 collective-permute-start.6
  14.8 0.0 collective-permute-done.1.refs_2_
  14.8 0.5 %collective-permute-start.5 = (bf16[216,256]{1,0:T(8,128)(2,1)S(1)}, bf16[216,256]{1,0:T(8,128)(2,1)S(1)}, u32[]{:S(2)}, u32[]{:S(2)}) collective-permute-start(bf16[216,256]{1,0:T(8,128)(2,1)S(1)} %collective-permute-done.1.refs_2_), channel_id=1, source_target_pairs={{0,1},{1,0},{2,3},{3,2},{4,5},{5,4},{6,7},{7,6},{8,9},{9,8},{10,11... | collective-permute-start | bytes 331784 | tf_op jit(solution)/shard_map/ppermute | solution.py:507
  15.3 0.0 collective-permute-done.refs_1_
  15.3 0.1 collective-permute-start.4
  15.3 0.0 collective-permute-done.3.refs_4_
  15.3 0.7 %collective-permute-done.6.refs_7_ = bf16[216,256]{1,0:T(8,128)(2,1)S(1)} collective-permute-done((bf16[216,256]{1,0:T(8,128)(2,1)S(1)}, bf16[216,256]{1,0:T(8,128)(2,1)S(1)}, u32[]{:S(2)}, u32[]{:S(2)}) %collective-permute-start.6) | collective-permute-done | bytes 110624 | tf_op jit(solution)/shard_map/ppermute | solution.py:507
  16.1 0.2 collective-permute-done.5.refs_6_
  16.2 0.4 collective-permute-done.4.refs_5_
  16.6 1.3 %shard_map.123 = (bf16[328,256]{1,0:T(8,128)(2,1)S(1)}, bf16[328,256]{1,0:T(8,128)(2,1)S(1)}, bf16[328,256]{1,0:T(8,128)(2,1)S(1)}, bf16[328,256]{1,0:T(8,128)(2,1)S(1)}) custom-call(bf16[216,256]{1,0:T(8,128)(2,1)S(1)} %shard_map.121.packed_ref.refs_0_, bf16[216,256]{1,0:T(8,128)(2,1)S(1)} %collective-permute-done.refs_1_, ...), custom_call_target="tpu_custom_call" | custom-call | tf_op jit(solution)/shard_map/pallas_call | solution.py:541
  17.9 2.9 %collective-permute-start.7 = (bf16[328,256]{1,0:T(8,128)(2,1)S(1)}, bf16[328,256]{1,0:T(8,128)(2,1)S(1)}, u32[]{:S(2)}, u32[]{:S(2)}) collective-permute-start(bf16[328,256]{1,0:T(8,128)(2,1)S(1)} %get-tuple-element.21), channel_id=1, source_target_pairs={{0,24},{8,16},{16,8},{24,0},{1,25},{9,17},{17,9},{25,1},{2,26},{10... | collective-permute-start | bytes 503816 | tf_op jit(solution)/shard_map/ppermute | solution.py:510
  20.8 0.5 %collective-permute-start.8 = (bf16[328,256]{1,0:T(8,128)(2,1)S(1)}, bf16[328,256]{1,0:T(8,128)(2,1)S(1)}, u32[]{:S(2)}, u32[]{:S(2)}) collective-permute-start(bf16[328,256]{1,0:T(8,128)(2,1)S(1)} %get-tuple-element.22), channel_id=1, source_target_pairs={{0,16},{8,24},{16,0},{24,8},{1,17},{9,25},{17,1},{25,9},{2,18},{10... | collective-permute-start | bytes 503816 | tf_op jit(solution)/shard_map/ppermute | solution.py:510
  21.3 0.2 collective-permute-start.9
  21.5 4.5 %collective-permute-done.7.refs_9_ = bf16[328,256]{1,0:T(8,128)(2,1)S(1)} collective-permute-done((bf16[328,256]{1,0:T(8,128)(2,1)S(1)}, bf16[328,256]{1,0:T(8,128)(2,1)S(1)}, u32[]{:S(2)}, u32[]{:S(2)}) %collective-permute-start.7) | collective-permute-done | bytes 167968 | tf_op jit(solution)/shard_map/ppermute | solution.py:510
  26.0 3.0 %collective-permute-done.8.refs_10_ = bf16[328,256]{1,0:T(8,128)(2,1)S(1)} collective-permute-done((bf16[328,256]{1,0:T(8,128)(2,1)S(1)}, bf16[328,256]{1,0:T(8,128)(2,1)S(1)}, u32[]{:S(2)}, u32[]{:S(2)}) %collective-permute-start.8) | collective-permute-done | bytes 167968 | tf_op jit(solution)/shard_map/ppermute | solution.py:510
  29.0 0.3 collective-permute-done.9.refs_11_
  29.3 0.1 add_convert_fusion.refs_0_
  29.3 0.1 collective-permute-start.10
  29.4 1.3 %collective-permute-done.10.refs_1_ = bf16[256,256]{1,0:T(8,128)(2,1)S(1)} collective-permute-done((bf16[256,256]{1,0:T(8,128)(2,1)S(1)}, bf16[256,256]{1,0:T(8,128)(2,1)S(1)}, u32[]{:S(2)}, u32[]{:S(2)}) %collective-permute-start.10) | collective-permute-done | bytes 131104 | tf_op jit(solution)/shard_map/ppermute | solution.py:507
  30.7 0.0 copy-done
  30.7 0.0 copy-done.1
  30.8 6.5 %shard_map.124 = (bf16[2,1,8,1024]{3,2,1,0:T(8,128)(2,1)}, f32[1,128]{1,0:T(1,128)}, bf16[2,1,8,1024]{3,2,1,0:T(8,128)(2,1)}) custom-call(bf16[256,256]{1,0:T(8,128)(2,1)S(1)} %add_convert_fusion.refs_0_, bf16[256,256]{1,0:T(8,128)(2,1)S(1)} %collective-permute-done.10.refs_1_, bf16[2,1,8,1024]{3,2,1,0:T(8,128)(2,1)S(1)} %copy-done, ...), custom_call_target="tpu_custom_call" | custom-call | tf_op jit(solution)/shard_map/pallas_call | solution.py:559
Async XLA Ops:
  2.0 28.8 %copy-start = (bf16[2,1,8,1024]{3,2,1,0:T(8,128)(2,1)S(1)}, bf16[2,1,8,1024]{3,2,1,0:T(8,128)(2,1)}, u32[]{:S(2)}) copy-start(bf16[2,1,8,1024]{3,2,1,0:T(8,128)(2,1)} %refs_2_.1) | copy-start | bytes 98308
  2.0 28.8 %copy-start.1 = (bf16[256]{0:T(256)(128)(2,1)S(1)}, bf16[256]{0:T(256)(128)(2,1)}, u32[]{:S(2)}) copy-start(bf16[256]{0:T(256)(128)(2,1)} %refs_7_.1) | copy-start | bytes 1540
  2.0 12.8 %collective-permute-start.2 = (bf16[216,256]{1,0:T(8,128)(2,1)S(1)}, bf16[216,256]{1,0:T(8,128)(2,1)S(1)}, u32[]{:S(2)}, u32[]{:S(2)}) collective-permute-start(bf16[216,256]{1,0:T(8,128)(2,1)S(1)} %shard_map.121.packed_ref.refs_0_), channel_id=1, source_target_pairs={{0,4},{1,5},{2,6},{3,7},{4,0},{5,1},{6,2},{7,3},{8,12},{9,13},{10,... | collective-permute-start | bytes 331784 | tf_op jit(solution)/shard_map/ppermute | solution.py:507
  6.1 8.7 %collective-permute-start.1 = (bf16[216,256]{1,0:T(8,128)(2,1)S(1)}, bf16[216,256]{1,0:T(8,128)(2,1)S(1)}, u32[]{:S(2)}, u32[]{:S(2)}) collective-permute-start(bf16[216,256]{1,0:T(8,128)(2,1)S(1)} %shard_map.121.packed_ref.refs_0_), channel_id=1, source_target_pairs={{0,6},{1,7},{2,4},{3,5},{4,2},{5,3},{6,0},{7,1},{8,14},{9,15},{10,... | collective-permute-start | bytes 331784 | tf_op jit(solution)/shard_map/ppermute | solution.py:507
  7.4 7.8 %collective-permute-start = (bf16[216,256]{1,0:T(8,128)(2,1)S(1)}, bf16[216,256]{1,0:T(8,128)(2,1)S(1)}, u32[]{:S(2)}, u32[]{:S(2)}) collective-permute-start(bf16[216,256]{1,0:T(8,128)(2,1)S(1)} %shard_map.121.packed_ref.refs_0_), channel_id=1, source_target_pairs={{0,2},{1,3},{2,0},{3,1},{4,6},{5,7},{6,4},{7,5},{8,10},{9,11},{10,... | collective-permute-start | bytes 331784 | tf_op jit(solution)/shard_map/ppermute | solution.py:507
  12.4 3.0 %collective-permute-start.3 = (bf16[216,256]{1,0:T(8,128)(2,1)S(1)}, bf16[216,256]{1,0:T(8,128)(2,1)S(1)}, u32[]{:S(2)}, u32[]{:S(2)}) collective-permute-start(bf16[216,256]{1,0:T(8,128)(2,1)S(1)} %get-tuple-element.18), channel_id=1, source_target_pairs={{0,1},{1,0},{2,3},{3,2},{4,5},{5,4},{6,7},{7,6},{8,9},{9,8},{10,11... | collective-permute-start | bytes 331784 | tf_op jit(solution)/shard_map/ppermute | solution.py:507
  14.8 1.3 %collective-permute-start.6 = (bf16[216,256]{1,0:T(8,128)(2,1)S(1)}, bf16[216,256]{1,0:T(8,128)(2,1)S(1)}, u32[]{:S(2)}, u32[]{:S(2)}) collective-permute-start(bf16[216,256]{1,0:T(8,128)(2,1)S(1)} %collective-permute-done.2.refs_3_), channel_id=1, source_target_pairs={{0,1},{1,0},{2,3},{3,2},{4,5},{5,4},{6,7},{7,6},{8,9},{9,8},{10,11... | collective-permute-start | bytes 331784 | tf_op jit(solution)/shard_map/ppermute | solution.py:507
  14.8 1.5 %collective-permute-start.5 = (bf16[216,256]{1,0:T(8,128)(2,1)S(1)}, bf16[216,256]{1,0:T(8,128)(2,1)S(1)}, u32[]{:S(2)}, u32[]{:S(2)}) collective-permute-start(bf16[216,256]{1,0:T(8,128)(2,1)S(1)} %collective-permute-done.1.refs_2_), channel_id=1, source_target_pairs={{0,1},{1,0},{2,3},{3,2},{4,5},{5,4},{6,7},{7,6},{8,9},{9,8},{10,11... | collective-permute-start | bytes 331784 | tf_op jit(solution)/shard_map/ppermute | solution.py:507
  15.3 1.3 %collective-permute-start.4 = (bf16[216,256]{1,0:T(8,128)(2,1)S(1)}, bf16[216,256]{1,0:T(8,128)(2,1)S(1)}, u32[]{:S(2)}, u32[]{:S(2)}) collective-permute-start(bf16[216,256]{1,0:T(8,128)(2,1)S(1)} %collective-permute-done.refs_1_), channel_id=1, source_target_pairs={{0,1},{1,0},{2,3},{3,2},{4,5},{5,4},{6,7},{7,6},{8,9},{9,8},{10,11... | collective-permute-start | bytes 331784 | tf_op jit(solution)/shard_map/ppermute | solution.py:507
  17.9 8.1 %collective-permute-start.7 = (bf16[328,256]{1,0:T(8,128)(2,1)S(1)}, bf16[328,256]{1,0:T(8,128)(2,1)S(1)}, u32[]{:S(2)}, u32[]{:S(2)}) collective-permute-start(bf16[328,256]{1,0:T(8,128)(2,1)S(1)} %get-tuple-element.21), channel_id=1, source_target_pairs={{0,24},{8,16},{16,8},{24,0},{1,25},{9,17},{17,9},{25,1},{2,26},{10... | collective-permute-start | bytes 503816 | tf_op jit(solution)/shard_map/ppermute | solution.py:510
  20.8 8.2 %collective-permute-start.8 = (bf16[328,256]{1,0:T(8,128)(2,1)S(1)}, bf16[328,256]{1,0:T(8,128)(2,1)S(1)}, u32[]{:S(2)}, u32[]{:S(2)}) collective-permute-start(bf16[328,256]{1,0:T(8,128)(2,1)S(1)} %get-tuple-element.22), channel_id=1, source_target_pairs={{0,16},{8,24},{16,0},{24,8},{1,17},{9,25},{17,1},{25,9},{2,18},{10... | collective-permute-start | bytes 503816 | tf_op jit(solution)/shard_map/ppermute | solution.py:510
  21.3 8.0 %collective-permute-start.9 = (bf16[328,256]{1,0:T(8,128)(2,1)S(1)}, bf16[328,256]{1,0:T(8,128)(2,1)S(1)}, u32[]{:S(2)}, u32[]{:S(2)}) collective-permute-start(bf16[328,256]{1,0:T(8,128)(2,1)S(1)} %get-tuple-element.23), channel_id=1, source_target_pairs={{0,8},{8,0},{16,24},{24,16},{1,9},{9,1},{17,25},{25,17},{2,10},{10... | collective-permute-start | bytes 503816 | tf_op jit(solution)/shard_map/ppermute | solution.py:510
  29.3 1.4 %collective-permute-start.10 = (bf16[256,256]{1,0:T(8,128)(2,1)S(1)}, bf16[256,256]{1,0:T(8,128)(2,1)S(1)}, u32[]{:S(2)}, u32[]{:S(2)}) collective-permute-start(bf16[256,256]{1,0:T(8,128)(2,1)S(1)} %add_convert_fusion.refs_0_), channel_id=1, source_target_pairs={{0,1},{1,0},{2,3},{3,2},{4,5},{5,4},{6,7},{7,6},{8,9},{9,8},{10,11... | collective-permute-start | bytes 393224 | tf_op jit(solution)/shard_map/ppermute | solution.py:507

commit v7 on v6

--- a/solution.py
+++ b/solution.py
@@ -11,7 +11,7 @@
 F32 = jnp.float32
 BF16 = jnp.bfloat16
 LABEL_ROWS = 8
-TILE = 256
+TILE = 128
 
 
 OFFSETS = [
@@ -285,7 +285,7 @@
 
 
 def far_first(zs):
-    return [0, 1] + list(range(zs - 1, 1, -1))
+    return list(range(zs - 1, 2, -1)) + [1, 2, 0]
 
 
 def attention_kernel(tok_n, zs, rows, own, *refs):
@@ -343,7 +343,7 @@
     nc, nt, ni, own_c, zs, tok_n, parts_n = sizes
     ours, theirs, r_ref, w1, w2, w1_t, w2_t, class_w, neck_w = refs[:9]
     parts = refs[9 : 9 + parts_n]
-    encoded_ref, loss_ref, grad_ref, grid, cols, slope1, grad2, cols3, hid1, hid2, parts_out = refs[9 + parts_n :]
+    encoded_ref, loss_ref, grad_ref, grid, cols, slope1, grad2, cols3, slope2, act, parts_out = refs[9 + parts_n :]
     channels = grid.shape[2]
     slab = nt * ni
     rows = nc * ni
@@ -379,29 +379,33 @@
 
     half_cells = cells // 2
 
-    def conv(weights, out):
-        for k in range(4):
-            matrix = weights[k].reshape(taps * channels, channels)
-            for m in range(0, half_cells, TILE):
+    def conv(weights, finish):
+        for m in range(0, half_cells, TILE):
+            for k in range(4):
+                matrix = weights[k].reshape(taps * channels, channels)
                 parts_out[k, m : m + TILE, :] = dot(cols[k, m : m + TILE, :], matrix)
-        for i in range(nc // 2):
-            m0, m1, m2, m3 = (parts_out[k, i * slab : (i + 1) * slab, :] for k in range(4))
-            out[2 * i * slab : (2 * i + 1) * slab, :] = m0 + m1 + m2
-            out[(2 * i + 1) * slab : (2 * i + 2) * slab, :] = m1 - m2 - m3
-
-    spread_all([grid[c] for c in range(nc)])
-    conv(w1, hid1)
-    for c in range(nc):
-        v = hid1[c * slab : (c + 1) * slab, :]
+            for i in range(m // slab, (m + TILE) // slab):
+                m0, m1, m2, m3 = (parts_out[k, i * slab : (i + 1) * slab, :] for k in range(4))
+                finish(2 * i, m0 + m1 + m2)
+                finish(2 * i + 1, m1 - m2 - m3)
+
+    class_row = class_w[...].astype(F32).reshape(1, channels)
+
+    def finish_one(c, v):
         s = sigma_of(v)
         slope1[c + 1, ni : ni + slab, :] = s * (1.0 + v * (1.0 - s))
         grid[c] = (v * s).astype(BF16).astype(F32)
+
+    def finish_two(c, v):
+        s = sigma_of(v)
+        slope2[c * slab : (c + 1) * slab, :] = s * (1.0 + v * (1.0 - s)) * class_row
+        act[c * slab : (c + 1) * slab, :] = (v * s).astype(BF16)
+
     spread_all([grid[c] for c in range(nc)])
-    conv(w2, hid2)
-    hidden_two = hid2[...]
-    sigma_two = sigma_of(hidden_two)
-    active_two = (hidden_two * sigma_two).astype(BF16)
-    class_row = class_w[...].astype(F32).reshape(1, channels)
+    conv(w1, finish_one)
+    spread_all([grid[c] for c in range(nc)])
+    conv(w2, finish_two)
+    active_two = act[...]
     logits = dot_t(active_two, jnp.broadcast_to(class_row, (128, channels)).astype(BF16))
     probability = sigma_of(logits)
     last = parts[0].shape[0] - LABEL_ROWS
@@ -424,11 +428,10 @@
         * probability
         * (1.0 - probability)
     )
-    wide = jnp.concatenate([grad_logits] * (channels // 128), axis=1)
-    slope_two = sigma_two * (1.0 + hidden_two * (1.0 - sigma_two))
-    g2 = wide * class_row * slope_two
     for c in range(nc):
-        grad2[c + 2, 2 * ni : 2 * ni + slab, :] = g2[c * slab : (c + 1) * slab, :]
+        rows_c = slice(c * slab, (c + 1) * slab)
+        wide = jnp.concatenate([grad_logits[rows_c, :]] * (channels // 128), axis=1)
+        grad2[c + 2, 2 * ni : 2 * ni + slab, :] = wide * slope2[rows_c, :]
 
     band = 4 * ni
     c0 = h * own_c
@@ -572,7 +575,7 @@
                 pltpu.VMEM((nc + 4, (nt + 6) * ni, channels), F32),
                 pltpu.VMEM(((own_c + 4) * 4 * ni, 9 * channels), BF16),
                 pltpu.VMEM((nc * slab, channels), F32),
-                pltpu.VMEM((nc * slab, channels), F32),
+                pltpu.VMEM((nc * slab, channels), BF16),
                 pltpu.VMEM((4, nc // 2 * slab, channels), F32),
             ],
             compiler_params=pltpu.CompilerParams(vmem_limit_bytes=36 * 2**20),
@@ -594,7 +597,7 @@
         and labels.shape[2] == 1
         and ni == LABEL_ROWS
         and nt == tok_n
-        and tok_n >= 4
+        and tok_n >= 8
         and power_of_two(tok_n)
         and power_of_two(heads_n)
         and residual.shape[0] * heads_n == nc

time: 37.4 us -> 37.4 us (level)
  transfers between devices with their start and end apart: 11 -> 11, of which waited for: 8 -> 7; matrix products, arithmetic and copies ran while one was open for 0% -> 0% of each run, Pallas kernels for 13% -> 13%
where the time goes in v7:
time: 37.4 us; the launch traced here: 37.3 us
  Pallas kernels  13.9 us (37%)
  waiting for transfers between devices  12.6 us (34%)
  starting transfers between devices  10 us (27%)
  between operations  0.71 us (2%)
    ppermute x3, waiting for transfers between devices, swap_heads(): return lax.ppermute(value, 'heads', [(i, i ^ bits) for i in range(heads_n)])  7.85 us
    pallas_call x1, Pallas kernels, whole_grid(): pl.pallas_call(functools.partial(decoder_kernel, (nc, nt, ni, own_c, zs,...  6.56 us
    ppermute x8, starting transfers between devices, swap_tok(): return lax.ppermute(value, 'tok', [(i, i ^ bits) for i in range(tok_n)])  6.34 us
    ppermute x8, waiting for transfers between devices, swap_tok(): return lax.ppermute(value, 'tok', [(i, i ^ bits) for i in range(tok_n)])  4.71 us
    pallas_call x1, Pallas kernels, whole_grid(): pl.pallas_call(weights_kernel, out_shape=[pltpu.VMEM((4,) + w_first.shape...  4.71 us
    ppermute x3, starting transfers between devices, swap_heads(): return lax.ppermute(value, 'heads', [(i, i ^ bits) for i in range(heads_n)])  3.68 us
    pallas_call x1, Pallas kernels, whole_grid(): pl.pallas_call(functools.partial(pack_kernel, tok_n), out_shape=pltpu.VME...  1.31 us
    pallas_call x1, Pallas kernels, whole_grid(): pl.pallas_call(functools.partial(attention_kernel, tok_n, zs, rows, own),...  1.31 us
  transfers between devices with their start and end apart: 11, of which 7 were waited for; matrix products, arithmetic and copies ran while one was open for 0% of the time, Pallas kernels for 13%

profile of v7, /device:TPU:0, one launch (start us, length us, event | category | flops | bytes accessed | tf_op | source)
XLA Modules:
  0.0 37.3 jit_solution(11733574549566632982)
XLA Ops:
  0.6 1.3 %shard_map.121.packed_ref.refs_3_ = bf16[216,256]{1,0:T(8,128)(2,1)S(1)} custom-call(bf16[1,8,8,256]{3,2,1,0:T(8,128)(2,1)} %q_ref.1, bf16[1,8,8,256]{3,2,1,0:T(8,128)(2,1)} %k_ref.1, bf16[1,8,8,256]{3,2,1,0:T(8,128)(2,1)} %v_ref.1, bf16[2,1,8,1024]{3,2,1,0:T(8,128)(2,1)} %refs_2_.1, bf16[1024,256]{1,0:T(8,128)(2,1)} %neck_ref.3, s32[2,1,8]{2,1,0:T(1,128)} %bitcast.5), custom_call_target="tpu_custom_call" | custom-call | tf_op jit(solution)/shard_map/pallas_call | solution.py:515
  2.0 0.0 copy-start
  2.0 0.0 copy-start.1
  2.0 4.1 %collective-permute-start.2 = (bf16[216,256]{1,0:T(8,128)(2,1)S(1)}, bf16[216,256]{1,0:T(8,128)(2,1)S(1)}, u32[]{:S(2)}, u32[]{:S(2)}) collective-permute-start(bf16[216,256]{1,0:T(8,128)(2,1)S(1)} %shard_map.121.packed_ref.refs_3_), channel_id=1, source_target_pairs={{0,4},{1,5},{2,6},{3,7},{4,0},{5,1},{6,2},{7,3},{8,12},{9,13},{10,... | collective-permute-start | bytes 331784 | tf_op jit(solution)/shard_map/ppermute | solution.py:510
  6.1 1.6 %collective-permute-start.1 = (bf16[216,256]{1,0:T(8,128)(2,1)S(1)}, bf16[216,256]{1,0:T(8,128)(2,1)S(1)}, u32[]{:S(2)}, u32[]{:S(2)}) collective-permute-start(bf16[216,256]{1,0:T(8,128)(2,1)S(1)} %shard_map.121.packed_ref.refs_3_), channel_id=1, source_target_pairs={{0,2},{1,3},{2,0},{3,1},{4,6},{5,7},{6,4},{7,5},{8,10},{9,11},{10,... | collective-permute-start | bytes 331784 | tf_op jit(solution)/shard_map/ppermute | solution.py:510
  7.7 0.0 collective-permute-start
  7.7 4.7 %shard_map.122 = (bf16[4,3,3,256,256]{4,3,2,1,0:T(8,128)(2,1)S(1)}, bf16[4,3,3,256,256]{4,3,2,1,0:T(8,128)(2,1)S(1)}, bf16[3,3,3,256,256]{4,3,2,1,0:T(8,128)(2,1...) custom-call(bf16[3,3,3,256,256]{4,3,2,1,0:T(8,128)(2,1)} %first_ref., ...), custom_call_target="tpu_custom_call" | custom-call | bytes 29360128 | tf_op jit(solution)/shard_map/pallas_call | solution.py:523
  12.4 0.1 collective-permute-start.6
  12.5 0.7 %collective-permute-done.2.refs_2_ = bf16[216,256]{1,0:T(8,128)(2,1)S(1)} collective-permute-done((bf16[216,256]{1,0:T(8,128)(2,1)S(1)}, bf16[216,256]{1,0:T(8,128)(2,1)S(1)}, u32[]{:S(2)}, u32[]{:S(2)}) %collective-permute-start.2) | collective-permute-done | bytes 110624 | tf_op jit(solution)/shard_map/ppermute | solution.py:510
  13.2 0.0 collective-permute-start.5
  13.2 0.0 collective-permute-done.1.refs_1_
  13.2 0.5 %collective-permute-start.4 = (bf16[216,256]{1,0:T(8,128)(2,1)S(1)}, bf16[216,256]{1,0:T(8,128)(2,1)S(1)}, u32[]{:S(2)}, u32[]{:S(2)}) collective-permute-start(bf16[216,256]{1,0:T(8,128)(2,1)S(1)} %collective-permute-done.1.refs_1_), channel_id=1, source_target_pairs={{0,1},{1,0},{2,3},{3,2},{4,5},{5,4},{6,7},{7,6},{8,9},{9,8},{10,11... | collective-permute-start | bytes 331784 | tf_op jit(solution)/shard_map/ppermute | solution.py:510
  13.7 1.4 %collective-permute-done.refs_0_ = bf16[216,256]{1,0:T(8,128)(2,1)S(1)} collective-permute-done((bf16[216,256]{1,0:T(8,128)(2,1)S(1)}, bf16[216,256]{1,0:T(8,128)(2,1)S(1)}, u32[]{:S(2)}, u32[]{:S(2)}) %collective-permute-start) | collective-permute-done | bytes 110624 | tf_op jit(solution)/shard_map/ppermute | solution.py:510
  15.0 0.0 collective-permute-start.3
  15.0 0.0 collective-permute-done.6.refs_7_
  15.0 0.0 collective-permute-done.5.refs_6_
  15.1 0.0 collective-permute-done.4.refs_5_
  15.1 1.3 %collective-permute-done.3.refs_4_ = bf16[216,256]{1,0:T(8,128)(2,1)S(1)} collective-permute-done((bf16[216,256]{1,0:T(8,128)(2,1)S(1)}, bf16[216,256]{1,0:T(8,128)(2,1)S(1)}, u32[]{:S(2)}, u32[]{:S(2)}) %collective-permute-start.3) | collective-permute-done | bytes 110624 | tf_op jit(solution)/shard_map/ppermute | solution.py:510
  16.4 1.3 %shard_map.123 = (bf16[328,256]{1,0:T(8,128)(2,1)S(1)}, bf16[328,256]{1,0:T(8,128)(2,1)S(1)}, bf16[328,256]{1,0:T(8,128)(2,1)S(1)}, bf16[328,256]{1,0:T(8,128)(2,1)S(1)}) custom-call(bf16[216,256]{1,0:T(8,128)(2,1)S(1)} %collective-permute-done.refs_0_, bf16[216,256]{1,0:T(8,128)(2,1)S(1)} %collective-permute-done.1.refs_1_, ...), custom_call_target="tpu_custom_call" | custom-call | tf_op jit(solution)/shard_map/pallas_call | solution.py:544
  17.7 3.0 %collective-permute-start.7 = (bf16[328,256]{1,0:T(8,128)(2,1)S(1)}, bf16[328,256]{1,0:T(8,128)(2,1)S(1)}, u32[]{:S(2)}, u32[]{:S(2)}) collective-permute-start(bf16[328,256]{1,0:T(8,128)(2,1)S(1)} %get-tuple-element.21), channel_id=1, source_target_pairs={{0,24},{8,16},{16,8},{24,0},{1,25},{9,17},{17,9},{25,1},{2,26},{10... | collective-permute-start | bytes 503816 | tf_op jit(solution)/shard_map/ppermute | solution.py:513
  20.7 0.5 %collective-permute-start.8 = (bf16[328,256]{1,0:T(8,128)(2,1)S(1)}, bf16[328,256]{1,0:T(8,128)(2,1)S(1)}, u32[]{:S(2)}, u32[]{:S(2)}) collective-permute-start(bf16[328,256]{1,0:T(8,128)(2,1)S(1)} %get-tuple-element.22), channel_id=1, source_target_pairs={{0,16},{8,24},{16,0},{24,8},{1,17},{9,25},{17,1},{25,9},{2,18},{10... | collective-permute-start | bytes 503816 | tf_op jit(solution)/shard_map/ppermute | solution.py:513
  21.2 0.1 collective-permute-start.9
  21.4 4.5 %collective-permute-done.7.refs_9_ = bf16[328,256]{1,0:T(8,128)(2,1)S(1)} collective-permute-done((bf16[328,256]{1,0:T(8,128)(2,1)S(1)}, bf16[328,256]{1,0:T(8,128)(2,1)S(1)}, u32[]{:S(2)}, u32[]{:S(2)}) %collective-permute-start.7) | collective-permute-done | bytes 167968 | tf_op jit(solution)/shard_map/ppermute | solution.py:513
  25.8 3.1 %collective-permute-done.8.refs_10_ = bf16[328,256]{1,0:T(8,128)(2,1)S(1)} collective-permute-done((bf16[328,256]{1,0:T(8,128)(2,1)S(1)}, bf16[328,256]{1,0:T(8,128)(2,1)S(1)}, u32[]{:S(2)}, u32[]{:S(2)}) %collective-permute-start.8) | collective-permute-done | bytes 167968 | tf_op jit(solution)/shard_map/ppermute | solution.py:513
  28.9 0.3 collective-permute-done.9.refs_11_
  29.2 0.1 add_convert_fusion.refs_0_
  29.3 0.1 collective-permute-start.10
  29.4 1.3 %collective-permute-done.10.refs_1_ = bf16[256,256]{1,0:T(8,128)(2,1)S(1)} collective-permute-done((bf16[256,256]{1,0:T(8,128)(2,1)S(1)}, bf16[256,256]{1,0:T(8,128)(2,1)S(1)}, u32[]{:S(2)}, u32[]{:S(2)}) %collective-permute-start.10) | collective-permute-done | bytes 131104 | tf_op jit(solution)/shard_map/ppermute | solution.py:510
  30.7 0.0 copy-done
  30.7 0.0 copy-done.1
  30.7 6.6 %shard_map.124 = (bf16[2,1,8,1024]{3,2,1,0:T(8,128)(2,1)}, f32[1,128]{1,0:T(1,128)}, bf16[2,1,8,1024]{3,2,1,0:T(8,128)(2,1)}) custom-call(bf16[256,256]{1,0:T(8,128)(2,1)S(1)} %add_convert_fusion.refs_0_, bf16[256,256]{1,0:T(8,128)(2,1)S(1)} %collective-permute-done.10.refs_1_, bf16[2,1,8,1024]{3,2,1,0:T(8,128)(2,1)S(1)} %copy-done, ...), custom_call_target="tpu_custom_call" | custom-call | tf_op jit(solution)/shard_map/pallas_call | solution.py:562
Async XLA Ops:
  2.0 28.8 %copy-start = (bf16[2,1,8,1024]{3,2,1,0:T(8,128)(2,1)S(1)}, bf16[2,1,8,1024]{3,2,1,0:T(8,128)(2,1)}, u32[]{:S(2)}) copy-start(bf16[2,1,8,1024]{3,2,1,0:T(8,128)(2,1)} %refs_2_.1) | copy-start | bytes 98308
  2.0 28.7 %copy-start.1 = (bf16[256]{0:T(256)(128)(2,1)S(1)}, bf16[256]{0:T(256)(128)(2,1)}, u32[]{:S(2)}) copy-start(bf16[256]{0:T(256)(128)(2,1)} %refs_7_.1) | copy-start | bytes 1540
  2.0 11.2 %collective-permute-start.2 = (bf16[216,256]{1,0:T(8,128)(2,1)S(1)}, bf16[216,256]{1,0:T(8,128)(2,1)S(1)}, u32[]{:S(2)}, u32[]{:S(2)}) collective-permute-start(bf16[216,256]{1,0:T(8,128)(2,1)S(1)} %shard_map.121.packed_ref.refs_3_), channel_id=1, source_target_pairs={{0,4},{1,5},{2,6},{3,7},{4,0},{5,1},{6,2},{7,3},{8,12},{9,13},{10,... | collective-permute-start | bytes 331784 | tf_op jit(solution)/shard_map/ppermute | solution.py:510
  6.1 7.1 %collective-permute-start.1 = (bf16[216,256]{1,0:T(8,128)(2,1)S(1)}, bf16[216,256]{1,0:T(8,128)(2,1)S(1)}, u32[]{:S(2)}, u32[]{:S(2)}) collective-permute-start(bf16[216,256]{1,0:T(8,128)(2,1)S(1)} %shard_map.121.packed_ref.refs_3_), channel_id=1, source_target_pairs={{0,2},{1,3},{2,0},{3,1},{4,6},{5,7},{6,4},{7,5},{8,10},{9,11},{10,... | collective-permute-start | bytes 331784 | tf_op jit(solution)/shard_map/ppermute | solution.py:510
  7.7 7.4 %collective-permute-start = (bf16[216,256]{1,0:T(8,128)(2,1)S(1)}, bf16[216,256]{1,0:T(8,128)(2,1)S(1)}, u32[]{:S(2)}, u32[]{:S(2)}) collective-permute-start(bf16[216,256]{1,0:T(8,128)(2,1)S(1)} %shard_map.121.packed_ref.refs_3_), channel_id=1, source_target_pairs={{0,6},{1,7},{2,4},{3,5},{4,2},{5,3},{6,0},{7,1},{8,14},{9,15},{10,... | collective-permute-start | bytes 331784 | tf_op jit(solution)/shard_map/ppermute | solution.py:510
  12.4 2.7 %collective-permute-start.6 = (bf16[216,256]{1,0:T(8,128)(2,1)S(1)}, bf16[216,256]{1,0:T(8,128)(2,1)S(1)}, u32[]{:S(2)}, u32[]{:S(2)}) collective-permute-start(bf16[216,256]{1,0:T(8,128)(2,1)S(1)} %get-tuple-element.18), channel_id=1, source_target_pairs={{0,1},{1,0},{2,3},{3,2},{4,5},{5,4},{6,7},{7,6},{8,9},{9,8},{10,11... | collective-permute-start | bytes 331784 | tf_op jit(solution)/shard_map/ppermute | solution.py:510
  13.2 1.9 %collective-permute-start.5 = (bf16[216,256]{1,0:T(8,128)(2,1)S(1)}, bf16[216,256]{1,0:T(8,128)(2,1)S(1)}, u32[]{:S(2)}, u32[]{:S(2)}) collective-permute-start(bf16[216,256]{1,0:T(8,128)(2,1)S(1)} %collective-permute-done.2.refs_2_), channel_id=1, source_target_pairs={{0,1},{1,0},{2,3},{3,2},{4,5},{5,4},{6,7},{7,6},{8,9},{9,8},{10,11... | collective-permute-start | bytes 331784 | tf_op jit(solution)/shard_map/ppermute | solution.py:510
  13.2 1.9 %collective-permute-start.4 = (bf16[216,256]{1,0:T(8,128)(2,1)S(1)}, bf16[216,256]{1,0:T(8,128)(2,1)S(1)}, u32[]{:S(2)}, u32[]{:S(2)}) collective-permute-start(bf16[216,256]{1,0:T(8,128)(2,1)S(1)} %collective-permute-done.1.refs_1_), channel_id=1, source_target_pairs={{0,1},{1,0},{2,3},{3,2},{4,5},{5,4},{6,7},{7,6},{8,9},{9,8},{10,11... | collective-permute-start | bytes 331784 | tf_op jit(solution)/shard_map/ppermute | solution.py:510
  15.0 1.3 %collective-permute-start.3 = (bf16[216,256]{1,0:T(8,128)(2,1)S(1)}, bf16[216,256]{1,0:T(8,128)(2,1)S(1)}, u32[]{:S(2)}, u32[]{:S(2)}) collective-permute-start(bf16[216,256]{1,0:T(8,128)(2,1)S(1)} %collective-permute-done.refs_0_), channel_id=1, source_target_pairs={{0,1},{1,0},{2,3},{3,2},{4,5},{5,4},{6,7},{7,6},{8,9},{9,8},{10,11... | collective-permute-start | bytes 331784 | tf_op jit(solution)/shard_map/ppermute | solution.py:510
  17.7 8.1 %collective-permute-start.7 = (bf16[328,256]{1,0:T(8,128)(2,1)S(1)}, bf16[328,256]{1,0:T(8,128)(2,1)S(1)}, u32[]{:S(2)}, u32[]{:S(2)}) collective-permute-start(bf16[328,256]{1,0:T(8,128)(2,1)S(1)} %get-tuple-element.21), channel_id=1, source_target_pairs={{0,24},{8,16},{16,8},{24,0},{1,25},{9,17},{17,9},{25,1},{2,26},{10... | collective-permute-start | bytes 503816 | tf_op jit(solution)/shard_map/ppermute | solution.py:513
  20.7 8.2 %collective-permute-start.8 = (bf16[328,256]{1,0:T(8,128)(2,1)S(1)}, bf16[328,256]{1,0:T(8,128)(2,1)S(1)}, u32[]{:S(2)}, u32[]{:S(2)}) collective-permute-start(bf16[328,256]{1,0:T(8,128)(2,1)S(1)} %get-tuple-element.22), channel_id=1, source_target_pairs={{0,16},{8,24},{16,0},{24,8},{1,17},{9,25},{17,1},{25,9},{2,18},{10... | collective-permute-start | bytes 503816 | tf_op jit(solution)/shard_map/ppermute | solution.py:513
  21.2 8.0 %collective-permute-start.9 = (bf16[328,256]{1,0:T(8,128)(2,1)S(1)}, bf16[328,256]{1,0:T(8,128)(2,1)S(1)}, u32[]{:S(2)}, u32[]{:S(2)}) collective-permute-start(bf16[328,256]{1,0:T(8,128)(2,1)S(1)} %get-tuple-element.23), channel_id=1, source_target_pairs={{0,8},{8,0},{16,24},{24,16},{1,9},{9,1},{17,25},{25,17},{2,10},{10... | collective-permute-start | bytes 503816 | tf_op jit(solution)/shard_map/ppermute | solution.py:513
  29.3 1.4 %collective-permute-start.10 = (bf16[256,256]{1,0:T(8,128)(2,1)S(1)}, bf16[256,256]{1,0:T(8,128)(2,1)S(1)}, u32[]{:S(2)}, u32[]{:S(2)}) collective-permute-start(bf16[256,256]{1,0:T(8,128)(2,1)S(1)} %add_convert_fusion.refs_0_), channel_id=1, source_target_pairs={{0,1},{1,0},{2,3},{3,2},{4,5},{5,4},{6,7},{7,6},{8,9},{9,8},{10,11... | collective-permute-start | bytes 393224 | tf_op jit(solution)/shard_map/ppermute | solution.py:510

commit v8 on v7

--- a/solution.py
+++ b/solution.py
@@ -328,22 +328,21 @@
     labels = labels.astype(BF16)
     first = dot(attended[0:rows, :], out_w[...])
     blocks = [first[i * own : (i + 1) * own, :] for i in range(rows // own)]
-    for d, ref in enumerate(part_refs):
-        ref[0:queries_n, :] = partial
+    sum_ref, enc_refs = part_refs[0], part_refs[1:]
+    sum_ref[0:queries_n, :] = partial
+    sum_ref[queries_n:, :] = labels
+    for d, ref in enumerate(enc_refs):
         picked = blocks[0]
         for i in range(1, len(blocks)):
             picked = jnp.where((h ^ d) == i, blocks[i], picked)
-        for i in range(picked.shape[1] // width):
-            at = queries_n + i * own
-            ref[at : at + own, :] = picked[:, i * width : (i + 1) * width].astype(BF16)
-        ref[ref.shape[0] - LABEL_ROWS :, :] = labels
+        ref[...] = picked.astype(BF16)
 
 
 def decoder_kernel(sizes, *refs):
     nc, nt, ni, own_c, zs, tok_n, parts_n = sizes
-    ours, theirs, r_ref, w1, w2, w1_t, w2_t, class_w, neck_w = refs[:9]
-    parts = refs[9 : 9 + parts_n]
-    encoded_ref, loss_ref, grad_ref, grid, cols, slope1, grad2, cols3, slope2, act, parts_out = refs[9 + parts_n :]
+    ours, theirs, w1, w2, w1_t, w2_t, class_w, neck_w = refs[:8]
+    parts = refs[8 : 8 + parts_n]
+    loss_ref, grad_ref, grid, cols, slope1, grad2, cols3, slope2, act, parts_out = refs[8 + parts_n :]
     channels = grid.shape[2]
     slab = nt * ni
     rows = nc * ni
@@ -471,15 +470,6 @@
     grad = dot_t(total.astype(BF16), neck_w[...])
     grad_ref[...] = grad.reshape(grad_ref.shape).astype(BF16)
 
-    own = own_c * ni
-    width = parts[0].shape[1]
-    base = rows * zs
-    for i in range(r_ref.shape[3] // width):
-        terms = [ref[base + i * own : base + (i + 1) * own, :].astype(F32) for ref in parts]
-        total = pairwise(terms).reshape(own_c, 1, ni, width)
-        lanes = slice(i * width, (i + 1) * width)
-        encoded_ref[:, :, :, lanes] = (r_ref[:, :, :, lanes].astype(F32) + total).astype(BF16)
-
 
 def pairwise(values):
     while len(values) > 1:
@@ -539,13 +529,13 @@
     theirs = [swap_tok(value, 1) for value in [again] + ours[1:]]
     order = far_first(zs)
     queries_n, keys_n = rows * zs, rows * tok_n
-    enc_rows = own * residual.shape[3] // width
-    part_shape = pltpu.VMEM((queries_n + LABEL_ROWS + enc_rows, channels), BF16)
+    part_shape = pltpu.VMEM((queries_n + LABEL_ROWS, channels), BF16)
+    enc_shape = pltpu.VMEM((own, residual.shape[3]), BF16)
     sent = pl.pallas_call(
         functools.partial(attention_kernel, tok_n, zs, rows, own),
-        out_shape=[part_shape] * heads_n,
+        out_shape=[part_shape] + [enc_shape] * heads_n,
         in_specs=[vmem()] * (2 * zs + 2),
-        out_specs=[vmem()] * heads_n,
+        out_specs=[vmem()] * (1 + heads_n),
         scratch_shapes=[
             pltpu.VMEM((queries_n, width), BF16),
             pltpu.VMEM((keys_n, width), BF16),
@@ -554,20 +544,19 @@
         ],
         compiler_params=pltpu.CompilerParams(vmem_limit_bytes=16 * 2**20),
     )(*[ours[d] for d in order], *[theirs[d] for d in order], out_w, joint)
-    parts = [swap_heads(sent[d], d) for d in range(heads_n - 1, 0, -1)] + [sent[0]]
+    parts = [swap_heads(sent[0], d) for d in range(heads_n - 1, 0, -1)] + [sent[0]]
     half = pairwise([part[:queries_n].astype(F32) for part in parts]).astype(BF16)
     other = swap_tok(half, 1)
     slab = nt * ni
-    return tuple(
+    loss, grad = (
         pl.pallas_call(
             functools.partial(decoder_kernel, (nc, nt, ni, own_c, zs, tok_n, heads_n)),
             out_shape=[
-                jax.ShapeDtypeStruct(residual.shape, BF16),
                 jax.ShapeDtypeStruct((1, 128), F32),
                 jax.ShapeDtypeStruct(residual.shape, BF16),
             ],
-            in_specs=[vmem()] * (9 + heads_n),
-            out_specs=[vmem()] * 3,
+            in_specs=[vmem()] * (8 + heads_n),
+            out_specs=[vmem()] * 2,
             scratch_shapes=[
                 pltpu.VMEM((nc, slab, channels), F32),
                 pltpu.VMEM((4, nc // 2 * slab, 9 * channels), BF16),
@@ -579,8 +568,12 @@
                 pltpu.VMEM((4, nc // 2 * slab, channels), F32),
             ],
             compiler_params=pltpu.CompilerParams(vmem_limit_bytes=36 * 2**20),
-        )(half, other, residual, first_in, second_in, first_t, second_t, w_class, neck_w, *parts)
-    )
+        )(half, other, first_in, second_in, first_t, second_t, w_class, neck_w, *parts)
+    )
+    pieces = [swap_heads(sent[1 + d], d) for d in range(heads_n - 1, 0, -1)] + [sent[1]]
+    total = pairwise([piece.astype(F32) for piece in pieces]).reshape(residual.shape)
+    encoded = (residual.astype(F32) + total).astype(BF16)
+    return (encoded, loss, grad)
 
 
 def power_of_two(n):

time: 37.4 us -> 36.9 us (0.987)
  waiting for transfers between devices: 12.6 us -> 6.46 us
  starting transfers between devices: 10 us -> 14.8 us
  other arithmetic: 0.07 us -> 0.71 us
    ppermute x3 -> x6, starting transfers between devices: 3.68 us -> 8.51 us  [swap_heads(): return lax.ppermute(value, 'heads', [(i, i ^ bits) for i in range(heads_n)])]
    ppermute x3 -> x6, waiting for transfers between devices: 7.85 us -> 3.08 us  [swap_heads(): return lax.ppermute(value, 'heads', [(i, i ^ bits) for i in range(heads_n)])]
    ppermute x8, waiting for transfers between devices: 4.71 us -> 3.38 us  [swap_tok(): return lax.ppermute(value, 'tok', [(i, i ^ bits) for i in range(tok_n)])]
    convert_element_type x0 -> x1, other arithmetic: none -> 0.64 us  [whole_grid(): encoded = (residual.astype(F32) + total).astype(BF16)]
  transfers between devices with their start and end apart: 11 -> 14, of which waited for: 7 -> 7; matrix products, arithmetic and copies ran while one was open for 0% -> 2% of each run, Pallas kernels for 13% -> 13%
where the time goes in v8:
time: 36.9 us; the launch traced here: 36.6 us
  starting transfers between devices  14.8 us (40%)
  Pallas kernels  13.9 us (38%)
  waiting for transfers between devices  6.46 us (18%)
  other arithmetic  0.71 us (2%)
  between operations  0.71 us (2%)
    ppermute x6, starting transfers between devices, swap_heads(): return lax.ppermute(value, 'heads', [(i, i ^ bits) for i in range(heads_n)])  8.51 us
    pallas_call x1, Pallas kernels, whole_grid(): pl.pallas_call(functools.partial(decoder_kernel, (nc, nt, ni, own_c, zs,...  6.56 us
    ppermute x8, starting transfers between devices, swap_tok(): return lax.ppermute(value, 'tok', [(i, i ^ bits) for i in range(tok_n)])  6.34 us
    pallas_call x1, Pallas kernels, whole_grid(): pl.pallas_call(weights_kernel, out_shape=[pltpu.VMEM((4,) + w_first.shape...  4.71 us
    ppermute x8, waiting for transfers between devices, swap_tok(): return lax.ppermute(value, 'tok', [(i, i ^ bits) for i in range(tok_n)])  3.38 us
    ppermute x6, waiting for transfers between devices, swap_heads(): return lax.ppermute(value, 'heads', [(i, i ^ bits) for i in range(heads_n)])  3.08 us
    pallas_call x1, Pallas kernels, whole_grid(): pl.pallas_call(functools.partial(pack_kernel, tok_n), out_shape=pltpu.VME...  1.31 us
    pallas_call x1, Pallas kernels, whole_grid(): pl.pallas_call(functools.partial(attention_kernel, tok_n, zs, rows, own),...  1.31 us
  transfers between devices with their start and end apart: 14, of which 7 were waited for; matrix products, arithmetic and copies ran while one was open for 2% of the time, Pallas kernels for 13%

profile of v8, /device:TPU:0, one launch (start us, length us, event | category | flops | bytes accessed | tf_op | source)
XLA Modules:
  0.0 36.6 jit_solution(18379817849956124782)
XLA Ops:
  0.6 1.3 %shard_map.121.packed_ref.refs_3_ = bf16[216,256]{1,0:T(8,128)(2,1)S(1)} custom-call(bf16[1,8,8,256]{3,2,1,0:T(8,128)(2,1)} %q_ref.1, bf16[1,8,8,256]{3,2,1,0:T(8,128)(2,1)} %k_ref.1, bf16[1,8,8,256]{3,2,1,0:T(8,128)(2,1)} %v_ref.1, bf16[2,1,8,1024]{3,2,1,0:T(8,128)(2,1)} %r_ref.1, bf16[1024,256]{1,0:T(8,128)(2,1)} %neck_ref.3, s32[2,1,8]{2,1,0:T(1,128)} %bitcast.11), custom_call_target="tpu_custom_call" | custom-call | tf_op jit(solution)/shard_map/pallas_call | solution.py:505
  2.0 0.0 copy-start.1
  2.0 0.0 copy-start
  2.0 4.1 %collective-permute-start.2 = (bf16[216,256]{1,0:T(8,128)(2,1)S(1)}, bf16[216,256]{1,0:T(8,128)(2,1)S(1)}, u32[]{:S(2)}, u32[]{:S(2)}) collective-permute-start(bf16[216,256]{1,0:T(8,128)(2,1)S(1)} %shard_map.121.packed_ref.refs_3_), channel_id=1, source_target_pairs={{0,4},{1,5},{2,6},{3,7},{4,0},{5,1},{6,2},{7,3},{8,12},{9,13},{10,... | collective-permute-start | bytes 331784 | tf_op jit(solution)/shard_map/ppermute | solution.py:500
  6.1 1.6 %collective-permute-start.1 = (bf16[216,256]{1,0:T(8,128)(2,1)S(1)}, bf16[216,256]{1,0:T(8,128)(2,1)S(1)}, u32[]{:S(2)}, u32[]{:S(2)}) collective-permute-start(bf16[216,256]{1,0:T(8,128)(2,1)S(1)} %shard_map.121.packed_ref.refs_3_), channel_id=1, source_target_pairs={{0,2},{1,3},{2,0},{3,1},{4,6},{5,7},{6,4},{7,5},{8,10},{9,11},{10,... | collective-permute-start | bytes 331784 | tf_op jit(solution)/shard_map/ppermute | solution.py:500
  7.7 4.7 %shard_map.122 = (bf16[4,3,3,256,256]{4,3,2,1,0:T(8,128)(2,1)S(1)}, bf16[4,3,3,256,256]{4,3,2,1,0:T(8,128)(2,1)S(1)}, bf16[3,3,3,256,256]{4,3,2,1,0:T(8,128)(2,1...) custom-call(bf16[3,3,3,256,256]{4,3,2,1,0:T(8,128)(2,1)} %first_ref., ...), custom_call_target="tpu_custom_call" | custom-call | bytes 29360128 | tf_op jit(solution)/shard_map/pallas_call | solution.py:513
  12.4 0.1 collective-permute-start.6
  12.5 0.7 %collective-permute-done.2.refs_2_ = bf16[216,256]{1,0:T(8,128)(2,1)S(1)} collective-permute-done((bf16[216,256]{1,0:T(8,128)(2,1)S(1)}, bf16[216,256]{1,0:T(8,128)(2,1)S(1)}, u32[]{:S(2)}, u32[]{:S(2)}) %collective-permute-start.2) | collective-permute-done | bytes 110624 | tf_op jit(solution)/shard_map/ppermute | solution.py:500
  13.2 0.0 collective-permute-start.5
  13.2 0.0 collective-permute-done.1.refs_1_
  13.2 0.5 %collective-permute-start.4 = (bf16[216,256]{1,0:T(8,128)(2,1)S(1)}, bf16[216,256]{1,0:T(8,128)(2,1)S(1)}, u32[]{:S(2)}, u32[]{:S(2)}) collective-permute-start(bf16[216,256]{1,0:T(8,128)(2,1)S(1)} %collective-permute-done.1.refs_1_), channel_id=1, source_target_pairs={{0,1},{1,0},{2,3},{3,2},{4,5},{5,4},{6,7},{7,6},{8,9},{9,8},{10,11... | collective-permute-start | bytes 331784 | tf_op jit(solution)/shard_map/ppermute | solution.py:500
  13.7 1.4 %collective-permute-done.refs_0_ = bf16[216,256]{1,0:T(8,128)(2,1)S(1)} collective-permute-done((bf16[216,256]{1,0:T(8,128)(2,1)S(1)}, bf16[216,256]{1,0:T(8,128)(2,1)S(1)}, u32[]{:S(2)}, u32[]{:S(2)}) %collective-permute-start) | collective-permute-done | bytes 110624 | tf_op jit(solution)/shard_map/ppermute | solution.py:500
  15.0 0.0 collective-permute-start.3
  15.0 0.0 collective-permute-done.6.refs_7_
  15.0 0.0 collective-permute-done.5.refs_6_
  15.1 1.3 %collective-permute-done.3.refs_4_ = bf16[216,256]{1,0:T(8,128)(2,1)S(1)} collective-permute-done((bf16[216,256]{1,0:T(8,128)(2,1)S(1)}, bf16[216,256]{1,0:T(8,128)(2,1)S(1)}, u32[]{:S(2)}, u32[]{:S(2)}) %collective-permute-start.3) | collective-permute-done | bytes 110624 | tf_op jit(solution)/shard_map/ppermute | solution.py:500
  16.4 1.3 %shard_map.123 = (bf16[264,256]{1,0:T(8,128)(2,1)S(1)}, bf16[16,1024]{1,0:T(8,128)(2,1)S(1)}, bf16[16,1024]{1,0:T(8,128)(2,1)S(1)}, bf16[16,1024]{1,0:T(8,128)(2,1)S(1)}, bf16[16,1024]{1,0:T(8,128)(2,1)S(1)}) custom-call(bf16[216,256]{1,0:T(8,128)(2,1)S(1)} %collective-permute-done.refs_0_, bf16[216,256]{1,0:T(8,128)(2,1)S(1)} %collective-permute-done.1.refs_1_, ...), custom_call_target="tpu_custom_call" | custom-call | tf_op jit(solution)/shard_map/pallas_call | solution.py:534
  17.7 2.1 %collective-permute-start.12 = (bf16[264,256]{1,0:T(8,128)(2,1)S(1)}, bf16[264,256]{1,0:T(8,128)(2,1)S(1)}, u32[]{:S(2)}, u32[]{:S(2)}) collective-permute-start(bf16[264,256]{1,0:T(8,128)(2,1)S(1)} %get-tuple-element.25.refs_11_), channel_id=1, source_target_pairs={{0,8},{8,0},{16,24},{24,16},{1,9},{9,1},{17,25},{25,17},{2,10},{10... | collective-permute-start | bytes 405512 | tf_op jit(solution)/shard_map/ppermute | solution.py:503
  19.8 1.5 %collective-permute-start.11 = (bf16[264,256]{1,0:T(8,128)(2,1)S(1)}, bf16[264,256]{1,0:T(8,128)(2,1)S(1)}, u32[]{:S(2)}, u32[]{:S(2)}) collective-permute-start(bf16[264,256]{1,0:T(8,128)(2,1)S(1)} %get-tuple-element.25.refs_11_), channel_id=1, source_target_pairs={{0,16},{8,24},{16,0},{24,8},{1,17},{9,25},{17,1},{25,9},{2,18},{10... | collective-permute-start | bytes 405512 | tf_op jit(solution)/shard_map/ppermute | solution.py:503
  21.3 0.0 collective-permute-start.10
  21.3 2.9 %collective-permute-start.7 = (bf16[16,1024]{1,0:T(8,128)(2,1)S(1)}, bf16[16,1024]{1,0:T(8,128)(2,1)S(1)}, u32[]{:S(2)}, u32[]{:S(2)}) collective-permute-start(bf16[16,1024]{1,0:T(8,128)(2,1)S(1)} %get-tuple-element.21), channel_id=1, source_target_pairs={{0,24},{8,16},{16,8},{24,0},{1,25},{9,17},{17,9},{25,1},{2,26},{10... | collective-permute-start | bytes 98312 | tf_op jit(solution)/shard_map/ppermute | solution.py:503
  24.2 0.5 %collective-permute-start.8 = (bf16[16,1024]{1,0:T(8,128)(2,1)S(1)}, bf16[16,1024]{1,0:T(8,128)(2,1)S(1)}, u32[]{:S(2)}, u32[]{:S(2)}) collective-permute-start(bf16[16,1024]{1,0:T(8,128)(2,1)S(1)} %get-tuple-element.22), channel_id=1, source_target_pairs={{0,16},{8,24},{16,0},{24,8},{1,17},{9,25},{17,1},{25,9},{2,18},{10... | collective-permute-start | bytes 98312 | tf_op jit(solution)/shard_map/ppermute | solution.py:503
  24.7 0.0 collective-permute-done.12.refs_10_
  24.7 1.5 %collective-permute-start.9 = (bf16[16,1024]{1,0:T(8,128)(2,1)S(1)}, bf16[16,1024]{1,0:T(8,128)(2,1)S(1)}, u32[]{:S(2)}, u32[]{:S(2)}) collective-permute-start(bf16[16,1024]{1,0:T(8,128)(2,1)S(1)} %get-tuple-element.23), channel_id=1, source_target_pairs={{0,8},{8,0},{16,24},{24,16},{1,9},{9,1},{17,25},{25,17},{2,10},{10... | collective-permute-start | bytes 98312 | tf_op jit(solution)/shard_map/ppermute | solution.py:503
  26.2 2.0 %collective-permute-done.11.refs_9_ = bf16[264,256]{1,0:T(8,128)(2,1)S(1)} collective-permute-done((bf16[264,256]{1,0:T(8,128)(2,1)S(1)}, bf16[264,256]{1,0:T(8,128)(2,1)S(1)}, u32[]{:S(2)}, u32[]{:S(2)}) %collective-permute-start.11) | collective-permute-done | bytes 135200 | tf_op jit(solution)/shard_map/ppermute | solution.py:503
  28.2 0.4 collective-permute-done.10.refs_8_
  28.5 0.1 add_convert_fusion.refs_0_
  28.6 0.1 collective-permute-start.13
  28.7 0.2 collective-permute-done.7
  28.9 0.5 %collective-permute-done.8 = bf16[16,1024]{1,0:T(8,128)(2,1)S(1)} collective-permute-done((bf16[16,1024]{1,0:T(8,128)(2,1)S(1)}, bf16[16,1024]{1,0:T(8,128)(2,1)S(1)}, u32[]{:S(2)}, u32[]{:S(2)}) %collective-permute-start.8) | collective-permute-done | bytes 32800 | tf_op jit(solution)/shard_map/ppermute | solution.py:503
  29.4 0.6 %fusion = bf16[2,1,8,1024]{3,2,1,0:T(8,128)(2,1)} fusion(bf16[16,1024]{1,0:T(8,128)(2,1)S(1)} %get-tuple-element.24, bf16[16,1024]{1,0:T(8,128)(2,1)S(1)} %collective-permute-done.9, bf16[16,1024]{1,0:T(8,128)(2,1)S(1)} %collective-permute-done.8, bf16[16,1024]{1,0:T(8,128)(2,1)S(1)} %collective-permute-done.7, bf16[2,1,8,1024]{3,2,1,0:T(8,128)(2,1)S(1)} %copy-done.1), kind=kLoop, calls=%fused_computation.2 | loop fusion | flops 163840 | bytes 196608 | tf_op jit(solution)/shard_map/convert_element_type | solution.py:575
  30.1 6.6 %shard_map.124 = (f32[1,128]{1,0:T(1,128)}, bf16[2,1,8,1024]{3,2,1,0:T(8,128)(2,1)}) custom-call(bf16[256,256]{1,0:T(8,128)(2,1)S(1)} %add_convert_fusion.refs_0_, bf16[256,256]{1,0:T(8,128)(2,1)S(1)} %collective-permute-done.13.refs_1_, bf16[4,3,3,256,256]{4,3,2,1,0:T(8,128)(2,1)S(1)} %get-tuple-element.26.refs_2_, ...), custom_call_target="tpu_custom_call" | custom-call | tf_op jit(solution)/shard_map/pallas_call | solution.py:552
  (6 shorter events, 0.0 us)
Async XLA Ops:
  2.0 27.5 %copy-start.1 = (bf16[2,1,8,1024]{3,2,1,0:T(8,128)(2,1)S(1)}, bf16[2,1,8,1024]{3,2,1,0:T(8,128)(2,1)}, u32[]{:S(2)}) copy-start(bf16[2,1,8,1024]{3,2,1,0:T(8,128)(2,1)} %r_ref.1) | copy-start | bytes 98308
  2.0 28.1 %copy-start = (bf16[256]{0:T(256)(128)(2,1)S(1)}, bf16[256]{0:T(256)(128)(2,1)}, u32[]{:S(2)}) copy-start(bf16[256]{0:T(256)(128)(2,1)} %refs_6_.1) | copy-start | bytes 1540
  2.0 11.2 %collective-permute-start.2 = (bf16[216,256]{1,0:T(8,128)(2,1)S(1)}, bf16[216,256]{1,0:T(8,128)(2,1)S(1)}, u32[]{:S(2)}, u32[]{:S(2)}) collective-permute-start(bf16[216,256]{1,0:T(8,128)(2,1)S(1)} %shard_map.121.packed_ref.refs_3_), channel_id=1, source_target_pairs={{0,4},{1,5},{2,6},{3,7},{4,0},{5,1},{6,2},{7,3},{8,12},{9,13},{10,... | collective-permute-start | bytes 331784 | tf_op jit(solution)/shard_map/ppermute | solution.py:500
  6.1 7.1 %collective-permute-start.1 = (bf16[216,256]{1,0:T(8,128)(2,1)S(1)}, bf16[216,256]{1,0:T(8,128)(2,1)S(1)}, u32[]{:S(2)}, u32[]{:S(2)}) collective-permute-start(bf16[216,256]{1,0:T(8,128)(2,1)S(1)} %shard_map.121.packed_ref.refs_3_), channel_id=1, source_target_pairs={{0,2},{1,3},{2,0},{3,1},{4,6},{5,7},{6,4},{7,5},{8,10},{9,11},{10,... | collective-permute-start | bytes 331784 | tf_op jit(solution)/shard_map/ppermute | solution.py:500
  7.7 7.4 %collective-permute-start = (bf16[216,256]{1,0:T(8,128)(2,1)S(1)}, bf16[216,256]{1,0:T(8,128)(2,1)S(1)}, u32[]{:S(2)}, u32[]{:S(2)}) collective-permute-start(bf16[216,256]{1,0:T(8,128)(2,1)S(1)} %shard_map.121.packed_ref.refs_3_), channel_id=1, source_target_pairs={{0,6},{1,7},{2,4},{3,5},{4,2},{5,3},{6,0},{7,1},{8,14},{9,15},{10,... | collective-permute-start | bytes 331784 | tf_op jit(solution)/shard_map/ppermute | solution.py:500
  12.4 2.7 %collective-permute-start.6 = (bf16[216,256]{1,0:T(8,128)(2,1)S(1)}, bf16[216,256]{1,0:T(8,128)(2,1)S(1)}, u32[]{:S(2)}, u32[]{:S(2)}) collective-permute-start(bf16[216,256]{1,0:T(8,128)(2,1)S(1)} %get-tuple-element.18), channel_id=1, source_target_pairs={{0,1},{1,0},{2,3},{3,2},{4,5},{5,4},{6,7},{7,6},{8,9},{9,8},{10,11... | collective-permute-start | bytes 331784 | tf_op jit(solution)/shard_map/ppermute | solution.py:500
  13.2 1.9 %collective-permute-start.5 = (bf16[216,256]{1,0:T(8,128)(2,1)S(1)}, bf16[216,256]{1,0:T(8,128)(2,1)S(1)}, u32[]{:S(2)}, u32[]{:S(2)}) collective-permute-start(bf16[216,256]{1,0:T(8,128)(2,1)S(1)} %collective-permute-done.2.refs_2_), channel_id=1, source_target_pairs={{0,1},{1,0},{2,3},{3,2},{4,5},{5,4},{6,7},{7,6},{8,9},{9,8},{10,11... | collective-permute-start | bytes 331784 | tf_op jit(solution)/shard_map/ppermute | solution.py:500
  13.2 1.9 %collective-permute-start.4 = (bf16[216,256]{1,0:T(8,128)(2,1)S(1)}, bf16[216,256]{1,0:T(8,128)(2,1)S(1)}, u32[]{:S(2)}, u32[]{:S(2)}) collective-permute-start(bf16[216,256]{1,0:T(8,128)(2,1)S(1)} %collective-permute-done.1.refs_1_), channel_id=1, source_target_pairs={{0,1},{1,0},{2,3},{3,2},{4,5},{5,4},{6,7},{7,6},{8,9},{9,8},{10,11... | collective-permute-start | bytes 331784 | tf_op jit(solution)/shard_map/ppermute | solution.py:500
  15.0 1.3 %collective-permute-start.3 = (bf16[216,256]{1,0:T(8,128)(2,1)S(1)}, bf16[216,256]{1,0:T(8,128)(2,1)S(1)}, u32[]{:S(2)}, u32[]{:S(2)}) collective-permute-start(bf16[216,256]{1,0:T(8,128)(2,1)S(1)} %collective-permute-done.refs_0_), channel_id=1, source_target_pairs={{0,1},{1,0},{2,3},{3,2},{4,5},{5,4},{6,7},{7,6},{8,9},{9,8},{10,11... | collective-permute-start | bytes 331784 | tf_op jit(solution)/shard_map/ppermute | solution.py:500
  17.7 7.0 %collective-permute-start.12 = (bf16[264,256]{1,0:T(8,128)(2,1)S(1)}, bf16[264,256]{1,0:T(8,128)(2,1)S(1)}, u32[]{:S(2)}, u32[]{:S(2)}) collective-permute-start(bf16[264,256]{1,0:T(8,128)(2,1)S(1)} %get-tuple-element.25.refs_11_), channel_id=1, source_target_pairs={{0,8},{8,0},{16,24},{24,16},{1,9},{9,1},{17,25},{25,17},{2,10},{10... | collective-permute-start | bytes 405512 | tf_op jit(solution)/shard_map/ppermute | solution.py:503
  19.8 8.4 %collective-permute-start.11 = (bf16[264,256]{1,0:T(8,128)(2,1)S(1)}, bf16[264,256]{1,0:T(8,128)(2,1)S(1)}, u32[]{:S(2)}, u32[]{:S(2)}) collective-permute-start(bf16[264,256]{1,0:T(8,128)(2,1)S(1)} %get-tuple-element.25.refs_11_), channel_id=1, source_target_pairs={{0,16},{8,24},{16,0},{24,8},{1,17},{9,25},{17,1},{25,9},{2,18},{10... | collective-permute-start | bytes 405512 | tf_op jit(solution)/shard_map/ppermute | solution.py:503
  21.3 7.3 %collective-permute-start.10 = (bf16[264,256]{1,0:T(8,128)(2,1)S(1)}, bf16[264,256]{1,0:T(8,128)(2,1)S(1)}, u32[]{:S(2)}, u32[]{:S(2)}) collective-permute-start(bf16[264,256]{1,0:T(8,128)(2,1)S(1)} %get-tuple-element.25.refs_11_), channel_id=1, source_target_pairs={{0,24},{8,16},{16,8},{24,0},{1,25},{9,17},{17,9},{25,1},{2,26},{10... | collective-permute-start | bytes 405512 | tf_op jit(solution)/shard_map/ppermute | solution.py:503
  21.3 7.6 %collective-permute-start.7 = (bf16[16,1024]{1,0:T(8,128)(2,1)S(1)}, bf16[16,1024]{1,0:T(8,128)(2,1)S(1)}, u32[]{:S(2)}, u32[]{:S(2)}) collective-permute-start(bf16[16,1024]{1,0:T(8,128)(2,1)S(1)} %get-tuple-element.21), channel_id=1, source_target_pairs={{0,24},{8,16},{16,8},{24,0},{1,25},{9,17},{17,9},{25,1},{2,26},{10... | collective-permute-start | bytes 98312 | tf_op jit(solution)/shard_map/ppermute | solution.py:503
  24.2 5.2 %collective-permute-start.8 = (bf16[16,1024]{1,0:T(8,128)(2,1)S(1)}, bf16[16,1024]{1,0:T(8,128)(2,1)S(1)}, u32[]{:S(2)}, u32[]{:S(2)}) collective-permute-start(bf16[16,1024]{1,0:T(8,128)(2,1)S(1)} %get-tuple-element.22), channel_id=1, source_target_pairs={{0,16},{8,24},{16,0},{24,8},{1,17},{9,25},{17,1},{25,9},{2,18},{10... | collective-permute-start | bytes 98312 | tf_op jit(solution)/shard_map/ppermute | solution.py:503
  24.7 4.7 %collective-permute-start.9 = (bf16[16,1024]{1,0:T(8,128)(2,1)S(1)}, bf16[16,1024]{1,0:T(8,128)(2,1)S(1)}, u32[]{:S(2)}, u32[]{:S(2)}) collective-permute-start(bf16[16,1024]{1,0:T(8,128)(2,1)S(1)} %get-tuple-element.23), channel_id=1, source_target_pairs={{0,8},{8,0},{16,24},{24,16},{1,9},{9,1},{17,25},{25,17},{2,10},{10... | collective-permute-start | bytes 98312 | tf_op jit(solution)/shard_map/ppermute | solution.py:503
  28.6 1.5 %collective-permute-start.13 = (bf16[256,256]{1,0:T(8,128)(2,1)S(1)}, bf16[256,256]{1,0:T(8,128)(2,1)S(1)}, u32[]{:S(2)}, u32[]{:S(2)}) collective-permute-start(bf16[256,256]{1,0:T(8,128)(2,1)S(1)} %add_convert_fusion.refs_0_), channel_id=1, source_target_pairs={{0,1},{1,0},{2,3},{3,2},{4,5},{5,4},{6,7},{7,6},{8,9},{9,8},{10,11... | collective-permute-start | bytes 393224 | tf_op jit(solution)/shard_map/ppermute | solution.py:500

commit v9 on v8

--- a/solution.py
+++ b/solution.py
@@ -292,8 +292,7 @@
     order = far_first(zs)
     ours = [refs[order.index(d)] for d in range(zs)]
     theirs = [refs[zs + order.index(d)] for d in range(zs)]
-    out_w, joint_w = refs[2 * zs : 2 + 2 * zs]
-    part_refs = refs[2 + 2 * zs : -4]
+    joint_w, sum_ref, own_ref = refs[2 * zs : 3 + 2 * zs]
     qq, kk, vv, part = refs[-4:]
     h, z, core, _ = place_of(tok_n)
     width = qq.shape[1]
@@ -326,11 +325,16 @@
         part[pl.ds(at, own), :] += ours[d][3 * rows : 3 * rows + own, :].astype(F32)
     partial = part[...].astype(BF16)
     labels = labels.astype(BF16)
-    first = dot(attended[0:rows, :], out_w[...])
-    blocks = [first[i * own : (i + 1) * own, :] for i in range(rows // own)]
-    sum_ref, enc_refs = part_refs[0], part_refs[1:]
+    own_ref[...] = attended[0:rows, :]
     sum_ref[0:queries_n, :] = partial
     sum_ref[queries_n:, :] = labels
+
+
+def output_kernel(tok_n, attended, out_w, *enc_refs):
+    h, _, _, _ = place_of(tok_n)
+    first = dot(attended[...], out_w[...])
+    own = enc_refs[0].shape[0]
+    blocks = [first[i * own : (i + 1) * own, :] for i in range(first.shape[0] // own)]
     for d, ref in enumerate(enc_refs):
         picked = blocks[0]
         for i in range(1, len(blocks)):
@@ -531,11 +535,11 @@
     queries_n, keys_n = rows * zs, rows * tok_n
     part_shape = pltpu.VMEM((queries_n + LABEL_ROWS, channels), BF16)
     enc_shape = pltpu.VMEM((own, residual.shape[3]), BF16)
-    sent = pl.pallas_call(
+    message, attended = pl.pallas_call(
         functools.partial(attention_kernel, tok_n, zs, rows, own),
-        out_shape=[part_shape] + [enc_shape] * heads_n,
-        in_specs=[vmem()] * (2 * zs + 2),
-        out_specs=[vmem()] * (1 + heads_n),
+        out_shape=[part_shape, pltpu.VMEM((rows, width), BF16)],
+        in_specs=[vmem()] * (2 * zs + 1),
+        out_specs=[vmem()] * 2,
         scratch_shapes=[
             pltpu.VMEM((queries_n, width), BF16),
             pltpu.VMEM((keys_n, width), BF16),
@@ -543,8 +547,15 @@
             pltpu.VMEM((queries_n, channels), F32),
         ],
         compiler_params=pltpu.CompilerParams(vmem_limit_bytes=16 * 2**20),
-    )(*[ours[d] for d in order], *[theirs[d] for d in order], out_w, joint)
-    parts = [swap_heads(sent[0], d) for d in range(heads_n - 1, 0, -1)] + [sent[0]]
+    )(*[ours[d] for d in order], *[theirs[d] for d in order], joint)
+    parts = [message] + [swap_heads(message, d) for d in range(1, heads_n)]
+    sent = pl.pallas_call(
+        functools.partial(output_kernel, tok_n),
+        out_shape=[enc_shape] * heads_n,
+        in_specs=[vmem()] * 2,
+        out_specs=[vmem()] * heads_n,
+        compiler_params=pltpu.CompilerParams(vmem_limit_bytes=16 * 2**20),
+    )(attended, out_w)
     half = pairwise([part[:queries_n].astype(F32) for part in parts]).astype(BF16)
     other = swap_tok(half, 1)
     slab = nt * ni
@@ -570,7 +581,7 @@
             compiler_params=pltpu.CompilerParams(vmem_limit_bytes=36 * 2**20),
         )(half, other, first_in, second_in, first_t, second_t, w_class, neck_w, *parts)
     )
-    pieces = [swap_heads(sent[1 + d], d) for d in range(heads_n - 1, 0, -1)] + [sent[1]]
+    pieces = [swap_heads(sent[d], d) for d in range(heads_n - 1, 0, -1)] + [sent[0]]
     total = pairwise([piece.astype(F32) for piece in pieces]).reshape(residual.shape)
     encoded = (residual.astype(F32) + total).astype(BF16)
     return (encoded, loss, grad)

time: 36.9 us -> 36.6 us (level)
  waiting for transfers between devices: 6.46 us -> 5.45 us
  starting transfers between devices: 14.8 us -> 15.6 us
    ppermute x6, waiting for transfers between devices: 3.08 us -> 1.93 us  [swap_heads(): return lax.ppermute(value, 'heads', [(i, i ^ bits) for i in range(heads_n)])]
    ppermute x6, starting transfers between devices: 8.51 us -> 9.22 us  [swap_heads(): return lax.ppermute(value, 'heads', [(i, i ^ bits) for i in range(heads_n)])]
  transfers between devices with their start and end apart: 14 -> 14, of which waited for: 7 -> 8; matrix products, arithmetic and copies ran while one was open for 2% -> 2% of each run, Pallas kernels for 13% -> 14%
where the time goes in v9:
time: 36.6 us; the launch traced here: 36.4 us
  starting transfers between devices  15.6 us (43%)
  Pallas kernels  14 us (38%)
  waiting for transfers between devices  5.45 us (15%)
  between operations  0.72 us (2%)
  other arithmetic  0.71 us (2%)
    ppermute x6, starting transfers between devices, swap_heads(): return lax.ppermute(value, 'heads', [(i, i ^ bits) for i in range(heads_n)])  9.22 us
    pallas_call x1, Pallas kernels, whole_grid(): pl.pallas_call(functools.partial(decoder_kernel, (nc, nt, ni, own_c, zs,...  6.56 us
    ppermute x8, starting transfers between devices, swap_tok(): return lax.ppermute(value, 'tok', [(i, i ^ bits) for i in range(tok_n)])  6.34 us
    pallas_call x1, Pallas kernels, whole_grid(): pl.pallas_call(weights_kernel, out_shape=[pltpu.VMEM((4,) + w_first.shape...  4.71 us
    ppermute x8, waiting for transfers between devices, swap_tok(): return lax.ppermute(value, 'tok', [(i, i ^ bits) for i in range(tok_n)])  3.52 us
    ppermute x6, waiting for transfers between devices, swap_heads(): return lax.ppermute(value, 'heads', [(i, i ^ bits) for i in range(heads_n)])  1.93 us
    pallas_call x1, Pallas kernels, whole_grid(): pl.pallas_call(functools.partial(pack_kernel, tok_n), out_shape=pltpu.VME...  1.31 us
    pallas_call x1, Pallas kernels, whole_grid(): pl.pallas_call(functools.partial(attention_kernel, tok_n, zs, rows, own),...  1.21 us
  transfers between devices with their start and end apart: 14, of which 8 were waited for; matrix products, arithmetic and copies ran while one was open for 2% of the time, Pallas kernels for 14%

profile of v9, /device:TPU:0, one launch (start us, length us, event | category | flops | bytes accessed | tf_op | source)
XLA Modules:
  0.0 36.4 jit_solution(2392354828870837799)
XLA Ops:
  0.6 1.3 %shard_map.121.packed_ref.refs_3_ = bf16[216,256]{1,0:T(8,128)(2,1)S(1)} custom-call(bf16[1,8,8,256]{3,2,1,0:T(8,128)(2,1)} %q_ref.1, bf16[1,8,8,256]{3,2,1,0:T(8,128)(2,1)} %k_ref.1, bf16[1,8,8,256]{3,2,1,0:T(8,128)(2,1)} %v_ref.1, bf16[2,1,8,1024]{3,2,1,0:T(8,128)(2,1)} %r_ref.1, bf16[1024,256]{1,0:T(8,128)(2,1)} %neck_ref.3, s32[2,1,8]{2,1,0:T(1,128)} %bitcast.11), custom_call_target="tpu_custom_call" | custom-call | tf_op jit(solution)/shard_map/pallas_call | solution.py:509
  2.0 0.0 copy-start.1
  2.0 0.0 copy-start
  2.0 4.1 %collective-permute-start.2 = (bf16[216,256]{1,0:T(8,128)(2,1)S(1)}, bf16[216,256]{1,0:T(8,128)(2,1)S(1)}, u32[]{:S(2)}, u32[]{:S(2)}) collective-permute-start(bf16[216,256]{1,0:T(8,128)(2,1)S(1)} %shard_map.121.packed_ref.refs_3_), channel_id=1, source_target_pairs={{0,4},{1,5},{2,6},{3,7},{4,0},{5,1},{6,2},{7,3},{8,12},{9,13},{10,... | collective-permute-start | bytes 331784 | tf_op jit(solution)/shard_map/ppermute | solution.py:504
  6.1 1.6 %collective-permute-start.1 = (bf16[216,256]{1,0:T(8,128)(2,1)S(1)}, bf16[216,256]{1,0:T(8,128)(2,1)S(1)}, u32[]{:S(2)}, u32[]{:S(2)}) collective-permute-start(bf16[216,256]{1,0:T(8,128)(2,1)S(1)} %shard_map.121.packed_ref.refs_3_), channel_id=1, source_target_pairs={{0,2},{1,3},{2,0},{3,1},{4,6},{5,7},{6,4},{7,5},{8,10},{9,11},{10,... | collective-permute-start | bytes 331784 | tf_op jit(solution)/shard_map/ppermute | solution.py:504
  7.7 0.0 collective-permute-start
  7.7 4.7 %shard_map.122 = (bf16[4,3,3,256,256]{4,3,2,1,0:T(8,128)(2,1)S(1)}, bf16[4,3,3,256,256]{4,3,2,1,0:T(8,128)(2,1)S(1)}, bf16[3,3,3,256,256]{4,3,2,1,0:T(8,128)(2,1...) custom-call(bf16[3,3,3,256,256]{4,3,2,1,0:T(8,128)(2,1)} %first_ref., ...), custom_call_target="tpu_custom_call" | custom-call | bytes 29360128 | tf_op jit(solution)/shard_map/pallas_call | solution.py:517
  12.4 0.1 collective-permute-start.6
  12.5 0.7 %collective-permute-done.2.refs_2_ = bf16[216,256]{1,0:T(8,128)(2,1)S(1)} collective-permute-done((bf16[216,256]{1,0:T(8,128)(2,1)S(1)}, bf16[216,256]{1,0:T(8,128)(2,1)S(1)}, u32[]{:S(2)}, u32[]{:S(2)}) %collective-permute-start.2) | collective-permute-done | bytes 110624 | tf_op jit(solution)/shard_map/ppermute | solution.py:504
  13.2 0.0 collective-permute-start.5
  13.2 0.5 %collective-permute-start.4 = (bf16[216,256]{1,0:T(8,128)(2,1)S(1)}, bf16[216,256]{1,0:T(8,128)(2,1)S(1)}, u32[]{:S(2)}, u32[]{:S(2)}) collective-permute-start(bf16[216,256]{1,0:T(8,128)(2,1)S(1)} %collective-permute-done.1.refs_1_), channel_id=1, source_target_pairs={{0,1},{1,0},{2,3},{3,2},{4,5},{5,4},{6,7},{7,6},{8,9},{9,8},{10,11... | collective-permute-start | bytes 331784 | tf_op jit(solution)/shard_map/ppermute | solution.py:504
  13.7 1.4 %collective-permute-done.refs_0_ = bf16[216,256]{1,0:T(8,128)(2,1)S(1)} collective-permute-done((bf16[216,256]{1,0:T(8,128)(2,1)S(1)}, bf16[216,256]{1,0:T(8,128)(2,1)S(1)}, u32[]{:S(2)}, u32[]{:S(2)}) %collective-permute-start) | collective-permute-done | bytes 110624 | tf_op jit(solution)/shard_map/ppermute | solution.py:504
  15.1 0.0 collective-permute-done.4.refs_5_
  15.1 1.3 %collective-permute-done.3.refs_4_ = bf16[216,256]{1,0:T(8,128)(2,1)S(1)} collective-permute-done((bf16[216,256]{1,0:T(8,128)(2,1)S(1)}, bf16[216,256]{1,0:T(8,128)(2,1)S(1)}, u32[]{:S(2)}, u32[]{:S(2)}) %collective-permute-start.3) | collective-permute-done | bytes 110624 | tf_op jit(solution)/shard_map/ppermute | solution.py:504
  16.4 1.2 %shard_map.123 = (bf16[264,256]{1,0:T(8,128)(2,1)S(1)}, bf16[64,256]{1,0:T(8,128)(2,1)S(1)}) custom-call(bf16[216,256]{1,0:T(8,128)(2,1)S(1)} %collective-permute-done.refs_0_, bf16[216,256]{1,0:T(8,128)(2,1)S(1)} %collective-permute-done.1.refs_1_, bf16[216,256]{1,0:T(8,128)(2,1)S(1)} %collective-permute-done.2.refs_2_, ...), custom_call_target="tpu_custom_call" | custom-call | tf_op jit(solution)/shard_map/pallas_call | solution.py:538
  17.6 3.0 %collective-permute-start.12 = (bf16[264,256]{1,0:T(8,128)(2,1)S(1)}, bf16[264,256]{1,0:T(8,128)(2,1)S(1)}, u32[]{:S(2)}, u32[]{:S(2)}) collective-permute-start(bf16[264,256]{1,0:T(8,128)(2,1)S(1)} %get-tuple-element.27.refs_8_), channel_id=1, source_target_pairs={{0,24},{8,16},{16,8},{24,0},{1,25},{9,17},{17,9},{25,1},{2,26},{10... | collective-permute-start | bytes 405512 | tf_op jit(solution)/shard_map/ppermute | solution.py:507
  20.6 0.5 %collective-permute-start.11 = (bf16[264,256]{1,0:T(8,128)(2,1)S(1)}, bf16[264,256]{1,0:T(8,128)(2,1)S(1)}, u32[]{:S(2)}, u32[]{:S(2)}) collective-permute-start(bf16[264,256]{1,0:T(8,128)(2,1)S(1)} %get-tuple-element.27.refs_8_), channel_id=1, source_target_pairs={{0,16},{8,24},{16,0},{24,8},{1,17},{9,25},{17,1},{25,9},{2,18},{10... | collective-permute-start | bytes 405512 | tf_op jit(solution)/shard_map/ppermute | solution.py:507
  21.1 0.1 collective-permute-start.10
  21.3 0.2 shard_map.124
  21.5 2.9 %collective-permute-start.7 = (bf16[16,1024]{1,0:T(8,128)(2,1)S(1)}, bf16[16,1024]{1,0:T(8,128)(2,1)S(1)}, u32[]{:S(2)}, u32[]{:S(2)}) collective-permute-start(bf16[16,1024]{1,0:T(8,128)(2,1)S(1)} %get-tuple-element.23), channel_id=1, source_target_pairs={{0,24},{8,16},{16,8},{24,0},{1,25},{9,17},{17,9},{25,1},{2,26},{10... | collective-permute-start | bytes 98312 | tf_op jit(solution)/shard_map/ppermute | solution.py:507
  24.4 0.5 %collective-permute-start.8 = (bf16[16,1024]{1,0:T(8,128)(2,1)S(1)}, bf16[16,1024]{1,0:T(8,128)(2,1)S(1)}, u32[]{:S(2)}, u32[]{:S(2)}) collective-permute-start(bf16[16,1024]{1,0:T(8,128)(2,1)S(1)} %get-tuple-element.24), channel_id=1, source_target_pairs={{0,16},{8,24},{16,0},{24,8},{1,17},{9,25},{17,1},{25,9},{2,18},{10... | collective-permute-start | bytes 98312 | tf_op jit(solution)/shard_map/ppermute | solution.py:507
  24.9 2.1 %collective-permute-start.9 = (bf16[16,1024]{1,0:T(8,128)(2,1)S(1)}, bf16[16,1024]{1,0:T(8,128)(2,1)S(1)}, u32[]{:S(2)}, u32[]{:S(2)}) collective-permute-start(bf16[16,1024]{1,0:T(8,128)(2,1)S(1)} %get-tuple-element.25), channel_id=1, source_target_pairs={{0,8},{8,0},{16,24},{24,16},{1,9},{9,1},{17,25},{25,17},{2,10},{10... | collective-permute-start | bytes 98312 | tf_op jit(solution)/shard_map/ppermute | solution.py:507
  27.0 0.8 %collective-permute-done.11.refs_10_ = bf16[264,256]{1,0:T(8,128)(2,1)S(1)} collective-permute-done((bf16[264,256]{1,0:T(8,128)(2,1)S(1)}, bf16[264,256]{1,0:T(8,128)(2,1)S(1)}, u32[]{:S(2)}, u32[]{:S(2)}) %collective-permute-start.11) | collective-permute-done | bytes 135200 | tf_op jit(solution)/shard_map/ppermute | solution.py:507
  27.9 0.5 %collective-permute-done.10.refs_9_ = bf16[264,256]{1,0:T(8,128)(2,1)S(1)} collective-permute-done((bf16[264,256]{1,0:T(8,128)(2,1)S(1)}, bf16[264,256]{1,0:T(8,128)(2,1)S(1)}, u32[]{:S(2)}, u32[]{:S(2)}) %collective-permute-start.10) | collective-permute-done | bytes 135200 | tf_op jit(solution)/shard_map/ppermute | solution.py:507
  28.4 0.1 add_convert_fusion.refs_0_
  28.5 0.1 collective-permute-start.13
  28.6 0.0 collective-permute-done.7
  28.6 0.2 collective-permute-done.8
  28.8 0.3 collective-permute-done.9
  29.1 0.6 %fusion = bf16[2,1,8,1024]{3,2,1,0:T(8,128)(2,1)} fusion(bf16[16,1024]{1,0:T(8,128)(2,1)S(1)} %get-tuple-element.26, bf16[16,1024]{1,0:T(8,128)(2,1)S(1)} %collective-permute-done.9, bf16[16,1024]{1,0:T(8,128)(2,1)S(1)} %collective-permute-done.8, bf16[16,1024]{1,0:T(8,128)(2,1)S(1)} %collective-permute-done.7, bf16[2,1,8,1024]{3,2,1,0:T(8,128)(2,1)S(1)} %copy-done.1), kind=kLoop, calls=%fused_computation.2 | loop fusion | flops 163840 | bytes 196608 | tf_op jit(solution)/shard_map/convert_element_type | solution.py:586
  29.7 0.1 collective-permute-done.13.refs_1_
  29.9 6.6 %shard_map.125 = (f32[1,128]{1,0:T(1,128)}, bf16[2,1,8,1024]{3,2,1,0:T(8,128)(2,1)}) custom-call(bf16[256,256]{1,0:T(8,128)(2,1)S(1)} %add_convert_fusion.refs_0_, bf16[256,256]{1,0:T(8,128)(2,1)S(1)} %collective-permute-done.13.refs_1_, bf16[4,3,3,256,256]{4,3,2,1,0:T(8,128)(2,1)S(1)} %get-tuple-element.28.refs_2_, ...), custom_call_target="tpu_custom_call" | custom-call | tf_op jit(solution)/shard_map/pallas_call | solution.py:563
  (7 shorter events, 0.0 us)
Async XLA Ops:
  2.0 27.2 %copy-start.1 = (bf16[2,1,8,1024]{3,2,1,0:T(8,128)(2,1)S(1)}, bf16[2,1,8,1024]{3,2,1,0:T(8,128)(2,1)}, u32[]{:S(2)}) copy-start(bf16[2,1,8,1024]{3,2,1,0:T(8,128)(2,1)} %r_ref.1) | copy-start | bytes 98308
  2.0 27.9 %copy-start = (bf16[256]{0:T(256)(128)(2,1)S(1)}, bf16[256]{0:T(256)(128)(2,1)}, u32[]{:S(2)}) copy-start(bf16[256]{0:T(256)(128)(2,1)} %refs_6_.1) | copy-start | bytes 1540
  2.0 11.2 %collective-permute-start.2 = (bf16[216,256]{1,0:T(8,128)(2,1)S(1)}, bf16[216,256]{1,0:T(8,128)(2,1)S(1)}, u32[]{:S(2)}, u32[]{:S(2)}) collective-permute-start(bf16[216,256]{1,0:T(8,128)(2,1)S(1)} %shard_map.121.packed_ref.refs_3_), channel_id=1, source_target_pairs={{0,4},{1,5},{2,6},{3,7},{4,0},{5,1},{6,2},{7,3},{8,12},{9,13},{10,... | collective-permute-start | bytes 331784 | tf_op jit(solution)/shard_map/ppermute | solution.py:504
  6.1 7.1 %collective-permute-start.1 = (bf16[216,256]{1,0:T(8,128)(2,1)S(1)}, bf16[216,256]{1,0:T(8,128)(2,1)S(1)}, u32[]{:S(2)}, u32[]{:S(2)}) collective-permute-start(bf16[216,256]{1,0:T(8,128)(2,1)S(1)} %shard_map.121.packed_ref.refs_3_), channel_id=1, source_target_pairs={{0,2},{1,3},{2,0},{3,1},{4,6},{5,7},{6,4},{7,5},{8,10},{9,11},{10,... | collective-permute-start | bytes 331784 | tf_op jit(solution)/shard_map/ppermute | solution.py:504
  7.7 7.4 %collective-permute-start = (bf16[216,256]{1,0:T(8,128)(2,1)S(1)}, bf16[216,256]{1,0:T(8,128)(2,1)S(1)}, u32[]{:S(2)}, u32[]{:S(2)}) collective-permute-start(bf16[216,256]{1,0:T(8,128)(2,1)S(1)} %shard_map.121.packed_ref.refs_3_), channel_id=1, source_target_pairs={{0,6},{1,7},{2,4},{3,5},{4,2},{5,3},{6,0},{7,1},{8,14},{9,15},{10,... | collective-permute-start | bytes 331784 | tf_op jit(solution)/shard_map/ppermute | solution.py:504
  12.4 2.7 %collective-permute-start.6 = (bf16[216,256]{1,0:T(8,128)(2,1)S(1)}, bf16[216,256]{1,0:T(8,128)(2,1)S(1)}, u32[]{:S(2)}, u32[]{:S(2)}) collective-permute-start(bf16[216,256]{1,0:T(8,128)(2,1)S(1)} %get-tuple-element.19), channel_id=1, source_target_pairs={{0,1},{1,0},{2,3},{3,2},{4,5},{5,4},{6,7},{7,6},{8,9},{9,8},{10,11... | collective-permute-start | bytes 331784 | tf_op jit(solution)/shard_map/ppermute | solution.py:504
  13.2 1.9 %collective-permute-start.5 = (bf16[216,256]{1,0:T(8,128)(2,1)S(1)}, bf16[216,256]{1,0:T(8,128)(2,1)S(1)}, u32[]{:S(2)}, u32[]{:S(2)}) collective-permute-start(bf16[216,256]{1,0:T(8,128)(2,1)S(1)} %collective-permute-done.2.refs_2_), channel_id=1, source_target_pairs={{0,1},{1,0},{2,3},{3,2},{4,5},{5,4},{6,7},{7,6},{8,9},{9,8},{10,11... | collective-permute-start | bytes 331784 | tf_op jit(solution)/shard_map/ppermute | solution.py:504
  13.2 1.9 %collective-permute-start.4 = (bf16[216,256]{1,0:T(8,128)(2,1)S(1)}, bf16[216,256]{1,0:T(8,128)(2,1)S(1)}, u32[]{:S(2)}, u32[]{:S(2)}) collective-permute-start(bf16[216,256]{1,0:T(8,128)(2,1)S(1)} %collective-permute-done.1.refs_1_), channel_id=1, source_target_pairs={{0,1},{1,0},{2,3},{3,2},{4,5},{5,4},{6,7},{7,6},{8,9},{9,8},{10,11... | collective-permute-start | bytes 331784 | tf_op jit(solution)/shard_map/ppermute | solution.py:504
  15.0 1.3 %collective-permute-start.3 = (bf16[216,256]{1,0:T(8,128)(2,1)S(1)}, bf16[216,256]{1,0:T(8,128)(2,1)S(1)}, u32[]{:S(2)}, u32[]{:S(2)}) collective-permute-start(bf16[216,256]{1,0:T(8,128)(2,1)S(1)} %collective-permute-done.refs_0_), channel_id=1, source_target_pairs={{0,1},{1,0},{2,3},{3,2},{4,5},{5,4},{6,7},{7,6},{8,9},{9,8},{10,11... | collective-permute-start | bytes 331784 | tf_op jit(solution)/shard_map/ppermute | solution.py:504
  17.6 7.3 %collective-permute-start.12 = (bf16[264,256]{1,0:T(8,128)(2,1)S(1)}, bf16[264,256]{1,0:T(8,128)(2,1)S(1)}, u32[]{:S(2)}, u32[]{:S(2)}) collective-permute-start(bf16[264,256]{1,0:T(8,128)(2,1)S(1)} %get-tuple-element.27.refs_8_), channel_id=1, source_target_pairs={{0,24},{8,16},{16,8},{24,0},{1,25},{9,17},{17,9},{25,1},{2,26},{10... | collective-permute-start | bytes 405512 | tf_op jit(solution)/shard_map/ppermute | solution.py:507
  20.6 7.2 %collective-permute-start.11 = (bf16[264,256]{1,0:T(8,128)(2,1)S(1)}, bf16[264,256]{1,0:T(8,128)(2,1)S(1)}, u32[]{:S(2)}, u32[]{:S(2)}) collective-permute-start(bf16[264,256]{1,0:T(8,128)(2,1)S(1)} %get-tuple-element.27.refs_8_), channel_id=1, source_target_pairs={{0,16},{8,24},{16,0},{24,8},{1,17},{9,25},{17,1},{25,9},{2,18},{10... | collective-permute-start | bytes 405512 | tf_op jit(solution)/shard_map/ppermute | solution.py:507
  21.1 7.3 %collective-permute-start.10 = (bf16[264,256]{1,0:T(8,128)(2,1)S(1)}, bf16[264,256]{1,0:T(8,128)(2,1)S(1)}, u32[]{:S(2)}, u32[]{:S(2)}) collective-permute-start(bf16[264,256]{1,0:T(8,128)(2,1)S(1)} %get-tuple-element.27.refs_8_), channel_id=1, source_target_pairs={{0,8},{8,0},{16,24},{24,16},{1,9},{9,1},{17,25},{25,17},{2,10},{10... | collective-permute-start | bytes 405512 | tf_op jit(solution)/shard_map/ppermute | solution.py:507
  21.5 7.1 %collective-permute-start.7 = (bf16[16,1024]{1,0:T(8,128)(2,1)S(1)}, bf16[16,1024]{1,0:T(8,128)(2,1)S(1)}, u32[]{:S(2)}, u32[]{:S(2)}) collective-permute-start(bf16[16,1024]{1,0:T(8,128)(2,1)S(1)} %get-tuple-element.23), channel_id=1, source_target_pairs={{0,24},{8,16},{16,8},{24,0},{1,25},{9,17},{17,9},{25,1},{2,26},{10... | collective-permute-start | bytes 98312 | tf_op jit(solution)/shard_map/ppermute | solution.py:507
  24.4 4.4 %collective-permute-start.8 = (bf16[16,1024]{1,0:T(8,128)(2,1)S(1)}, bf16[16,1024]{1,0:T(8,128)(2,1)S(1)}, u32[]{:S(2)}, u32[]{:S(2)}) collective-permute-start(bf16[16,1024]{1,0:T(8,128)(2,1)S(1)} %get-tuple-element.24), channel_id=1, source_target_pairs={{0,16},{8,24},{16,0},{24,8},{1,17},{9,25},{17,1},{25,9},{2,18},{10... | collective-permute-start | bytes 98312 | tf_op jit(solution)/shard_map/ppermute | solution.py:507
  24.9 4.2 %collective-permute-start.9 = (bf16[16,1024]{1,0:T(8,128)(2,1)S(1)}, bf16[16,1024]{1,0:T(8,128)(2,1)S(1)}, u32[]{:S(2)}, u32[]{:S(2)}) collective-permute-start(bf16[16,1024]{1,0:T(8,128)(2,1)S(1)} %get-tuple-element.25), channel_id=1, source_target_pairs={{0,8},{8,0},{16,24},{24,16},{1,9},{9,1},{17,25},{25,17},{2,10},{10... | collective-permute-start | bytes 98312 | tf_op jit(solution)/shard_map/ppermute | solution.py:507
  28.5 1.4 %collective-permute-start.13 = (bf16[256,256]{1,0:T(8,128)(2,1)S(1)}, bf16[256,256]{1,0:T(8,128)(2,1)S(1)}, u32[]{:S(2)}, u32[]{:S(2)}) collective-permute-start(bf16[256,256]{1,0:T(8,128)(2,1)S(1)} %add_convert_fusion.refs_0_), channel_id=1, source_target_pairs={{0,1},{1,0},{2,3},{3,2},{4,5},{5,4},{6,7},{7,6},{8,9},{9,8},{10,11... | collective-permute-start | bytes 393224 | tf_op jit(solution)/shard_map/ppermute | solution.py:504

commit v10 on v9

--- a/solution.py
+++ b/solution.py
@@ -581,7 +581,7 @@
             compiler_params=pltpu.CompilerParams(vmem_limit_bytes=36 * 2**20),
         )(half, other, first_in, second_in, first_t, second_t, w_class, neck_w, *parts)
     )
-    pieces = [swap_heads(sent[d], d) for d in range(heads_n - 1, 0, -1)] + [sent[0]]
+    pieces = [sent[0]] + [swap_heads(sent[d], d) for d in range(1, heads_n)]
     total = pairwise([piece.astype(F32) for piece in pieces]).reshape(residual.shape)
     encoded = (residual.astype(F32) + total).astype(BF16)
     return (encoded, loss, grad)

time: 36.6 us -> 37.2 us (1.016)
  starting transfers between devices: 15.6 us -> 16.5 us
    ppermute x6, starting transfers between devices: 9.22 us -> 10.2 us  [swap_heads(): return lax.ppermute(value, 'heads', [(i, i ^ bits) for i in range(heads_n)])]
  transfers between devices with their start and end apart: 14 -> 14, of which waited for: 8 -> 6; matrix products, arithmetic and copies ran while one was open for 2% -> 2% of each run, Pallas kernels for 14% -> 13%
where the time goes in v10:
time: 37.2 us; the launch traced here: 37.1 us
  starting transfers between devices  16.5 us (44%)
  Pallas kernels  14 us (38%)
  waiting for transfers between devices  5.12 us (14%)
  between operations  0.72 us (2%)
  other arithmetic  0.71 us (2%)
    ppermute x6, starting transfers between devices, swap_heads(): return lax.ppermute(value, 'heads', [(i, i ^ bits) for i in range(heads_n)])  10.2 us
    pallas_call x1, Pallas kernels, whole_grid(): pl.pallas_call(functools.partial(decoder_kernel, (nc, nt, ni, own_c, zs,...  6.56 us
    ppermute x8, starting transfers between devices, swap_tok(): return lax.ppermute(value, 'tok', [(i, i ^ bits) for i in range(tok_n)])  6.34 us
    pallas_call x1, Pallas kernels, whole_grid(): pl.pallas_call(weights_kernel, out_shape=[pltpu.VMEM((4,) + w_first.shape...  4.71 us
    ppermute x8, waiting for transfers between devices, swap_tok(): return lax.ppermute(value, 'tok', [(i, i ^ bits) for i in range(tok_n)])  3.38 us
    ppermute x6, waiting for transfers between devices, swap_heads(): return lax.ppermute(value, 'heads', [(i, i ^ bits) for i in range(heads_n)])  1.74 us
    pallas_call x1, Pallas kernels, whole_grid(): pl.pallas_call(functools.partial(pack_kernel, tok_n), out_shape=pltpu.VME...  1.31 us
    pallas_call x1, Pallas kernels, whole_grid(): pl.pallas_call(functools.partial(attention_kernel, tok_n, zs, rows, own),...  1.21 us
  transfers between devices with their start and end apart: 14, of which 6 were waited for; matrix products, arithmetic and copies ran while one was open for 2% of the time, Pallas kernels for 13%

profile of v10, /device:TPU:0, one launch (start us, length us, event | category | flops | bytes accessed | tf_op | source)
XLA Modules:
  0.0 37.1 jit_solution(8214380660527758848)
XLA Ops:
  0.6 1.3 %shard_map.121.packed_ref.refs_3_ = bf16[216,256]{1,0:T(8,128)(2,1)S(1)} custom-call(bf16[1,8,8,256]{3,2,1,0:T(8,128)(2,1)} %q_ref.1, bf16[1,8,8,256]{3,2,1,0:T(8,128)(2,1)} %k_ref.1, bf16[1,8,8,256]{3,2,1,0:T(8,128)(2,1)} %v_ref.1, bf16[2,1,8,1024]{3,2,1,0:T(8,128)(2,1)} %r_ref.1, bf16[1024,256]{1,0:T(8,128)(2,1)} %neck_ref.3, s32[2,1,8]{2,1,0:T(1,128)} %bitcast.11), custom_call_target="tpu_custom_call" | custom-call | tf_op jit(solution)/shard_map/pallas_call | solution.py:509
  2.0 0.0 copy-start.1
  2.0 0.0 copy-start
  2.0 4.1 %collective-permute-start.2 = (bf16[216,256]{1,0:T(8,128)(2,1)S(1)}, bf16[216,256]{1,0:T(8,128)(2,1)S(1)}, u32[]{:S(2)}, u32[]{:S(2)}) collective-permute-start(bf16[216,256]{1,0:T(8,128)(2,1)S(1)} %shard_map.121.packed_ref.refs_3_), channel_id=1, source_target_pairs={{0,4},{1,5},{2,6},{3,7},{4,0},{5,1},{6,2},{7,3},{8,12},{9,13},{10,... | collective-permute-start | bytes 331784 | tf_op jit(solution)/shard_map/ppermute | solution.py:504
  6.1 1.6 %collective-permute-start.1 = (bf16[216,256]{1,0:T(8,128)(2,1)S(1)}, bf16[216,256]{1,0:T(8,128)(2,1)S(1)}, u32[]{:S(2)}, u32[]{:S(2)}) collective-permute-start(bf16[216,256]{1,0:T(8,128)(2,1)S(1)} %shard_map.121.packed_ref.refs_3_), channel_id=1, source_target_pairs={{0,2},{1,3},{2,0},{3,1},{4,6},{5,7},{6,4},{7,5},{8,10},{9,11},{10,... | collective-permute-start | bytes 331784 | tf_op jit(solution)/shard_map/ppermute | solution.py:504
  7.7 4.7 %shard_map.122 = (bf16[4,3,3,256,256]{4,3,2,1,0:T(8,128)(2,1)S(1)}, bf16[4,3,3,256,256]{4,3,2,1,0:T(8,128)(2,1)S(1)}, bf16[3,3,3,256,256]{4,3,2,1,0:T(8,128)(2,1...) custom-call(bf16[3,3,3,256,256]{4,3,2,1,0:T(8,128)(2,1)} %first_ref., ...), custom_call_target="tpu_custom_call" | custom-call | bytes 29360128 | tf_op jit(solution)/shard_map/pallas_call | solution.py:517
  12.4 0.1 collective-permute-start.6
  12.5 0.7 %collective-permute-done.2.refs_2_ = bf16[216,256]{1,0:T(8,128)(2,1)S(1)} collective-permute-done((bf16[216,256]{1,0:T(8,128)(2,1)S(1)}, bf16[216,256]{1,0:T(8,128)(2,1)S(1)}, u32[]{:S(2)}, u32[]{:S(2)}) %collective-permute-start.2) | collective-permute-done | bytes 110624 | tf_op jit(solution)/shard_map/ppermute | solution.py:504
  13.2 0.0 collective-permute-start.5
  13.2 0.0 collective-permute-done.1.refs_1_
  13.2 0.5 %collective-permute-start.4 = (bf16[216,256]{1,0:T(8,128)(2,1)S(1)}, bf16[216,256]{1,0:T(8,128)(2,1)S(1)}, u32[]{:S(2)}, u32[]{:S(2)}) collective-permute-start(bf16[216,256]{1,0:T(8,128)(2,1)S(1)} %collective-permute-done.1.refs_1_), channel_id=1, source_target_pairs={{0,1},{1,0},{2,3},{3,2},{4,5},{5,4},{6,7},{7,6},{8,9},{9,8},{10,11... | collective-permute-start | bytes 331784 | tf_op jit(solution)/shard_map/ppermute | solution.py:504
  13.7 1.4 %collective-permute-done.refs_0_ = bf16[216,256]{1,0:T(8,128)(2,1)S(1)} collective-permute-done((bf16[216,256]{1,0:T(8,128)(2,1)S(1)}, bf16[216,256]{1,0:T(8,128)(2,1)S(1)}, u32[]{:S(2)}, u32[]{:S(2)}) %collective-permute-start) | collective-permute-done | bytes 110624 | tf_op jit(solution)/shard_map/ppermute | solution.py:504
  15.0 0.0 collective-permute-start.3
  15.0 0.0 collective-permute-done.6.refs_7_
  15.0 0.0 collective-permute-done.5.refs_6_
  15.1 1.3 %collective-permute-done.3.refs_4_ = bf16[216,256]{1,0:T(8,128)(2,1)S(1)} collective-permute-done((bf16[216,256]{1,0:T(8,128)(2,1)S(1)}, bf16[216,256]{1,0:T(8,128)(2,1)S(1)}, u32[]{:S(2)}, u32[]{:S(2)}) %collective-permute-start.3) | collective-permute-done | bytes 110624 | tf_op jit(solution)/shard_map/ppermute | solution.py:504
  16.4 1.2 %shard_map.123 = (bf16[264,256]{1,0:T(8,128)(2,1)S(1)}, bf16[64,256]{1,0:T(8,128)(2,1)S(1)}) custom-call(bf16[216,256]{1,0:T(8,128)(2,1)S(1)} %collective-permute-done.refs_0_, bf16[216,256]{1,0:T(8,128)(2,1)S(1)} %collective-permute-done.1.refs_1_, bf16[216,256]{1,0:T(8,128)(2,1)S(1)} %collective-permute-done.2.refs_2_, ...), custom_call_target="tpu_custom_call" | custom-call | tf_op jit(solution)/shard_map/pallas_call | solution.py:538
  17.6 3.0 %collective-permute-start.12 = (bf16[264,256]{1,0:T(8,128)(2,1)S(1)}, bf16[264,256]{1,0:T(8,128)(2,1)S(1)}, u32[]{:S(2)}, u32[]{:S(2)}) collective-permute-start(bf16[264,256]{1,0:T(8,128)(2,1)S(1)} %get-tuple-element.27.refs_8_), channel_id=1, source_target_pairs={{0,24},{8,16},{16,8},{24,0},{1,25},{9,17},{17,9},{25,1},{2,26},{10... | collective-permute-start | bytes 405512 | tf_op jit(solution)/shard_map/ppermute | solution.py:507
  20.6 0.5 %collective-permute-start.11 = (bf16[264,256]{1,0:T(8,128)(2,1)S(1)}, bf16[264,256]{1,0:T(8,128)(2,1)S(1)}, u32[]{:S(2)}, u32[]{:S(2)}) collective-permute-start(bf16[264,256]{1,0:T(8,128)(2,1)S(1)} %get-tuple-element.27.refs_8_), channel_id=1, source_target_pairs={{0,16},{8,24},{16,0},{24,8},{1,17},{9,25},{17,1},{25,9},{2,18},{10... | collective-permute-start | bytes 405512 | tf_op jit(solution)/shard_map/ppermute | solution.py:507
  21.1 0.1 collective-permute-start.10
  21.3 0.2 shard_map.124
  21.5 2.0 %collective-permute-start.7 = (bf16[16,1024]{1,0:T(8,128)(2,1)S(1)}, bf16[16,1024]{1,0:T(8,128)(2,1)S(1)}, u32[]{:S(2)}, u32[]{:S(2)}) collective-permute-start(bf16[16,1024]{1,0:T(8,128)(2,1)S(1)} %get-tuple-element.24), channel_id=1, source_target_pairs={{0,8},{8,0},{16,24},{24,16},{1,9},{9,1},{17,25},{25,17},{2,10},{10... | collective-permute-start | bytes 98312 | tf_op jit(solution)/shard_map/ppermute | solution.py:507
  23.4 1.5 %collective-permute-start.8 = (bf16[16,1024]{1,0:T(8,128)(2,1)S(1)}, bf16[16,1024]{1,0:T(8,128)(2,1)S(1)}, u32[]{:S(2)}, u32[]{:S(2)}) collective-permute-start(bf16[16,1024]{1,0:T(8,128)(2,1)S(1)} %get-tuple-element.25), channel_id=1, source_target_pairs={{0,16},{8,24},{16,0},{24,8},{1,17},{9,25},{17,1},{25,9},{2,18},{10... | collective-permute-start | bytes 98312 | tf_op jit(solution)/shard_map/ppermute | solution.py:507
  25.0 0.0 collective-permute-done.12.refs_11_
  25.0 3.0 %collective-permute-start.9 = (bf16[16,1024]{1,0:T(8,128)(2,1)S(1)}, bf16[16,1024]{1,0:T(8,128)(2,1)S(1)}, u32[]{:S(2)}, u32[]{:S(2)}) collective-permute-start(bf16[16,1024]{1,0:T(8,128)(2,1)S(1)} %get-tuple-element.26), channel_id=1, source_target_pairs={{0,24},{8,16},{16,8},{24,0},{1,25},{9,17},{17,9},{25,1},{2,26},{10... | collective-permute-start | bytes 98312 | tf_op jit(solution)/shard_map/ppermute | solution.py:507
  28.0 0.4 %collective-permute-done.10.refs_9_ = bf16[264,256]{1,0:T(8,128)(2,1)S(1)} collective-permute-done((bf16[264,256]{1,0:T(8,128)(2,1)S(1)}, bf16[264,256]{1,0:T(8,128)(2,1)S(1)}, u32[]{:S(2)}, u32[]{:S(2)}) %collective-permute-start.10) | collective-permute-done | bytes 135200 | tf_op jit(solution)/shard_map/ppermute | solution.py:507
  28.4 0.1 add_convert_fusion.refs_0_
  28.5 0.1 collective-permute-start.13
  28.6 0.2 collective-permute-done.7
  28.8 1.1 %collective-permute-done.9 = bf16[16,1024]{1,0:T(8,128)(2,1)S(1)} collective-permute-done((bf16[16,1024]{1,0:T(8,128)(2,1)S(1)}, bf16[16,1024]{1,0:T(8,128)(2,1)S(1)}, u32[]{:S(2)}, u32[]{:S(2)}) %collective-permute-start.9) | collective-permute-done | bytes 32800 | tf_op jit(solution)/shard_map/ppermute | solution.py:507
  29.9 0.6 %fusion = bf16[2,1,8,1024]{3,2,1,0:T(8,128)(2,1)} fusion(bf16[16,1024]{1,0:T(8,128)(2,1)S(1)} %collective-permute-done.9, bf16[16,1024]{1,0:T(8,128)(2,1)S(1)} %collective-permute-done.8, bf16[16,1024]{1,0:T(8,128)(2,1)S(1)} %collective-permute-done.7, bf16[16,1024]{1,0:T(8,128)(2,1)S(1)} %get-tuple-element.23, bf16[2,1,8,1024]{3,2,1,0:T(8,128)(2,1)S(1)} %copy-done.1), kind=kLoop, calls=%fused_computation.2 | loop fusion | flops 163840 | bytes 196608 | tf_op jit(solution)/shard_map/convert_element_type | solution.py:586
  30.5 6.6 %shard_map.125 = (f32[1,128]{1,0:T(1,128)}, bf16[2,1,8,1024]{3,2,1,0:T(8,128)(2,1)}) custom-call(bf16[256,256]{1,0:T(8,128)(2,1)S(1)} %add_convert_fusion.refs_0_, bf16[256,256]{1,0:T(8,128)(2,1)S(1)} %collective-permute-done.13.refs_1_, bf16[4,3,3,256,256]{4,3,2,1,0:T(8,128)(2,1)S(1)} %get-tuple-element.28.refs_2_, ...), custom_call_target="tpu_custom_call" | custom-call | tf_op jit(solution)/shard_map/pallas_call | solution.py:563
  (7 shorter events, 0.0 us)
Async XLA Ops:
  2.0 27.9 %copy-start.1 = (bf16[2,1,8,1024]{3,2,1,0:T(8,128)(2,1)S(1)}, bf16[2,1,8,1024]{3,2,1,0:T(8,128)(2,1)}, u32[]{:S(2)}) copy-start(bf16[2,1,8,1024]{3,2,1,0:T(8,128)(2,1)} %r_ref.1) | copy-start | bytes 98308
  2.0 28.6 %copy-start = (bf16[256]{0:T(256)(128)(2,1)S(1)}, bf16[256]{0:T(256)(128)(2,1)}, u32[]{:S(2)}) copy-start(bf16[256]{0:T(256)(128)(2,1)} %refs_6_.1) | copy-start | bytes 1540
  2.0 11.2 %collective-permute-start.2 = (bf16[216,256]{1,0:T(8,128)(2,1)S(1)}, bf16[216,256]{1,0:T(8,128)(2,1)S(1)}, u32[]{:S(2)}, u32[]{:S(2)}) collective-permute-start(bf16[216,256]{1,0:T(8,128)(2,1)S(1)} %shard_map.121.packed_ref.refs_3_), channel_id=1, source_target_pairs={{0,4},{1,5},{2,6},{3,7},{4,0},{5,1},{6,2},{7,3},{8,12},{9,13},{10,... | collective-permute-start | bytes 331784 | tf_op jit(solution)/shard_map/ppermute | solution.py:504
  6.1 7.1 %collective-permute-start.1 = (bf16[216,256]{1,0:T(8,128)(2,1)S(1)}, bf16[216,256]{1,0:T(8,128)(2,1)S(1)}, u32[]{:S(2)}, u32[]{:S(2)}) collective-permute-start(bf16[216,256]{1,0:T(8,128)(2,1)S(1)} %shard_map.121.packed_ref.refs_3_), channel_id=1, source_target_pairs={{0,2},{1,3},{2,0},{3,1},{4,6},{5,7},{6,4},{7,5},{8,10},{9,11},{10,... | collective-permute-start | bytes 331784 | tf_op jit(solution)/shard_map/ppermute | solution.py:504
  7.7 7.4 %collective-permute-start = (bf16[216,256]{1,0:T(8,128)(2,1)S(1)}, bf16[216,256]{1,0:T(8,128)(2,1)S(1)}, u32[]{:S(2)}, u32[]{:S(2)}) collective-permute-start(bf16[216,256]{1,0:T(8,128)(2,1)S(1)} %shard_map.121.packed_ref.refs_3_), channel_id=1, source_target_pairs={{0,6},{1,7},{2,4},{3,5},{4,2},{5,3},{6,0},{7,1},{8,14},{9,15},{10,... | collective-permute-start | bytes 331784 | tf_op jit(solution)/shard_map/ppermute | solution.py:504
  12.4 2.7 %collective-permute-start.6 = (bf16[216,256]{1,0:T(8,128)(2,1)S(1)}, bf16[216,256]{1,0:T(8,128)(2,1)S(1)}, u32[]{:S(2)}, u32[]{:S(2)}) collective-permute-start(bf16[216,256]{1,0:T(8,128)(2,1)S(1)} %get-tuple-element.19), channel_id=1, source_target_pairs={{0,1},{1,0},{2,3},{3,2},{4,5},{5,4},{6,7},{7,6},{8,9},{9,8},{10,11... | collective-permute-start | bytes 331784 | tf_op jit(solution)/shard_map/ppermute | solution.py:504
  13.2 1.9 %collective-permute-start.5 = (bf16[216,256]{1,0:T(8,128)(2,1)S(1)}, bf16[216,256]{1,0:T(8,128)(2,1)S(1)}, u32[]{:S(2)}, u32[]{:S(2)}) collective-permute-start(bf16[216,256]{1,0:T(8,128)(2,1)S(1)} %collective-permute-done.2.refs_2_), channel_id=1, source_target_pairs={{0,1},{1,0},{2,3},{3,2},{4,5},{5,4},{6,7},{7,6},{8,9},{9,8},{10,11... | collective-permute-start | bytes 331784 | tf_op jit(solution)/shard_map/ppermute | solution.py:504
  13.2 1.9 %collective-permute-start.4 = (bf16[216,256]{1,0:T(8,128)(2,1)S(1)}, bf16[216,256]{1,0:T(8,128)(2,1)S(1)}, u32[]{:S(2)}, u32[]{:S(2)}) collective-permute-start(bf16[216,256]{1,0:T(8,128)(2,1)S(1)} %collective-permute-done.1.refs_1_), channel_id=1, source_target_pairs={{0,1},{1,0},{2,3},{3,2},{4,5},{5,4},{6,7},{7,6},{8,9},{9,8},{10,11... | collective-permute-start | bytes 331784 | tf_op jit(solution)/shard_map/ppermute | solution.py:504
  15.0 1.3 %collective-permute-start.3 = (bf16[216,256]{1,0:T(8,128)(2,1)S(1)}, bf16[216,256]{1,0:T(8,128)(2,1)S(1)}, u32[]{:S(2)}, u32[]{:S(2)}) collective-permute-start(bf16[216,256]{1,0:T(8,128)(2,1)S(1)} %collective-permute-done.refs_0_), channel_id=1, source_target_pairs={{0,1},{1,0},{2,3},{3,2},{4,5},{5,4},{6,7},{7,6},{8,9},{9,8},{10,11... | collective-permute-start | bytes 331784 | tf_op jit(solution)/shard_map/ppermute | solution.py:504
  17.6 7.4 %collective-permute-start.12 = (bf16[264,256]{1,0:T(8,128)(2,1)S(1)}, bf16[264,256]{1,0:T(8,128)(2,1)S(1)}, u32[]{:S(2)}, u32[]{:S(2)}) collective-permute-start(bf16[264,256]{1,0:T(8,128)(2,1)S(1)} %get-tuple-element.27.refs_8_), channel_id=1, source_target_pairs={{0,24},{8,16},{16,8},{24,0},{1,25},{9,17},{17,9},{25,1},{2,26},{10... | collective-permute-start | bytes 405512 | tf_op jit(solution)/shard_map/ppermute | solution.py:507
  20.6 7.4 %collective-permute-start.11 = (bf16[264,256]{1,0:T(8,128)(2,1)S(1)}, bf16[264,256]{1,0:T(8,128)(2,1)S(1)}, u32[]{:S(2)}, u32[]{:S(2)}) collective-permute-start(bf16[264,256]{1,0:T(8,128)(2,1)S(1)} %get-tuple-element.27.refs_8_), channel_id=1, source_target_pairs={{0,16},{8,24},{16,0},{24,8},{1,17},{9,25},{17,1},{25,9},{2,18},{10... | collective-permute-start | bytes 405512 | tf_op jit(solution)/shard_map/ppermute | solution.py:507
  21.1 7.3 %collective-permute-start.10 = (bf16[264,256]{1,0:T(8,128)(2,1)S(1)}, bf16[264,256]{1,0:T(8,128)(2,1)S(1)}, u32[]{:S(2)}, u32[]{:S(2)}) collective-permute-start(bf16[264,256]{1,0:T(8,128)(2,1)S(1)} %get-tuple-element.27.refs_8_), channel_id=1, source_target_pairs={{0,8},{8,0},{16,24},{24,16},{1,9},{9,1},{17,25},{25,17},{2,10},{10... | collective-permute-start | bytes 405512 | tf_op jit(solution)/shard_map/ppermute | solution.py:507
  21.5 7.3 %collective-permute-start.7 = (bf16[16,1024]{1,0:T(8,128)(2,1)S(1)}, bf16[16,1024]{1,0:T(8,128)(2,1)S(1)}, u32[]{:S(2)}, u32[]{:S(2)}) collective-permute-start(bf16[16,1024]{1,0:T(8,128)(2,1)S(1)} %get-tuple-element.24), channel_id=1, source_target_pairs={{0,8},{8,0},{16,24},{24,16},{1,9},{9,1},{17,25},{25,17},{2,10},{10... | collective-permute-start | bytes 98312 | tf_op jit(solution)/shard_map/ppermute | solution.py:507
  23.4 5.3 %collective-permute-start.8 = (bf16[16,1024]{1,0:T(8,128)(2,1)S(1)}, bf16[16,1024]{1,0:T(8,128)(2,1)S(1)}, u32[]{:S(2)}, u32[]{:S(2)}) collective-permute-start(bf16[16,1024]{1,0:T(8,128)(2,1)S(1)} %get-tuple-element.25), channel_id=1, source_target_pairs={{0,16},{8,24},{16,0},{24,8},{1,17},{9,25},{17,1},{25,9},{2,18},{10... | collective-permute-start | bytes 98312 | tf_op jit(solution)/shard_map/ppermute | solution.py:507
  25.0 4.9 %collective-permute-start.9 = (bf16[16,1024]{1,0:T(8,128)(2,1)S(1)}, bf16[16,1024]{1,0:T(8,128)(2,1)S(1)}, u32[]{:S(2)}, u32[]{:S(2)}) collective-permute-start(bf16[16,1024]{1,0:T(8,128)(2,1)S(1)} %get-tuple-element.26), channel_id=1, source_target_pairs={{0,24},{8,16},{16,8},{24,0},{1,25},{9,17},{17,9},{25,1},{2,26},{10... | collective-permute-start | bytes 98312 | tf_op jit(solution)/shard_map/ppermute | solution.py:507
  28.5 2.1 %collective-permute-start.13 = (bf16[256,256]{1,0:T(8,128)(2,1)S(1)}, bf16[256,256]{1,0:T(8,128)(2,1)S(1)}, u32[]{:S(2)}, u32[]{:S(2)}) collective-permute-start(bf16[256,256]{1,0:T(8,128)(2,1)S(1)} %add_convert_fusion.refs_0_), channel_id=1, source_target_pairs={{0,1},{1,0},{2,3},{3,2},{4,5},{5,4},{6,7},{7,6},{8,9},{9,8},{10,11... | collective-permute-start | bytes 393224 | tf_op jit(solution)/shard_map/ppermute | solution.py:504
